TPU v7x, 256 devices: a whole 4x4x8 slice. The times are simulated.
256 devices in a mesh: dp: 8 (over z), seq: 32 (over y, x, core).
Axes of the slice: x: 4, y: 4, z: 8, core: 2. Of those that a mesh axis runs over, the one named last changes fastest.
Arguments:
- latents: bfloat16 [8, 32, 256, 1152], P('dp', 'seq'), may hold values from -6 to 6
- cotangent: bfloat16 [8, 32, 256, 1152], P('dp', 'seq'), may hold values from -6 to 6
- qkv_weight: bfloat16 [1152, 3456], replicated, may hold values from -0.1875 to 0.1875
- out_weight: bfloat16 [1152, 1152], replicated, may hold values from -0.1875 to 0.1875
- modulation: float32 [8, 4, 3, 1152], P('dp'), may hold values from -3 to 3
- frame_clip: int32 [8, 32], P('dp'), may hold values from 0 to 3, never falling along the last dimension, each value on 1 to 16 neighbouring positions
- clip_patches: int32 [8, 4], P('dp'), may hold values from 32 to 256, as said below
Outputs:
- block_out: bfloat16 [8, 32, 256, 1152], P('dp', 'seq')
- latent_grad: bfloat16 [8, 32, 256, 1152], P('dp', 'seq')
- weight_grads: float32 [1152, 1152], P('seq')
Inputs may be any that keep to these rules, and one draw needn't show every extreme that they name: `frame_clip`: frames of one clip are consecutive in their group; every group holds 4 clips of 1 to 16 frames, one of exactly 16. `clip_patches`: in every group some clip fills all 256 patch slots.
All inputs are finite; a program needn't handle non-finite values.
Results may differ from a plain program's by a relative error of at most 0.029.
Values may be sent and summed in bfloat16 or wider, within the bound.
No kernel may reach another device: no remote copies, remote signals or barrier semaphores. Data moves between devices by JAX's collectives and lax.ppermute only.
A program may use at most 128 MiB of HBM per device.

v0:
```python
import jax
import jax.numpy as jnp
from jax import lax
from jax.sharding import PartitionSpec as P

HEADS = 16


def norm_parts(values):
    center = values - jnp.mean(values, axis=-1, keepdims=True)
    spread = jnp.mean(center * center, axis=-1, keepdims=True)
    inv_std = lax.rsqrt(spread + 1e-06)
    return (center * inv_std, inv_std)


def contract_rows(left, right):
    return lax.dot_general(
        left, right, (((0,), (0,)), ((), ())), preferred_element_type=jnp.float32
    )


def split_heads(items, head_count):
    frames_n, items_n, wide_n = items.shape
    model_w = wide_n // 3
    shape_h = (frames_n, items_n, head_count, model_w // head_count)
    query_h = items[..., :model_w].reshape(shape_h)
    key_h = items[..., model_w : 2 * model_w].reshape(shape_h)
    value_h = items[..., 2 * model_w :].reshape(shape_h)
    return (query_h, key_h, value_h)


def probabilities(query_h, key_h, same_clip):
    att_scale = query_h.shape[3] ** (-0.5)
    scores = jnp.einsum("fnhd,gnhd->nhfg", query_h, key_h, preferred_element_type=jnp.float32)
    expo = jnp.exp(scores * att_scale) * same_clip[None, None]
    return expo / jnp.sum(expo, axis=-1, keepdims=True)


def attend(items, same_clip, head_count):
    query_h, key_h, value_h = split_heads(items, head_count)
    attn_prob = probabilities(query_h, key_h, same_clip)
    prob_low = attn_prob.astype(jnp.bfloat16)
    attended = jnp.einsum("nhfg,gnhd->fnhd", prob_low, value_h, preferred_element_type=jnp.float32)
    return attended.astype(jnp.bfloat16).reshape(
        items.shape[0], items.shape[1], items.shape[2] // 3
    )


def attend_back(items, d_att, same_clip, head_count):
    query_h, key_h, value_h = split_heads(items, head_count)
    att_scale = query_h.shape[3] ** (-0.5)
    attn_prob = probabilities(query_h, key_h, same_clip)
    prob_low = attn_prob.astype(jnp.bfloat16)
    d_heads = d_att.reshape(query_h.shape)
    grad_v = jnp.einsum(
        "nhfg,fnhd->gnhd", prob_low, d_heads, preferred_element_type=jnp.float32
    ).astype(jnp.bfloat16)
    d_prob = jnp.einsum("fnhd,gnhd->nhfg", d_heads, value_h, preferred_element_type=jnp.float32)
    d_score = attn_prob * (d_prob - jnp.sum(attn_prob * d_prob, axis=-1, keepdims=True))
    score_low = (d_score * att_scale).astype(jnp.bfloat16)
    grad_q = jnp.einsum(
        "nhfg,gnhd->fnhd", score_low, key_h, preferred_element_type=jnp.float32
    ).astype(jnp.bfloat16)
    grad_k = jnp.einsum(
        "nhfg,fnhd->gnhd", score_low, query_h, preferred_element_type=jnp.float32
    ).astype(jnp.bfloat16)
    flat_shape = (items.shape[0], items.shape[1], items.shape[2] // 3)
    return jnp.concatenate(
        [grad_q.reshape(flat_shape), grad_k.reshape(flat_shape), grad_v.reshape(flat_shape)], axis=2
    )


def per_device(latents, cotangent, qkv_weight, out_weight, modulation, frame_clip, clip_patches):
    frames_dev = latents.shape[1]
    patches_n = latents.shape[2]
    model_w = latents.shape[3]
    clips_n = modulation.shape[1]
    group_clip = frame_clip[0]
    own_clip = lax.dynamic_slice_in_dim(group_clip, lax.axis_index("seq") * frames_dev, frames_dev)
    onehot = own_clip[:, None] == jnp.arange(clips_n, dtype=jnp.int32)[None, :]
    per_frame = jnp.dot(
        onehot.astype(jnp.float32),
        modulation[0].reshape(clips_n, 3 * model_w),
        precision=lax.Precision.HIGHEST,
    )
    per_frame = per_frame.reshape(frames_dev, 3, model_w)
    shifts = per_frame[:, 0][:, None, :]
    scales = per_frame[:, 1][:, None, :]
    gates = per_frame[:, 2][:, None, :]
    frame_count = jnp.sum(jnp.where(onehot, clip_patches[0][None, :], 0), axis=1)
    valid_rows = (jnp.arange(patches_n, dtype=jnp.int32)[None, :] < frame_count[:, None]).astype(
        jnp.float32
    )[..., None]
    latent_f = latents[0].astype(jnp.float32)
    normed, inv_std = norm_parts(latent_f)
    xmod = (normed * (1.0 + scales) + shifts).astype(jnp.bfloat16)
    same_clip = (group_clip[:, None] == group_clip[None, :]).astype(jnp.float32)
    qkv = jnp.dot(xmod.reshape(-1, model_w), qkv_weight, preferred_element_type=jnp.float32).astype(
        jnp.bfloat16
    )
    qkv = qkv.reshape(frames_dev, patches_n, 3 * model_w)
    items = lax.all_to_all(qkv, "seq", split_axis=1, concat_axis=0, tiled=True)
    att_patch = attend(items, same_clip, HEADS)
    attended = lax.all_to_all(att_patch, "seq", split_axis=0, concat_axis=1, tiled=True)
    att_flat = attended.reshape(-1, model_w)
    proj = jnp.dot(att_flat, out_weight, preferred_element_type=jnp.float32).reshape(
        frames_dev, patches_n, model_w
    )
    block_out = (latent_f + valid_rows * gates * proj).astype(jnp.bfloat16)
    cot_f = cotangent[0].astype(jnp.float32)
    gdy = (valid_rows * gates * cot_f).astype(jnp.bfloat16)
    gdy_flat = gdy.reshape(-1, model_w)
    d_att = lax.dot_general(
        gdy_flat, out_weight, (((1,), (1,)), ((), ())), preferred_element_type=jnp.float32
    )
    d_att = d_att.astype(jnp.bfloat16).reshape(frames_dev, patches_n, model_w)
    d_att_patch = lax.all_to_all(d_att, "seq", split_axis=1, concat_axis=0, tiled=True)
    dqkv_patch = attend_back(items, d_att_patch, same_clip, HEADS)
    dqkv = lax.all_to_all(dqkv_patch, "seq", split_axis=0, concat_axis=1, tiled=True).reshape(
        -1, 3 * model_w
    )
    dxmod = lax.dot_general(
        dqkv, qkv_weight, (((1,), (1,)), ((), ())), preferred_element_type=jnp.float32
    )
    dxmod = dxmod.reshape(frames_dev, patches_n, model_w)
    dnorm = dxmod * (1.0 + scales)
    branch = inv_std * (
        dnorm
        - jnp.mean(dnorm, axis=-1, keepdims=True)
        - normed * jnp.mean(dnorm * normed, axis=-1, keepdims=True)
    )
    latent_grad = (cot_f + branch).astype(jnp.bfloat16)
    local_grad = contract_rows(gdy_flat, att_flat)
    group_grad = lax.psum(local_grad.astype(jnp.bfloat16), "dp")
    weight_grads = lax.psum_scatter(group_grad, "seq", scatter_dimension=0, tiled=True).astype(
        jnp.float32
    )
    return (block_out[None], latent_grad[None], weight_grads)


def solution(mesh):
    in_specs = (
        P("dp", "seq", None, None),
        P("dp", "seq", None, None),
        P(),
        P(),
        P("dp", None, None, None),
        P("dp", None),
        P("dp", None),
    )
    out_specs = (P("dp", "seq", None, None), P("dp", "seq", None, None), P("seq", None))
    return jax.shard_map(
        per_device, mesh=mesh, in_specs=in_specs, out_specs=out_specs, check_vma=False
    )
```

profile of v0, /device:TPU:2, one launch (start us, length us, event | category | flops | bytes accessed | tf_op | source)
XLA Modules:
  0.0 401.8 jit_solution(16930642057206446062)
XLA Ops:
  17.4 6.0 %reduce.17 = bf16[256,1152]{1,0:T(8,128)(2,1)} reduce(bf16[256,1,1152]{2,1,0:T(2,128)(2,1)} %bitcast.147, bf16[]{:T(256)} %broadcast.227), dimensions={1}, to_apply=%bitcast.143.reduce_sub_computation | reduce | bytes 1179650
  25.9 8.1 %all-to-all-start.2 = ((bf16[32,2,4608]{2,1,0:T(2,128)(2,1)}), bf16[32,2,4608]{2,1,0:T(2,128)(2,1)}, u32[]{:S(2)}, u32[]{:S(2)}) async-start(bf16[32,2,4608]{2,1,0:T(2,128)(2,1)} %reshape.416), calls=%async_computation.2 | async-start | bytes 1179648 | tf_op jit(solution)/shard_map/all_to_all | solution.py:117
  34.5 6.0 %fusion.2 = bf16[1,256,3456]{2,1,0:T(8,128)(2,1)S(1)} fusion(bf16[1152,3456]{1,0:T(8,128)(2,1)} %param.9, bf16[1,1,256,1152]{3,2,1,0:T(8,128)(2,1)S(1)} %copy-done.1, f32[1152]{0:T(1024)S(1)} %get-tuple-element.7, f32[1152]{0:T(1024)S(1)} %get-tuple-element.6, f32[256]{0:T(256)S(1)} %add_rsqrt_fusion, f32[256]{0:T(256)S(1)} %broadcast_multiply_fusion.2), kind=kOutput, calls=%fused_computation.3 | convolution fusion | flops 2041085952 | bytes 10333184 | tf_op jit(solution)/shard_map/dot_general | solution.py:98
  40.5 4.5 %copy.89 = bf16[1,256,3456]{2,0,1:T(2,128)(2,1)} copy(bf16[1,256,3456]{2,1,0:T(8,128)(2,1)S(1)} %fusion.2) | data formatting | bytes 3538944 | tf_op jit(solution)/shard_map/reshape | solution.py:101
  45.0 13.0 %reduce.16 = bf16[256,3456]{1,0:T(8,128)(2,1)} reduce(bf16[256,1,3456]{2,1,0:T(2,128)(2,1)} %bitcast.144, bf16[]{:T(256)} %broadcast.227), dimensions={1}, to_apply=%bitcast.142.reduce_sub_computation | reduce | bytes 3538946
  58.0 4.5 %reshape.414 = bf16[32,2,13824]{2,1,0:T(2,128)(2,1)} reshape(bf16[256,3456]{1,0:T(8,128)(2,1)} %reduce.16) | data formatting | bytes 3538944
  62.6 8.0 %all-to-all-start = ((bf16[32,2,13824]{2,1,0:T(2,128)(2,1)}), bf16[32,2,13824]{2,1,0:T(2,128)(2,1)}, u32[]{:S(2)}, u32[]{:S(2)}) async-start(bf16[32,2,13824]{2,1,0:T(2,128)(2,1)} %reshape.414), calls=%async_computation | async-start | bytes 3538944 | tf_op jit(solution)/shard_map/all_to_all | solution.py:102
  70.7 4.7 %reshape.417 = bf16[256,1,1152]{2,1,0:T(2,128)(2,1)} reshape(bf16[32,2,4608]{2,1,0:T(2,128)(2,1)} %all-to-all-done.2) | data formatting | bytes 1179648
  75.3 5.5 %bitcast_reduce_fusion = bf16[256,1152]{1,0:T(8,128)(2,1)} fusion(bf16[256,1,1152]{2,1,0:T(2,128)(2,1)} %reshape.417), kind=kLoop, calls=%fused_computation.110 | loop fusion | bytes 1179648 | tf_op jit(solution)/shard_map/all_to_all | solution.py:117
  80.8 3.7 reshape.399
  84.5 10.0 %all-to-all-done = bf16[32,2,13824]{2,1,0:T(2,128)(2,1)} async-done(((bf16[32,2,13824]{2,1,0:T(2,128)(2,1)}), bf16[32,2,13824]{2,1,0:T(2,128)(2,1)}, u32[]{:S(2)}, u32[]{:S(2)}) %all-to-all-start) | async-done | bytes 1769504 | tf_op jit(solution)/shard_map/all_to_all | solution.py:102
  94.6 10.0 %reshape.415 = bf16[256,1,3456]{2,1,0:T(2,128)(2,1)} reshape(bf16[32,2,13824]{2,1,0:T(2,128)(2,1)} %all-to-all-done) | data formatting | bytes 3538944
  108.1 3.7 reshape.394
  111.8 3.7 reshape.395
  115.5 4.1 %reshape.393 = bf16[32,8,16,72]{3,2,1,0:T(8,128)(2,1)} reshape(bf16[32,8,1152]{2,1,0:T(8,128)(2,1)} %get-tuple-element.10) | data formatting | bytes 1179648 | tf_op jit(solution)/shard_map/reshape | solution.py:28
  119.6 4.4 %fusion.54 = f32[8,16,32,32]{2,3,1,0:T(8,128)} fusion(bf16[32,8,16,72]{3,2,1,0:T(8,128)(2,1)} %reshape.399, bf16[32,8,16,72]{3,2,1,0:T(8,128)(2,1)} %reshape.393), kind=kOutput, calls=%fused_computation.57 | convolution fusion | flops 18874368 | bytes 1703936 | tf_op jit(solution)/shard_map/fnhd,gnhd->nhfg/dot_general | solution.py:58
  131.4 2.9 reshape.396
  134.3 6.8 %all-to-all-start.1 = ((bf16[32,8,1152]{2,1,0:T(8,128)(2,1)}), bf16[32,8,1152]{2,1,0:T(8,128)(2,1)}, u32[]{:S(2)}, u32[]{:S(2)}) async-start(bf16[32,8,1152]{2,1,0:T(8,128)(2,1)} %reshape.396), calls=%async_computation.1 | async-start | bytes 1179648 | tf_op jit(solution)/shard_map/all_to_all | solution.py:104
  141.2 6.7 %fusion.32 = bf16[32,8,16,72]{3,0,2,1:T(8,128)(2,1)} fusion(f32[8,16,32,32]{2,3,1,0:T(8,128)} %fusion.54, bf16[32,8,16,72]{3,2,1,0:T(8,128)(2,1)} %reshape.395, f32[8,16,32,32]{2,3,1,0:T(8,128)} %copy-done.11, f32[8,16,32]{2,1,0:T(8,128)S(1)} %get-tuple-element.11, f32[32,32]{0,1:T(8,128)S(1)} %compare_convert_fusion), kind=kOutput, calls=%fused_computation.37 | convolution fusion | flops 20615200 | bytes 2248704 | tf_op jit(solution)/shard_map/nhfg,gnhd->fnhd/dot_general | solution.py:61
  147.8 6.4 %fusion.29 = bf16[32,8,16,72]{3,0,2,1:T(8,128)(2,1)} fusion(f32[8,16,32,32]{2,3,1,0:T(8,128)} %fusion.54, bf16[32,8,16,72]{3,2,1,0:T(8,128)(2,1)} %reshape.394, f32[8,16,32,32]{2,3,1,0:T(8,128)} %copy-done.11, f32[8,16,32]{2,1,0:T(8,128)S(1)} %get-tuple-element.11, f32[32,32]{0,1:T(8,128)S(1)} %compare_convert_fusion), kind=kOutput, calls=%fused_computation.36 | convolution fusion | flops 20615200 | bytes 2248704 | tf_op jit(solution)/shard_map/nhfg,fnhd->gnhd/dot_general | solution.py:64
  156.8 2.9 reshape.400
  162.3 2.9 reshape.401
  167.9 2.9 reshape.402
  173.6 7.5 %all-to-all-start.3 = ((bf16[32,8,3456]{2,1,0:T(8,128)(2,1)}), bf16[32,8,3456]{2,1,0:T(8,128)(2,1)}, u32[]{:S(2)}, u32[]{:S(2)}) async-start(bf16[32,8,3456]{2,1,0:T(8,128)(2,1)} %pad_maximum_fusion), calls=%async_computation.3 | async-start | bytes 3538944 | tf_op jit(solution)/shard_map/all_to_all | solution.py:119
  181.2 3.9 convolution_convert_fusion
  185.0 82.3 %fusion = bf16[48,1152]{1,0:T(8,128)(2,1)S(1)} fusion(bf16[1152,1152]{1,0:T(8,128)(2,1)} %convolution_convert_fusion), kind=kCustom, calls=%all-reduce-scatter | all-reduce-scatter fusion | flops 1769473 | bytes 2765824
  272.5 3.8 collective-permute-start.2
  278.5 4.6 %collective-permute-start.4 = (bf16[48,1152]{1,0:T(8,128)(2,1)S(1)}, bf16[48,1152]{1,0:T(8,128)(2,1)}, u32[]{:S(2)}, u32[]{:S(2)}) collective-permute-start(bf16[48,1152]{1,0:T(8,128)(2,1)S(1)} %fusion), channel_id=1, source_target_pairs={{0,5},{1,6},{2,7},{3,8},{4,9},{5,10},{6,11},{7,12},{8,13},{9,14},{... | collective-permute-start | bytes 331784
  283.1 9.5 %collective-permute-start.5 = (bf16[48,1152]{1,0:T(8,128)(2,1)S(1)}, bf16[48,1152]{1,0:T(8,128)(2,1)}, u32[]{:S(2)}, u32[]{:S(2)}) collective-permute-start(bf16[48,1152]{1,0:T(8,128)(2,1)S(1)} %fusion), channel_id=1, source_target_pairs={{0,6},{1,7},{2,8},{3,9},{4,10},{5,11},{6,12},{7,13},{8,14},{9,15},... | collective-permute-start | bytes 331784
  296.9 14.4 %concatenate.4 = bf16[420,1152]{1,0:T(8,128)(2,1)} concatenate(bf16[36,1152]{1,0:T(8,128)(2,1)} %copy-done.8, bf16[48,1152]{1,0:T(8,128)(2,1)} %collective-permute-done.6, bf16[48,1152]{1,0:T(8,128)(2,1)} %collective-permute-done.5, bf16[48,1152]{1,0:T(8,128)(2,1)} %collective-permute-done.4, bf16[48,1152]{1,0:T(8,128)(2,1)} %collective-permute-done.3, ...), dimensions={0} | concatenate | bytes 1935360
  315.7 69.5 %all-reduce.4.cloned.1.call-done = bf16[36,1152]{1,0:T(8,128)(2,1)} async-done(((bf16[36,1152]{1,0:T(8,128)(2,1)}), bf16[36,1152]{1,0:T(8,128)(2,1)}) %all-reduce.4.cloned.1.call-update) | async-done | bytes 82960 | tf_op jit(solution)/shard_map/psum | solution.py:134
  386.9 6.5 %fusion.101 = (f32[256]{0:T(256)S(1)}, f32[256]{0:T(256)S(1)}, f32[256,1152]{1,0:T(8,128)S(1)}) fusion(f32[256]{0:T(256)S(1)} %add_rsqrt_fusion, f32[256]{0:T(256)S(1)} %broadcast_multiply_fusion.2, bf16[1,1,256,1152]{3,2,1,0:T(8,128)(2,1)S(1)} %copy-done.1, f32[1152]{0:T(1024)S(1)} %get-tuple-element.6, bf16[1152,3456]{1,0:T(8,128)(2,1)} %param.9, ...), kind=kOutput, calls=%fused_computation.107 | convolution fusion | flops 2040495616 | bytes 11510272 | tf_op jit(solution)/shard_map/dot_general | solution.py:122
  (73 shorter events, 52.9 us)
Async XLA Ops:
  7.2 5.7 %copy-start = (bf16[1152,1152]{1,0:T(8,128)(2,1)S(1)}, bf16[1152,1152]{1,0:T(8,128)(2,1)}, u32[]{:S(2)}) copy-start(bf16[1152,1152]{1,0:T(8,128)(2,1)} %param.10) | copy-start | bytes 7962628
  16.9 17.0 %copy-start.1 = (bf16[1,1,256,1152]{3,2,1,0:T(8,128)(2,1)S(1)}, bf16[1,1,256,1152]{3,2,1,0:T(8,128)(2,1)}, u32[]{:S(2)}) copy-start(bf16[1,1,256,1152]{3,2,1,0:T(8,128)(2,1)} %param.7) | copy-start | bytes 1769476
  25.9 36.7 %all-to-all-start.2 = ((bf16[32,2,4608]{2,1,0:T(2,128)(2,1)}), bf16[32,2,4608]{2,1,0:T(2,128)(2,1)}, u32[]{:S(2)}, u32[]{:S(2)}) async-start(bf16[32,2,4608]{2,1,0:T(2,128)(2,1)} %reshape.416), calls=%async_computation.2 | async-start | bytes 1179648 | tf_op jit(solution)/shard_map/all_to_all | solution.py:117
  62.6 8.0 %copy-start.9 = (s32[1,32]{1,0:T(1,128)S(1)}, s32[1,32]{1,0:T(1,128)}, u32[]{:S(2)}) copy-start(s32[1,32]{1,0:T(1,128)} %param.12) | copy-start | bytes 388
  62.6 32.0 %all-to-all-start = ((bf16[32,2,13824]{2,1,0:T(2,128)(2,1)}), bf16[32,2,13824]{2,1,0:T(2,128)(2,1)}, u32[]{:S(2)}, u32[]{:S(2)}) async-start(bf16[32,2,13824]{2,1,0:T(2,128)(2,1)} %reshape.414), calls=%async_computation | async-start | bytes 3538944 | tf_op jit(solution)/shard_map/all_to_all | solution.py:102
  119.6 4.5 %copy-start.5 = (bf16[32,8,16,72]{3,2,1,0:T(8,128)(2,1)S(1)}, bf16[32,8,16,72]{3,2,1,0:T(8,128)(2,1)}, u32[]{:S(2)}) copy-start(bf16[32,8,16,72]{3,2,1,0:T(8,128)(2,1)} %reshape.394) | copy-start | bytes 1769476
  119.6 4.4 %copy-start.6 = (bf16[32,8,16,72]{3,2,1,0:T(8,128)(2,1)S(1)}, bf16[32,8,16,72]{3,2,1,0:T(8,128)(2,1)}, u32[]{:S(2)}) copy-start(bf16[32,8,16,72]{3,2,1,0:T(8,128)(2,1)} %reshape.395) | copy-start | bytes 1769476
  124.1 1.8 copy-start.3
  125.9 1.4 copy-start.11
  125.9 2.0 copy-start.2
  134.3 39.2 %all-to-all-start.1 = ((bf16[32,8,1152]{2,1,0:T(8,128)(2,1)}), bf16[32,8,1152]{2,1,0:T(8,128)(2,1)}, u32[]{:S(2)}, u32[]{:S(2)}) async-start(bf16[32,8,1152]{2,1,0:T(8,128)(2,1)} %reshape.396), calls=%async_computation.1 | async-start | bytes 1179648 | tf_op jit(solution)/shard_map/all_to_all | solution.py:104
  173.6 213.3 %all-to-all-start.3 = ((bf16[32,8,3456]{2,1,0:T(8,128)(2,1)}), bf16[32,8,3456]{2,1,0:T(8,128)(2,1)}, u32[]{:S(2)}, u32[]{:S(2)}) async-start(bf16[32,8,3456]{2,1,0:T(8,128)(2,1)} %pad_maximum_fusion), calls=%async_computation.3 | async-start | bytes 3538944 | tf_op jit(solution)/shard_map/all_to_all | solution.py:119
  181.1 204.2 %all-reduce.4.cloned.1.call-start = ((), (), s32[]{:S(2)}) async-start(), calls=%async_computation.4 | async-start | bytes 184320 | tf_op jit(solution)/shard_map/psum | solution.py:134
  185.0 110.2 %copy-start.10 = (u32[256]{0:T(256)S(1)}, u32[256]{0:T(256)}, u32[]{:S(2)}) copy-start(u32[256]{0:T(256)} %constant.30) | copy-start | bytes 3076
  267.3 15.8 %collective-permute-start = (bf16[48,1152]{1,0:T(8,128)(2,1)S(1)}, bf16[48,1152]{1,0:T(8,128)(2,1)S(1)}, u32[]{:S(2)}, u32[]{:S(2)}) collective-permute-start(bf16[48,1152]{1,0:T(8,128)(2,1)S(1)} %fusion), channel_id=1, source_target_pairs={{0,1},{1,2},{2,3},{3,4},{4,5},{5,6},{6,7},{7,8},{8,9},{9,10},{10,1... | collective-permute-start | bytes 331784
  269.2 23.4 %collective-permute-start.1 = (bf16[48,1152]{1,0:T(8,128)(2,1)S(1)}, bf16[48,1152]{1,0:T(8,128)(2,1)S(1)}, u32[]{:S(2)}, u32[]{:S(2)}) collective-permute-start(bf16[48,1152]{1,0:T(8,128)(2,1)S(1)} %fusion), channel_id=1, source_target_pairs={{0,2},{1,3},{2,4},{3,5},{4,6},{5,7},{6,8},{7,9},{8,10},{9,11},{10,... | collective-permute-start | bytes 331784
  271.2 7.3 %collective-permute-start.7 = (bf16[36,1152]{1,0:T(8,128)(2,1)S(1)}, bf16[36,1152]{1,0:T(8,128)(2,1)S(1)}, u32[]{:S(2)}, u32[]{:S(2)}) collective-permute-start(bf16[36,1152]{1,0:T(8,128)(2,1)S(1)} %slice.33), channel_id=1, source_target_pairs={{0,8},{1,9},{2,10},{3,11},{4,12},{5,13},{6,14},{7,15},{8,16},{9,17... | collective-permute-start | bytes 248840
  272.5 23.9 %collective-permute-start.2 = (bf16[48,1152]{1,0:T(8,128)(2,1)S(1)}, bf16[48,1152]{1,0:T(8,128)(2,1)}, u32[]{:S(2)}, u32[]{:S(2)}) collective-permute-start(bf16[48,1152]{1,0:T(8,128)(2,1)S(1)} %fusion), channel_id=1, source_target_pairs={{0,3},{1,4},{2,5},{3,6},{4,7},{5,8},{6,9},{7,10},{8,11},{9,12},{10... | collective-permute-start | bytes 331784
  276.3 20.2 %collective-permute-start.3 = (bf16[48,1152]{1,0:T(8,128)(2,1)S(1)}, bf16[48,1152]{1,0:T(8,128)(2,1)}, u32[]{:S(2)}, u32[]{:S(2)}) collective-permute-start(bf16[48,1152]{1,0:T(8,128)(2,1)S(1)} %fusion), channel_id=1, source_target_pairs={{0,4},{1,5},{2,6},{3,7},{4,8},{5,9},{6,10},{7,11},{8,12},{9,13},{1... | collective-permute-start | bytes 331784
  278.5 16.7 %copy-start.8 = (bf16[36,1152]{1,0:T(8,128)(2,1)}, bf16[36,1152]{1,0:T(8,128)(2,1)S(1)}, u32[]{:S(2)}) copy-start(bf16[36,1152]{1,0:T(8,128)(2,1)S(1)} %collective-permute-done.7) | copy-start | bytes 248836
  278.5 18.0 %collective-permute-start.4 = (bf16[48,1152]{1,0:T(8,128)(2,1)S(1)}, bf16[48,1152]{1,0:T(8,128)(2,1)}, u32[]{:S(2)}, u32[]{:S(2)}) collective-permute-start(bf16[48,1152]{1,0:T(8,128)(2,1)S(1)} %fusion), channel_id=1, source_target_pairs={{0,5},{1,6},{2,7},{3,8},{4,9},{5,10},{6,11},{7,12},{8,13},{9,14},{... | collective-permute-start | bytes 331784
  283.1 13.4 %collective-permute-start.5 = (bf16[48,1152]{1,0:T(8,128)(2,1)S(1)}, bf16[48,1152]{1,0:T(8,128)(2,1)}, u32[]{:S(2)}, u32[]{:S(2)}) collective-permute-start(bf16[48,1152]{1,0:T(8,128)(2,1)S(1)} %fusion), channel_id=1, source_target_pairs={{0,6},{1,7},{2,8},{3,9},{4,10},{5,11},{6,12},{7,13},{8,14},{9,15},... | collective-permute-start | bytes 331784
  292.6 0.6 copy-start.7
  293.3 3.6 collective-permute-start.6
  386.9 6.6 %copy-start.4 = (bf16[1,1,256,1152]{3,2,1,0:T(8,128)(2,1)S(1)}, bf16[1,1,256,1152]{3,2,1,0:T(8,128)(2,1)}, u32[]{:S(2)}) copy-start(bf16[1,1,256,1152]{3,2,1,0:T(8,128)(2,1)} %param.8) | copy-start | bytes 1769476
Sparse Core Ops, SparseCore 0:
  313.0 72.2 all-reduce.3
where the time goes:
time: 410 us; the launch traced here: 402 us
  local copies, waits for them, and re-layouts  93.2 us (23%)
  blocking collectives  82.3 us (20%)
  waiting for transfers between devices  80 us (20%)
  starting transfers between devices  57.7 us (14%)
  matrix products  45.6 us (11%)
  other arithmetic  27.9 us (7%)
  between operations  15.2 us (4%)
    unnamed x1, blocking collectives  82.3 us
    psum x1, waiting for transfers between devices, per_device(): group_grad = lax.psum(local_grad.astype(jnp.bfloat16), 'dp')  69.5 us
    unnamed x34, local copies, waits for them, and re-layouts  42.5 us
    unnamed x8, starting transfers between devices  27.2 us
    unnamed x2, other arithmetic  19 us
    all_to_all x1, waiting for transfers between devices, per_device(): items = lax.all_to_all(qkv, 'seq', split_axis=1, concat_axis=0, tiled=True)  10 us
  transfers between devices with their start and end apart: 13, of which 3 were waited for; matrix products, arithmetic and copies ran while one was open for 45% of the time, Pallas kernels for 0%

commit v1 on v0

v1 whole, which is shorter than its diff:
```python
import jax
import jax.numpy as jnp
from jax import lax
from jax.experimental import pallas as pl
from jax.experimental.pallas import tpu as pltpu
from jax.sharding import PartitionSpec as P

HEADS = 16
LANES = 128
CHUNK = 384
MIB = 1024 * 1024

NN = (((1,), (0,)), ((), ()))
NT = (((1,), (1,)), ((), ()))
TN = (((0,), (0,)), ((), ()))


def dot(left, right, dims):
    return lax.dot_general(left, right, dims, preferred_element_type=jnp.float32)


def head_span(head, head_dim):
    first, last = head * head_dim, (head + 1) * head_dim
    low = first // LANES * LANES
    high = -(-last // LANES) * LANES
    return first, last, low, high


def head_mask(first, last, low, high):
    lane = lax.broadcasted_iota(jnp.int32, (1, high - low), 1) + low
    return jnp.where((lane >= first) & (lane < last), 1.0, 0.0).astype(jnp.bfloat16)


def add_tiles(parts, low, value):
    for start in range(0, value.shape[1], LANES):
        tile = (low + start) // LANES
        piece = value[:, start : start + LANES]
        parts[tile] = parts[tile] + piece if tile in parts else piece


def flush_tiles(parts, done, store):
    for tile in sorted(parts):
        if (tile + 1) * LANES <= done:
            store(tile * LANES, parts.pop(tile))


def normalize(tokens):
    center = tokens - jnp.mean(tokens, axis=-1, keepdims=True)
    spread = jnp.mean(center * center, axis=-1, keepdims=True)
    inv_std = lax.rsqrt(spread + 1e-06)
    return center * inv_std, inv_std


def valid_patches(base, count, patches):
    index = base + lax.broadcasted_iota(jnp.int32, (patches, 1), 0)
    return (index < count).astype(jnp.float32)


def forward_kernel(
    clip_ref, count_ref, place_ref,
    tokens_ref, mod_ref, wqkv_ref,
    qkv_ref, prob_ref, att_ref, gdy_ref, grad_ref,
    xmod_ref, same_ref, sum_ref,
):
    frames, both, model = tokens_ref.shape
    patches = both // 2
    rows = frames * patches
    head_dim = model // HEADS
    base = place_ref[0]
    core = place_ref[1]

    def pair_step(step, carry):
        xmods, gdys = [], []
        for k in range(2):
            frame = 2 * step + k
            clip = clip_ref[0, frame]
            shift = mod_ref[clip, pl.ds(0, 1), :]
            scale = mod_ref[clip, pl.ds(1, 1), :]
            gate = mod_ref[clip, pl.ds(2, 1), :]
            both_f = tokens_ref[frame].astype(jnp.float32)
            normed, _ = normalize(both_f[:patches])
            xmods.append(normed * (1.0 + scale) + shift)
            valid = valid_patches(base, count_ref[0, clip], patches)
            gdys.append(valid * gate * both_f[patches:])
        where = pl.ds(pl.multiple_of(step * both, both), both)
        xmod_ref[where, :] = jnp.concatenate(xmods, axis=0).astype(jnp.bfloat16)
        gdy_ref[where, :] = jnp.concatenate(gdys, axis=0).astype(jnp.bfloat16)
        return carry

    lax.fori_loop(0, frames // 2, pair_step, 0)

    starts = []
    for clip in range(1, mod_ref.shape[0]):
        start = jnp.int32(0)
        for frame in range(frames):
            start = start + jnp.where(clip_ref[0, frame] < clip, 1, 0)
        starts.append(start)

    def key_of(index):
        frame = index // patches
        key = index % patches
        for start in starts:
            key = key + jnp.where(frame >= start, patches, 0)
        return key

    key_e = key_of(lax.broadcasted_iota(jnp.int32, (rows, 1), 0))
    key_f = key_of(lax.broadcasted_iota(jnp.int32, (1, rows), 1))
    same_ref[...] = (key_e == key_f).astype(jnp.float32)

    xmod = xmod_ref[...]
    for start in range(0, 3 * model, CHUNK):
        qkv_ref[:, start : start + CHUNK] = dot(
            xmod, wqkv_ref[:, start : start + CHUNK], NN
        ).astype(jnp.bfloat16)

    def store_att(low, value):
        att_ref[:, low : low + LANES] = value.astype(jnp.bfloat16)

    parts = {}
    for head in range(HEADS):
        first, last, low, high = head_span(head, head_dim)
        mask = head_mask(first, last, low, high)
        query = qkv_ref[:, low:high] * mask
        key = qkv_ref[:, model + low : model + high]
        value = qkv_ref[:, 2 * model + low : 2 * model + high] * mask
        expo = jnp.exp(dot(key, query, NT) * head_dim ** (-0.5)) * same_ref[...]
        prob = (expo * (1.0 / jnp.sum(expo, axis=0, keepdims=True))).astype(jnp.bfloat16)
        prob_ref[head] = prob
        add_tiles(parts, low, dot(prob, value, TN))
        flush_tiles(parts, last, store_att)

    att = att_ref[...]
    for start in range(0, model, LANES):
        sum_ref[start : start + LANES, :] = dot(gdy_ref[:, start : start + LANES], att, TN)
    chips = grad_ref.shape[1]
    held = grad_ref.shape[2]
    share = model // (2 * chips)
    for chip in range(0, chips):
        for side in range(2):
            start = (2 * chip + side) * share
            slot = jnp.where(core == side, 0, 1)
            grad_ref[slot, chip] = sum_ref[start : start + held, :].astype(jnp.bfloat16)


def backward_kernel(
    clip_ref, count_ref, place_ref,
    tokens_ref, mod_ref, wqkv_ref, wout_ref, qkv_ref, prob_ref, att_ref, gdy_ref,
    out_ref,
    datt_ref, dqkv_ref, proj_ref, dxmod_ref,
):
    frames, both, model = tokens_ref.shape
    patches = both // 2
    head_dim = model // HEADS
    att_scale = head_dim ** (-0.5)
    base = place_ref[0]

    gdy = gdy_ref[...]
    att = att_ref[...]
    for start in range(0, model, CHUNK):
        datt_ref[:, start : start + CHUNK] = dot(
            gdy, wout_ref[start : start + CHUNK, :], NT
        ).astype(jnp.bfloat16)
    for start in range(0, model, CHUNK):
        proj_ref[:, start : start + CHUNK] = dot(att, wout_ref[:, start : start + CHUNK], NN)

    def store_at(offset, factor):
        def store(low, value):
            dqkv_ref[:, offset + low : offset + low + LANES] = (value * factor).astype(jnp.bfloat16)
        return store

    parts_q, parts_k, parts_v = {}, {}, {}
    for head in range(HEADS):
        first, last, low, high = head_span(head, head_dim)
        mask = head_mask(first, last, low, high)
        query = qkv_ref[:, low:high] * mask
        key = qkv_ref[:, model + low : model + high] * mask
        value = qkv_ref[:, 2 * model + low : 2 * model + high]
        datt = datt_ref[:, low:high] * mask
        prob_low = prob_ref[head]
        add_tiles(parts_v, low, dot(prob_low, datt, NN))
        prob = prob_low.astype(jnp.float32)
        dprob = dot(value, datt, NT)
        total = jnp.sum(prob * dprob, axis=0, keepdims=True)
        dscore = (prob * (dprob - total)).astype(jnp.bfloat16)
        add_tiles(parts_k, low, dot(dscore, query, NN))
        add_tiles(parts_q, low, dot(dscore, key, TN))
        flush_tiles(parts_q, last, store_at(0, att_scale))
        flush_tiles(parts_k, last, store_at(model, att_scale))
        flush_tiles(parts_v, last, store_at(2 * model, 1.0))

    dqkv = dqkv_ref[...]
    for start in range(0, model, CHUNK):
        dxmod_ref[:, start : start + CHUNK] = dot(dqkv, wqkv_ref[start : start + CHUNK, :], NT)

    def frame_step(frame, carry):
        clip = clip_ref[0, frame]
        scale = mod_ref[clip, pl.ds(1, 1), :]
        gate = mod_ref[clip, pl.ds(2, 1), :]
        valid = valid_patches(base, count_ref[0, clip], patches)
        where = pl.ds(pl.multiple_of(frame * patches, patches), patches)
        both_f = tokens_ref[frame].astype(jnp.float32)
        latent = both_f[:patches]
        block_out = latent + valid * gate * proj_ref[where, :]
        normed, inv_std = normalize(latent)
        dnorm = dxmod_ref[where, :] * (1.0 + scale)
        branch = inv_std * (
            dnorm
            - jnp.mean(dnorm, axis=-1, keepdims=True)
            - normed * jnp.mean(dnorm * normed, axis=-1, keepdims=True)
        )
        out_ref[frame] = jnp.concatenate(
            [block_out, both_f[patches:] + branch], axis=0
        ).astype(jnp.bfloat16)
        return carry

    lax.fori_loop(0, frames, frame_step, 0)


def smem():
    return pl.BlockSpec(memory_space=pltpu.SMEM)


def vmem():
    return pl.BlockSpec(memory_space=pltpu.VMEM)


def run_forward(frame_clip, clip_patches, place, tokens, modulation, qkv_weight, chips, held):
    frames, both, model = tokens.shape
    rows = frames * both // 2
    low = jnp.bfloat16
    return pl.pallas_call(
        forward_kernel,
        out_shape=(
            jax.ShapeDtypeStruct((rows, 3 * model), low),
            jax.ShapeDtypeStruct((HEADS, rows, rows), low),
            jax.ShapeDtypeStruct((rows, model), low),
            jax.ShapeDtypeStruct((rows, model), low),
            jax.ShapeDtypeStruct((2, chips, held, model), low),
        ),
        in_specs=[smem()] * 3 + [vmem()] * 3,
        out_specs=(vmem(),) * 5,
        scratch_shapes=[
            pltpu.VMEM((rows, model), low),
            pltpu.VMEM((rows, rows), jnp.float32),
            pltpu.VMEM((model + 16, model), jnp.float32),
        ],
        compiler_params=pltpu.CompilerParams(vmem_limit_bytes=48 * MIB),
        cost_estimate=pl.CostEstimate(
            flops=2 * rows * model * 4 * model, bytes_accessed=12 * MIB, transcendentals=0
        ),
        name="forward",
    )(frame_clip, clip_patches, place, tokens, modulation, qkv_weight)


def run_backward(
    frame_clip, clip_patches, place, tokens, modulation, qkv_weight, out_weight, qkv, prob, att, gdy
):
    frames, both, model = tokens.shape
    rows = frames * both // 2
    low = jnp.bfloat16
    return pl.pallas_call(
        backward_kernel,
        out_shape=jax.ShapeDtypeStruct((frames, both, model), low),
        in_specs=[smem()] * 3 + [vmem()] * 8,
        out_specs=vmem(),
        scratch_shapes=[
            pltpu.VMEM((rows, model), low),
            pltpu.VMEM((rows, 3 * model), low),
            pltpu.VMEM((rows, model), jnp.float32),
            pltpu.VMEM((rows, model), jnp.float32),
        ],
        compiler_params=pltpu.CompilerParams(vmem_limit_bytes=48 * MIB),
        cost_estimate=pl.CostEstimate(
            flops=2 * rows * model * 6 * model, bytes_accessed=16 * MIB, transcendentals=0
        ),
        name="backward",
    )(frame_clip, clip_patches, place, tokens, modulation, qkv_weight, out_weight, qkv, prob, att, gdy)


def per_device(latents, cotangent, qkv_weight, out_weight, modulation, frame_clip, clip_patches):
    seq = lax.axis_size("seq")
    groups = lax.axis_size("dp")
    chips = seq // 2
    patches, model = latents.shape[2], latents.shape[3]
    mine = patches // seq
    share = model // seq
    held = -(-share // 8) * 8
    index = lax.axis_index("seq")
    place = jnp.stack([index * mine, index % 2]).astype(jnp.int32)

    outgoing = jnp.concatenate(
        [latents.reshape(seq, mine, model), cotangent.reshape(seq, mine, model)], axis=1
    )
    tokens = lax.all_to_all(outgoing, "seq", 0, 0, tiled=True)
    qkv, prob, att, gdy, grad = run_forward(
        frame_clip, clip_patches, place, tokens, modulation[0], qkv_weight, chips, held
    )
    other = lax.ppermute(grad[1], "seq", [(i, i ^ 1) for i in range(seq)])
    pair = (grad[0].astype(jnp.float32) + other.astype(jnp.float32)).astype(jnp.bfloat16)
    same_core = [[2 * chip + core for chip in range(chips)] for core in range(2)]
    terms = lax.all_to_all(pair, "seq", 0, 0, tiled=True, axis_index_groups=same_core)
    results = run_backward(
        frame_clip, clip_patches, place, tokens, modulation[0], qkv_weight, out_weight,
        qkv, prob, att, gdy,
    )
    returned = lax.all_to_all(results, "seq", 0, 0, tiled=True)
    block_out = returned[:, :mine].reshape(latents.shape)
    latent_grad = returned[:, mine:].reshape(latents.shape)
    own = jnp.sum(terms.astype(jnp.float32), axis=0).astype(jnp.bfloat16)
    total = own.astype(jnp.float32)
    for step in range(1, groups):
        total = total + lax.ppermute(
            own, "dp", [(i, (i + step) % groups) for i in range(groups)]
        ).astype(jnp.float32)
    return block_out, latent_grad, total[:share]


def solution(mesh):
    in_specs = (
        P("dp", "seq", None, None),
        P("dp", "seq", None, None),
        P(),
        P(),
        P("dp", None, None, None),
        P("dp", None),
        P("dp", None),
    )
    out_specs = (P("dp", "seq", None, None), P("dp", "seq", None, None), P("seq", None))
    return jax.shard_map(
        per_device, mesh=mesh, in_specs=in_specs, out_specs=out_specs, check_vma=False
    )
```

time: 410 us -> 134 us (0.33)
  the two profiles are of different devices: /device:TPU:2 before, /device:TPU:32 now
where the time goes in v1:
time: 134 us; the launch traced here: 133 us
  waiting for transfers between devices  43.2 us (32%)
  Pallas kernels  38.6 us (29%)
  starting transfers between devices  38.2 us (29%)
  local copies, waits for them, and re-layouts  6.35 us (5%)
  other arithmetic  6.3 us (5%)
    pallas_call x1, Pallas kernels, run_backward(): pl.pallas_call(backward_kernel, out_shape=jax.ShapeDtypeStruct((frames, b...  24.5 us
    ppermute x7, starting transfers between devices, per_device(): lax.ppermute(own, 'dp', [(i, (i + step) % groups) for i in range(groups)])  18.8 us
    all_to_all x1, waiting for transfers between devices, per_device(): tokens = lax.all_to_all(outgoing, 'seq', 0, 0, tiled=True)  18.3 us
    pallas_call x1, Pallas kernels, run_forward(): pl.pallas_call(forward_kernel, out_shape=(jax.ShapeDtypeStruct((rows, 3 *...  14.2 us
    all_to_all x1, waiting for transfers between devices, per_device(): returned = lax.all_to_all(results, 'seq', 0, 0, tiled=True)  10.9 us
    ppermute x7, waiting for transfers between devices, per_device(): lax.ppermute(own, 'dp', [(i, (i + step) % groups) for i in range(groups)])  10.7 us
    all_to_all x1, starting transfers between devices, per_device(): tokens = lax.all_to_all(outgoing, 'seq', 0, 0, tiled=True)  7.45 us
    all_to_all x1, starting transfers between devices, per_device(): returned = lax.all_to_all(results, 'seq', 0, 0, tiled=True)  7.21 us
  transfers between devices with their start and end apart: 11, of which 7 were waited for; matrix products, arithmetic and copies ran while one was open for 3% of the time, Pallas kernels for 18%

profile of v1, /device:TPU:32, one launch (start us, length us, event | category | flops | bytes accessed | tf_op | source)
XLA Modules:
  0.0 133.4 jit_solution(12377301712088142700)
XLA Ops:
  0.6 2.4 %pad_maximum_fusion = bf16[32,16,1152]{2,1,0:T(8,128)(2,1)} fusion(bf16[32,8,1152]{2,1,0:T(8,128)(2,1)} %bitcast.18, bf16[32,8,1152]{2,1,0:T(8,128)(2,1)} %bitcast.19), kind=kLoop, calls=%fused_computation.3 | loop fusion | flops 2359296 | bytes 2359296 | tf_op jit(solution)/shard_map/concatenate | solution.py:291
  3.0 7.5 %all-to-all-start = ((bf16[32,16,1152]{2,1,0:T(8,128)(2,1)}), bf16[32,16,1152]{2,1,0:T(8,128)(2,1)S(1)}, u32[]{:S(2)}, u32[]{:S(2)}) async-start(bf16[32,16,1152]{2,1,0:T(8,128)(2,1)} %pad_maximum_fusion), calls=%async_computation | async-start | bytes 2359296 | tf_op jit(solution)/shard_map/all_to_all | solution.py:294
  10.5 0.7 copy.12
  11.1 0.1 pad_add_fusion.place_ref
  11.2 18.3 %all-to-all-done.tokens_ref = bf16[32,16,1152]{2,1,0:T(8,128)(2,1)S(1)} async-done(((bf16[32,16,1152]{2,1,0:T(8,128)(2,1)}), bf16[32,16,1152]{2,1,0:T(8,128)(2,1)S(1)}, u32[]{:S(2)}, u32[]{:S(2)}) %all-to-all-start) | async-done | bytes 1179680 | tf_op jit(solution)/shard_map/all_to_all | solution.py:294
  29.5 0.9 copy-done.2
  30.4 14.2 %forward.1 = (bf16[256,3456]{1,0:T(8,128)(2,1)S(1)}, bf16[16,256,256]{2,1,0:T(8,128)(2,1)}, bf16[256,1152]{1,0:T(8,128)(2,1)S(1)}, bf16[256,1152]{1,0:T(8,128)(2,1)S(1)}, bf16[2,16,40,1152]{3,2,1,0:T(8,128)(2,1)}) custom-call(s32[1,32]{1,0:T(1,128)S(1)} %copy-done.4, s32[1,4]{1,0:T(1,128)S(1)} %copy-done.5, s32[2]{0:T(128)S(1)} %pad_add_fusion.place_ref, ...), custom_call_target="tpu_custom_call" | custom-call | flops 2717908992 | bytes 12582912 | tf_op jit(solution)/shard_map/forward/pallas_call | solution.py:231
  44.5 1.8 %slice_bitcast_fusion = bf16[16,40,1152]{2,1,0:T(8,128)(2,1)S(1)} fusion(bf16[2,16,40,1152]{3,2,1,0:T(8,128)(2,1)} %get-tuple-element.12), kind=kLoop, calls=%fused_computation.2 | loop fusion | bytes 2949120 | tf_op jit(solution)/shard_map/squeeze | solution.py:298
  46.3 0.1 collective-permute-start
  46.4 3.3 %collective-permute-done = bf16[16,40,1152]{2,1,0:T(8,128)(2,1)S(1)} collective-permute-done((bf16[16,40,1152]{2,1,0:T(8,128)(2,1)S(1)}, bf16[16,40,1152]{2,1,0:T(8,128)(2,1)S(1)}, u32[]{:S(2)}, u32[]{:S(2)}) %collective-permute-start) | collective-permute-done | bytes 1474592 | tf_op jit(solution)/shard_map/ppermute | solution.py:298
  49.7 1.5 %fusion = bf16[16,40,1152]{2,1,0:T(8,128)(2,1)} fusion(bf16[16,40,1152]{2,1,0:T(8,128)(2,1)S(1)} %collective-permute-done, bf16[2,16,40,1152]{3,2,1,0:T(8,128)(2,1)S(1)} %copy-done.6), kind=kLoop, calls=%fused_computation.1 | loop fusion | flops 2949120 | bytes 4423680 | tf_op jit(solution)/shard_map/convert_element_type | solution.py:299
  51.1 4.6 %all-to-all-start.2 = ((bf16[16,40,1152]{2,1,0:T(8,128)(2,1)}), bf16[16,40,1152]{2,1,0:T(8,128)(2,1)}, u32[]{:S(2)}, u32[]{:S(2)}) async-start(bf16[16,40,1152]{2,1,0:T(8,128)(2,1)} %fusion), calls=%async_computation.2 | async-start | bytes 2949120 | tf_op jit(solution)/shard_map/all_to_all | solution.py:301
  55.7 0.0 copy-start.1
  55.7 1.1 copy-done.1
  56.8 0.9 copy-done.3
  57.7 24.5 %backward.1 = bf16[32,16,1152]{2,1,0:T(8,128)(2,1)} custom-call(s32[1,32]{1,0:T(1,128)S(1)} %copy-done.4, s32[1,4]{1,0:T(1,128)S(1)} %copy-done.5, s32[2]{0:T(128)S(1)} %pad_add_fusion.place_ref, bf16[32,16,1152]{2,1,0:T(8,128)(2,1)S(1)} %all-to-all-done.tokens_ref, f32[4,3,1152]{2,1,0:T(4,128)S(1)} %bitcast.17, bf16[1152,3456]{1,0:T(8,128)(2,1)} %wqkv_ref.3, ...), custom_call_target="tpu_custom_call" | custom-call | flops 4076863488 | bytes 16777216 | tf_op jit(solution)/shard_map/backward/pallas_call | solution.py:261
  82.2 7.2 %all-to-all-start.1 = ((bf16[32,16,1152]{2,1,0:T(8,128)(2,1)}), bf16[32,16,1152]{2,1,0:T(8,128)(2,1)S(1)}, u32[]{:S(2)}, u32[]{:S(2)}) async-start(bf16[32,16,1152]{2,1,0:T(8,128)(2,1)} %backward.1), calls=%async_computation.1 | async-start | bytes 2359296 | tf_op jit(solution)/shard_map/all_to_all | solution.py:306
  89.4 1.6 %reduce_sum.12 = bf16[40,1152]{1,0:T(8,128)(2,1)S(1)} reduce(bf16[16,40,1152]{2,1,0:T(8,128)(2,1)} %all-to-all-done.2, bf16[]{:T(256)} %constant.21.clone.1), dimensions={0}, to_apply=%region_0.1 | reduce | flops 691200 | bytes 1566722 | tf_op jit(solution)/shard_map/reduce_sum | solution.py:309
  91.0 3.4 %collective-permute-start.2 = (bf16[40,1152]{1,0:T(8,128)(2,1)S(1)}, bf16[40,1152]{1,0:T(8,128)(2,1)S(1)}, u32[]{:S(2)}, u32[]{:S(2)}) collective-permute-start(bf16[40,1152]{1,0:T(8,128)(2,1)S(1)} %reduce_sum.12), channel_id=1, source_target_pairs={{0,64},{32,96},{64,128},{96,160},{128,192},{160,224},{192,0},{224,... | collective-permute-start | bytes 276488 | tf_op jit(solution)/shard_map/ppermute | solution.py:312
  94.3 3.1 %collective-permute-start.1 = (bf16[40,1152]{1,0:T(8,128)(2,1)S(1)}, bf16[40,1152]{1,0:T(8,128)(2,1)S(1)}, u32[]{:S(2)}, u32[]{:S(2)}) collective-permute-start(bf16[40,1152]{1,0:T(8,128)(2,1)S(1)} %reduce_sum.12), channel_id=1, source_target_pairs={{0,32},{32,64},{64,96},{96,128},{128,160},{160,192},{192,224},{224... | collective-permute-start | bytes 276488 | tf_op jit(solution)/shard_map/ppermute | solution.py:312
  97.4 10.9 %all-to-all-done.1 = bf16[32,16,1152]{2,1,0:T(8,128)(2,1)S(1)} async-done(((bf16[32,16,1152]{2,1,0:T(8,128)(2,1)}), bf16[32,16,1152]{2,1,0:T(8,128)(2,1)S(1)}, u32[]{:S(2)}, u32[]{:S(2)}) %all-to-all-start.1) | async-done | bytes 1179680 | tf_op jit(solution)/shard_map/all_to_all | solution.py:306
  108.4 1.1 slice_bitcast_fusion.1
  109.5 0.1 collective-permute-start.7
  109.6 6.3 %collective-permute-start.6 = (bf16[40,1152]{1,0:T(8,128)(2,1)S(1)}, bf16[40,1152]{1,0:T(8,128)(2,1)S(1)}, u32[]{:S(2)}, u32[]{:S(2)}) collective-permute-start(bf16[40,1152]{1,0:T(8,128)(2,1)S(1)} %reduce_sum.12), channel_id=1, source_target_pairs={{0,192},{32,224},{64,0},{96,32},{128,64},{160,96},{192,128},{224,1... | collective-permute-start | bytes 276488 | tf_op jit(solution)/shard_map/ppermute | solution.py:312
  115.9 1.0 collective-permute-start.5
  116.9 4.5 %collective-permute-start.4 = (bf16[40,1152]{1,0:T(8,128)(2,1)S(1)}, bf16[40,1152]{1,0:T(8,128)(2,1)S(1)}, u32[]{:S(2)}, u32[]{:S(2)}) collective-permute-start(bf16[40,1152]{1,0:T(8,128)(2,1)S(1)} %reduce_sum.12), channel_id=1, source_target_pairs={{0,128},{32,160},{64,192},{96,224},{128,0},{160,32},{192,64},{224,... | collective-permute-start | bytes 276488 | tf_op jit(solution)/shard_map/ppermute | solution.py:312
  121.4 0.4 collective-permute-start.3
  121.9 2.7 %collective-permute-done.6 = bf16[40,1152]{1,0:T(8,128)(2,1)S(1)} collective-permute-done((bf16[40,1152]{1,0:T(8,128)(2,1)S(1)}, bf16[40,1152]{1,0:T(8,128)(2,1)S(1)}, u32[]{:S(2)}, u32[]{:S(2)}) %collective-permute-start.6) | collective-permute-done | bytes 92192 | tf_op jit(solution)/shard_map/ppermute | solution.py:312
  124.6 3.0 %collective-permute-done.5 = bf16[40,1152]{1,0:T(8,128)(2,1)S(1)} collective-permute-done((bf16[40,1152]{1,0:T(8,128)(2,1)S(1)}, bf16[40,1152]{1,0:T(8,128)(2,1)S(1)}, u32[]{:S(2)}, u32[]{:S(2)}) %collective-permute-start.5) | collective-permute-done | bytes 92192 | tf_op jit(solution)/shard_map/ppermute | solution.py:312
  127.5 4.6 %collective-permute-done.4 = bf16[40,1152]{1,0:T(8,128)(2,1)S(1)} collective-permute-done((bf16[40,1152]{1,0:T(8,128)(2,1)S(1)}, bf16[40,1152]{1,0:T(8,128)(2,1)S(1)}, u32[]{:S(2)}, u32[]{:S(2)}) %collective-permute-start.4) | collective-permute-done | bytes 92192 | tf_op jit(solution)/shard_map/ppermute | solution.py:312
  132.1 0.5 collective-permute-done.3
  132.6 0.8 fusion.5
  (18 shorter events, 0.1 us)
Async XLA Ops:
  3.0 7.5 %copy-start.7 = (f32[1,4,3,1152]{3,1,2,0:T(4,128)S(1)}, f32[1,4,3,1152]{3,1,2,0:T(4,128)}, u32[]{:S(2)}) copy-start(f32[1,4,3,1152]{3,1,2,0:T(4,128)} %param.11) | copy-start | bytes 165892
  3.0 26.5 %copy-start.4 = (s32[1,32]{1,0:T(1,128)S(1)}, s32[1,32]{1,0:T(1,128)}, u32[]{:S(2)}) copy-start(s32[1,32]{1,0:T(1,128)} %clip_ref.3) | copy-start | bytes 388
  3.0 26.5 %copy-start.5 = (s32[1,4]{1,0:T(1,128)S(1)}, s32[1,4]{1,0:T(1,128)}, u32[]{:S(2)}) copy-start(s32[1,4]{1,0:T(1,128)} %count_ref.3) | copy-start | bytes 52
  3.0 26.5 %all-to-all-start = ((bf16[32,16,1152]{2,1,0:T(8,128)(2,1)}), bf16[32,16,1152]{2,1,0:T(8,128)(2,1)S(1)}, u32[]{:S(2)}, u32[]{:S(2)}) async-start(bf16[32,16,1152]{2,1,0:T(8,128)(2,1)} %pad_maximum_fusion), calls=%async_computation | async-start | bytes 2359296 | tf_op jit(solution)/shard_map/all_to_all | solution.py:294
  29.5 0.9 copy-start.2
  44.5 1.8 %copy-start = (bf16[256,1152]{1,0:T(8,128)(2,1)}, bf16[256,1152]{1,0:T(8,128)(2,1)S(1)}, u32[]{:S(2)}) copy-start(bf16[256,1152]{1,0:T(8,128)(2,1)S(1)} %get-tuple-element.11.gdy_ref) | copy-start | bytes 1769476
  44.5 5.1 %copy-start.6 = (bf16[2,16,40,1152]{3,2,1,0:T(8,128)(2,1)S(1)}, bf16[2,16,40,1152]{3,2,1,0:T(8,128)(2,1)}, u32[]{:S(2)}) copy-start(bf16[2,16,40,1152]{3,2,1,0:T(8,128)(2,1)} %get-tuple-element.12) | copy-start | bytes 8847364
  46.3 3.4 %collective-permute-start = (bf16[16,40,1152]{2,1,0:T(8,128)(2,1)S(1)}, bf16[16,40,1152]{2,1,0:T(8,128)(2,1)S(1)}, u32[]{:S(2)}, u32[]{:S(2)}) collective-permute-start(bf16[16,40,1152]{2,1,0:T(8,128)(2,1)S(1)} %slice_bitcast_fusion), channel_id=1, source_target_pairs={{0,1},{1,0},{2,3},{3,2},{4,5},{5,4},{6,7},{7,6},{8,9},{9,8},{10,11... | collective-permute-start | bytes 4423688 | tf_op jit(solution)/shard_map/ppermute | solution.py:298
  51.1 31.0 %all-to-all-start.2 = ((bf16[16,40,1152]{2,1,0:T(8,128)(2,1)}), bf16[16,40,1152]{2,1,0:T(8,128)(2,1)}, u32[]{:S(2)}, u32[]{:S(2)}) async-start(bf16[16,40,1152]{2,1,0:T(8,128)(2,1)} %fusion), calls=%async_computation.2 | async-start | bytes 2949120 | tf_op jit(solution)/shard_map/all_to_all | solution.py:301
  55.7 1.1 copy-start.1
  56.8 0.9 copy-start.3
  82.2 26.2 %all-to-all-start.1 = ((bf16[32,16,1152]{2,1,0:T(8,128)(2,1)}), bf16[32,16,1152]{2,1,0:T(8,128)(2,1)S(1)}, u32[]{:S(2)}, u32[]{:S(2)}) async-start(bf16[32,16,1152]{2,1,0:T(8,128)(2,1)} %backward.1), calls=%async_computation.1 | async-start | bytes 2359296 | tf_op jit(solution)/shard_map/all_to_all | solution.py:306
  91.0 25.9 %collective-permute-start.2 = (bf16[40,1152]{1,0:T(8,128)(2,1)S(1)}, bf16[40,1152]{1,0:T(8,128)(2,1)S(1)}, u32[]{:S(2)}, u32[]{:S(2)}) collective-permute-start(bf16[40,1152]{1,0:T(8,128)(2,1)S(1)} %reduce_sum.12), channel_id=1, source_target_pairs={{0,64},{32,96},{64,128},{96,160},{128,192},{160,224},{192,0},{224,... | collective-permute-start | bytes 276488 | tf_op jit(solution)/shard_map/ppermute | solution.py:312
  94.3 27.1 %collective-permute-start.1 = (bf16[40,1152]{1,0:T(8,128)(2,1)S(1)}, bf16[40,1152]{1,0:T(8,128)(2,1)S(1)}, u32[]{:S(2)}, u32[]{:S(2)}) collective-permute-start(bf16[40,1152]{1,0:T(8,128)(2,1)S(1)} %reduce_sum.12), channel_id=1, source_target_pairs={{0,32},{32,64},{64,96},{96,128},{128,160},{160,192},{192,224},{224... | collective-permute-start | bytes 276488 | tf_op jit(solution)/shard_map/ppermute | solution.py:312
  109.5 12.4 %collective-permute-start.7 = (bf16[40,1152]{1,0:T(8,128)(2,1)S(1)}, bf16[40,1152]{1,0:T(8,128)(2,1)S(1)}, u32[]{:S(2)}, u32[]{:S(2)}) collective-permute-start(bf16[40,1152]{1,0:T(8,128)(2,1)S(1)} %reduce_sum.12), channel_id=1, source_target_pairs={{0,224},{32,0},{64,32},{96,64},{128,96},{160,128},{192,160},{224,1... | collective-permute-start | bytes 276488 | tf_op jit(solution)/shard_map/ppermute | solution.py:312
  109.6 15.0 %collective-permute-start.6 = (bf16[40,1152]{1,0:T(8,128)(2,1)S(1)}, bf16[40,1152]{1,0:T(8,128)(2,1)S(1)}, u32[]{:S(2)}, u32[]{:S(2)}) collective-permute-start(bf16[40,1152]{1,0:T(8,128)(2,1)S(1)} %reduce_sum.12), channel_id=1, source_target_pairs={{0,192},{32,224},{64,0},{96,32},{128,64},{160,96},{192,128},{224,1... | collective-permute-start | bytes 276488 | tf_op jit(solution)/shard_map/ppermute | solution.py:312
  115.9 11.6 %collective-permute-start.5 = (bf16[40,1152]{1,0:T(8,128)(2,1)S(1)}, bf16[40,1152]{1,0:T(8,128)(2,1)S(1)}, u32[]{:S(2)}, u32[]{:S(2)}) collective-permute-start(bf16[40,1152]{1,0:T(8,128)(2,1)S(1)} %reduce_sum.12), channel_id=1, source_target_pairs={{0,160},{32,192},{64,224},{96,0},{128,32},{160,64},{192,96},{224,1... | collective-permute-start | bytes 276488 | tf_op jit(solution)/shard_map/ppermute | solution.py:312
  116.9 15.2 %collective-permute-start.4 = (bf16[40,1152]{1,0:T(8,128)(2,1)S(1)}, bf16[40,1152]{1,0:T(8,128)(2,1)S(1)}, u32[]{:S(2)}, u32[]{:S(2)}) collective-permute-start(bf16[40,1152]{1,0:T(8,128)(2,1)S(1)} %reduce_sum.12), channel_id=1, source_target_pairs={{0,128},{32,160},{64,192},{96,224},{128,0},{160,32},{192,64},{224,... | collective-permute-start | bytes 276488 | tf_op jit(solution)/shard_map/ppermute | solution.py:312
  121.4 11.2 %collective-permute-start.3 = (bf16[40,1152]{1,0:T(8,128)(2,1)S(1)}, bf16[40,1152]{1,0:T(8,128)(2,1)S(1)}, u32[]{:S(2)}, u32[]{:S(2)}) collective-permute-start(bf16[40,1152]{1,0:T(8,128)(2,1)S(1)} %reduce_sum.12), channel_id=1, source_target_pairs={{0,96},{32,128},{64,160},{96,192},{128,224},{160,0},{192,32},{224,... | collective-permute-start | bytes 276488 | tf_op jit(solution)/shard_map/ppermute | solution.py:312

commit v2 on v1

--- a/solution.py
+++ b/solution.py
@@ -59,7 +59,7 @@
 def forward_kernel(
     clip_ref, count_ref, place_ref,
     tokens_ref, mod_ref, wqkv_ref,
-    qkv_ref, prob_ref, att_ref, gdy_ref, grad_ref,
+    qkv_ref, prob_ref, att_ref, gdy_ref, keep_ref, send_ref,
     xmod_ref, same_ref, sum_ref,
 ):
     frames, both, model = tokens_ref.shape
@@ -74,9 +74,9 @@
         for k in range(2):
             frame = 2 * step + k
             clip = clip_ref[0, frame]
-            shift = mod_ref[clip, pl.ds(0, 1), :]
-            scale = mod_ref[clip, pl.ds(1, 1), :]
-            gate = mod_ref[clip, pl.ds(2, 1), :]
+            shift = mod_ref[0, pl.ds(clip, 1), :]
+            scale = mod_ref[1, pl.ds(clip, 1), :]
+            gate = mod_ref[2, pl.ds(clip, 1), :]
             both_f = tokens_ref[frame].astype(jnp.float32)
             normed, _ = normalize(both_f[:patches])
             xmods.append(normed * (1.0 + scale) + shift)
@@ -87,10 +87,10 @@
         gdy_ref[where, :] = jnp.concatenate(gdys, axis=0).astype(jnp.bfloat16)
         return carry
 
-    lax.fori_loop(0, frames // 2, pair_step, 0)
+    lax.fori_loop(0, frames // 2, pair_step, 0, unroll=4)
 
     starts = []
-    for clip in range(1, mod_ref.shape[0]):
+    for clip in range(1, mod_ref.shape[1]):
         start = jnp.int32(0)
         for frame in range(frames):
             start = start + jnp.where(clip_ref[0, frame] < clip, 1, 0)
@@ -132,14 +132,17 @@
     att = att_ref[...]
     for start in range(0, model, LANES):
         sum_ref[start : start + LANES, :] = dot(gdy_ref[:, start : start + LANES], att, TN)
-    chips = grad_ref.shape[1]
-    held = grad_ref.shape[2]
+    chips, held, _ = keep_ref.shape
     share = model // (2 * chips)
-    for chip in range(0, chips):
-        for side in range(2):
-            start = (2 * chip + side) * share
-            slot = jnp.where(core == side, 0, 1)
-            grad_ref[slot, chip] = sum_ref[start : start + held, :].astype(jnp.bfloat16)
+    for side in range(2):
+
+        def store_share(target_ref, side=side):
+            for chip in range(chips):
+                start = (2 * chip + side) * share
+                target_ref[chip] = sum_ref[start : start + held, :].astype(jnp.bfloat16)
+
+        pl.when(core == side)(lambda: store_share(keep_ref))
+        pl.when(core != side)(lambda: store_share(send_ref))
 
 
 def backward_kernel(
@@ -194,8 +197,8 @@
 
     def frame_step(frame, carry):
         clip = clip_ref[0, frame]
-        scale = mod_ref[clip, pl.ds(1, 1), :]
-        gate = mod_ref[clip, pl.ds(2, 1), :]
+        scale = mod_ref[1, pl.ds(clip, 1), :]
+        gate = mod_ref[2, pl.ds(clip, 1), :]
         valid = valid_patches(base, count_ref[0, clip], patches)
         where = pl.ds(pl.multiple_of(frame * patches, patches), patches)
         both_f = tokens_ref[frame].astype(jnp.float32)
@@ -213,7 +216,7 @@
         ).astype(jnp.bfloat16)
         return carry
 
-    lax.fori_loop(0, frames, frame_step, 0)
+    lax.fori_loop(0, frames, frame_step, 0, unroll=8)
 
 
 def smem():
@@ -235,16 +238,17 @@
             jax.ShapeDtypeStruct((HEADS, rows, rows), low),
             jax.ShapeDtypeStruct((rows, model), low),
             jax.ShapeDtypeStruct((rows, model), low),
-            jax.ShapeDtypeStruct((2, chips, held, model), low),
+            jax.ShapeDtypeStruct((chips, held, model), low),
+            jax.ShapeDtypeStruct((chips, held, model), low),
         ),
         in_specs=[smem()] * 3 + [vmem()] * 3,
-        out_specs=(vmem(),) * 5,
+        out_specs=(vmem(),) * 6,
         scratch_shapes=[
             pltpu.VMEM((rows, model), low),
             pltpu.VMEM((rows, rows), jnp.float32),
             pltpu.VMEM((model + 16, model), jnp.float32),
         ],
-        compiler_params=pltpu.CompilerParams(vmem_limit_bytes=48 * MIB),
+        compiler_params=pltpu.CompilerParams(vmem_limit_bytes=30 * MIB),
         cost_estimate=pl.CostEstimate(
             flops=2 * rows * model * 4 * model, bytes_accessed=12 * MIB, transcendentals=0
         ),
@@ -269,12 +273,50 @@
             pltpu.VMEM((rows, model), jnp.float32),
             pltpu.VMEM((rows, model), jnp.float32),
         ],
-        compiler_params=pltpu.CompilerParams(vmem_limit_bytes=48 * MIB),
+        compiler_params=pltpu.CompilerParams(vmem_limit_bytes=30 * MIB),
         cost_estimate=pl.CostEstimate(
             flops=2 * rows * model * 6 * model, bytes_accessed=16 * MIB, transcendentals=0
         ),
         name="backward",
     )(frame_clip, clip_patches, place, tokens, modulation, qkv_weight, out_weight, qkv, prob, att, gdy)
+
+
+def finish_kernel(returned_ref, own_ref, *refs):
+    other_refs, (block_ref, latent_ref, grad_ref) = refs[:-3], refs[-3:]
+    groups, both, _ = returned_ref.shape
+    patches = both // 2
+    for step in range(groups // 2):
+        pair = [returned_ref[2 * step + k].astype(jnp.float32) for k in range(2)]
+        where = slice(step * both, (step + 1) * both)
+        block_ref[where, :] = jnp.concatenate([part[:patches] for part in pair], axis=0).astype(
+            jnp.bfloat16
+        )
+        latent_ref[where, :] = jnp.concatenate([part[patches:] for part in pair], axis=0).astype(
+            jnp.bfloat16
+        )
+    total = own_ref[...].astype(jnp.float32)
+    for other_ref in other_refs:
+        total = total + other_ref[...].astype(jnp.float32)
+    grad_ref[...] = total[: grad_ref.shape[0]]
+
+
+def run_finish(returned, own, others, share):
+    groups, both, model = returned.shape
+    low = jnp.bfloat16
+    rows = groups * both // 2
+    return pl.pallas_call(
+        finish_kernel,
+        out_shape=(
+            jax.ShapeDtypeStruct((rows, model), low),
+            jax.ShapeDtypeStruct((rows, model), low),
+            jax.ShapeDtypeStruct((share, model), jnp.float32),
+        ),
+        in_specs=[vmem()] * (2 + len(others)),
+        out_specs=(vmem(),) * 3,
+        compiler_params=pltpu.CompilerParams(vmem_limit_bytes=12 * MIB),
+        cost_estimate=pl.CostEstimate(flops=0, bytes_accessed=4 * MIB, transcendentals=0),
+        name="finish",
+    )(returned, own, *others)
 
 
 def per_device(latents, cotangent, qkv_weight, out_weight, modulation, frame_clip, clip_patches):
@@ -292,27 +334,25 @@
         [latents.reshape(seq, mine, model), cotangent.reshape(seq, mine, model)], axis=1
     )
     tokens = lax.all_to_all(outgoing, "seq", 0, 0, tiled=True)
-    qkv, prob, att, gdy, grad = run_forward(
-        frame_clip, clip_patches, place, tokens, modulation[0], qkv_weight, chips, held
-    )
-    other = lax.ppermute(grad[1], "seq", [(i, i ^ 1) for i in range(seq)])
-    pair = (grad[0].astype(jnp.float32) + other.astype(jnp.float32)).astype(jnp.bfloat16)
+    mod = modulation[0].transpose(1, 0, 2)
+    qkv, prob, att, gdy, keep, send = run_forward(
+        frame_clip, clip_patches, place, tokens, mod, qkv_weight, chips, held
+    )
+    other = lax.ppermute(send, "seq", [(i, i ^ 1) for i in range(seq)])
+    pair = (keep.astype(jnp.float32) + other.astype(jnp.float32)).astype(jnp.bfloat16)
     same_core = [[2 * chip + core for chip in range(chips)] for core in range(2)]
     terms = lax.all_to_all(pair, "seq", 0, 0, tiled=True, axis_index_groups=same_core)
     results = run_backward(
-        frame_clip, clip_patches, place, tokens, modulation[0], qkv_weight, out_weight,
-        qkv, prob, att, gdy,
-    )
+        frame_clip, clip_patches, place, tokens, mod, qkv_weight, out_weight, qkv, prob, att, gdy
+    )
+    own = jnp.sum(terms.astype(jnp.float32), axis=0).astype(jnp.bfloat16)
+    others = [
+        lax.ppermute(own, "dp", [(i, (i + step) % groups) for i in range(groups)])
+        for step in range(1, groups)
+    ]
     returned = lax.all_to_all(results, "seq", 0, 0, tiled=True)
-    block_out = returned[:, :mine].reshape(latents.shape)
-    latent_grad = returned[:, mine:].reshape(latents.shape)
-    own = jnp.sum(terms.astype(jnp.float32), axis=0).astype(jnp.bfloat16)
-    total = own.astype(jnp.float32)
-    for step in range(1, groups):
-        total = total + lax.ppermute(
-            own, "dp", [(i, (i + step) % groups) for i in range(groups)]
-        ).astype(jnp.float32)
-    return block_out, latent_grad, total[:share]
+    block_out, latent_grad, total = run_finish(returned, own, others, share)
+    return block_out.reshape(latents.shape), latent_grad.reshape(latents.shape), total
 
 
 def solution(mesh):

time: 134 us -> 115 us (0.86)
  the two profiles are of different devices: /device:TPU:32 before, /device:TPU:2 now
where the time goes in v2:
time: 115 us; the launch traced here: 114 us
  starting transfers between devices  38.5 us (33%)
  waiting for transfers between devices  32.8 us (29%)
  Pallas kernels  21.7 us (19%)
  local copies, waits for them, and re-layouts  14.7 us (13%)
  other arithmetic  5.53 us (5%)
    all_to_all x1, waiting for transfers between devices, per_device(): tokens = lax.all_to_all(outgoing, 'seq', 0, 0, tiled=True)  17.4 us
    ppermute x7, starting transfers between devices, per_device(): lax.ppermute(own, 'dp', [(i, (i + step) % groups) for i in range(groups)])  17.2 us
    unnamed x24, local copies, waits for them, and re-layouts  14.7 us
    pallas_call x1, Pallas kernels, run_backward(): pl.pallas_call(backward_kernel, out_shape=jax.ShapeDtypeStruct((frames, b...  12.9 us
    ppermute x7, waiting for transfers between devices, per_device(): lax.ppermute(own, 'dp', [(i, (i + step) % groups) for i in range(groups)])  12.3 us
    all_to_all x1, starting transfers between devices, per_device(): tokens = lax.all_to_all(outgoing, 'seq', 0, 0, tiled=True)  7.75 us
    pallas_call x1, Pallas kernels, run_forward(): pl.pallas_call(forward_kernel, out_shape=(jax.ShapeDtypeStruct((rows, 3 *...  7.64 us
    all_to_all x1, starting transfers between devices, per_device(): returned = lax.all_to_all(results, 'seq', 0, 0, tiled=True)  7.43 us
  transfers between devices with their start and end apart: 11, of which 6 were waited for; matrix products, arithmetic and copies ran while one was open for 1% of the time, Pallas kernels for 11%

profile of v2, /device:TPU:2, one launch (start us, length us, event | category | flops | bytes accessed | tf_op | source)
XLA Modules:
  0.0 114.0 jit_solution(9112284814745266664)
XLA Ops:
  0.6 2.4 %pad_maximum_fusion = bf16[32,16,1152]{2,1,0:T(8,128)(2,1)} fusion(bf16[32,8,1152]{2,1,0:T(8,128)(2,1)} %bitcast.11, bf16[32,8,1152]{2,1,0:T(8,128)(2,1)} %bitcast.12), kind=kLoop, calls=%fused_computation.1 | loop fusion | flops 2359296 | bytes 2359296 | tf_op jit(solution)/shard_map/concatenate | solution.py:333
  3.0 7.8 %all-to-all-start = ((bf16[32,16,1152]{2,1,0:T(8,128)(2,1)}), bf16[32,16,1152]{2,1,0:T(8,128)(2,1)S(1)}, u32[]{:S(2)}, u32[]{:S(2)}) async-start(bf16[32,16,1152]{2,1,0:T(8,128)(2,1)} %pad_maximum_fusion), calls=%async_computation | async-start | bytes 2359296 | tf_op jit(solution)/shard_map/all_to_all | solution.py:336
  10.8 0.1 pad_add_fusion.place_ref
  10.9 17.4 %all-to-all-done.tokens_ref = bf16[32,16,1152]{2,1,0:T(8,128)(2,1)S(1)} async-done(((bf16[32,16,1152]{2,1,0:T(8,128)(2,1)}), bf16[32,16,1152]{2,1,0:T(8,128)(2,1)S(1)}, u32[]{:S(2)}, u32[]{:S(2)}) %all-to-all-start) | async-done | bytes 1179680 | tf_op jit(solution)/shard_map/all_to_all | solution.py:336
  28.3 3.3 %copy-done = bf16[1152,3456]{1,0:T(8,128)(2,1)S(1)} copy-done((bf16[1152,3456]{1,0:T(8,128)(2,1)S(1)}, bf16[1152,3456]{1,0:T(8,128)(2,1)}, u32[]{:S(2)}) %copy-start) | copy-done | bytes 7962648
  31.6 7.6 %forward.1 = (bf16[256,3456]{1,0:T(8,128)(2,1)S(1)}, bf16[16,256,256]{2,1,0:T(8,128)(2,1)S(1)}, bf16[256,1152]{1,0:T(8,128)(2,1)S(1)}, bf16[256,1152]{1,0:T(8,12...) custom-call(s32[1,32]{1,0:T(1,128)S(1)} %copy-done.10, s32[1,4]{1,0:T(1,128)S(1)} %copy-done.11, ...), custom_call_target="tpu_custom_call" | custom-call | flops 2717908992 | bytes 12582912 | tf_op jit(solution)/shard_map/forward/pallas_call | solution.py:234
  39.2 1.2 %copy-done.3 = bf16[256,3456]{1,0:T(8,128)(2,1)} copy-done((bf16[256,3456]{1,0:T(8,128)(2,1)}, bf16[256,3456]{1,0:T(8,128)(2,1)S(1)}, u32[]{:S(2)}) %copy-start.3) | copy-done | bytes 1769496
  40.5 0.8 copy-done.5
  41.3 0.8 copy-done.7
  42.1 0.2 collective-permute-start
  42.3 3.1 %collective-permute-done = bf16[16,40,1152]{2,1,0:T(8,128)(2,1)S(1)} collective-permute-done((bf16[16,40,1152]{2,1,0:T(8,128)(2,1)S(1)}, bf16[16,40,1152]{2,1,0:T(8,128)(2,1)S(1)}, u32[]{:S(2)}, u32[]{:S(2)}) %collective-permute-start) | collective-permute-done | bytes 1474592 | tf_op jit(solution)/shard_map/ppermute | solution.py:341
  45.4 1.5 %add_convert_fusion = bf16[16,40,1152]{2,1,0:T(8,128)(2,1)} fusion(bf16[16,40,1152]{2,1,0:T(8,128)(2,1)S(1)} %collective-permute-done, bf16[16,40,1152]{2,1,0:T(8,128)(2,1)S(1)} %get-tuple-element.16), kind=kLoop, calls=%fused_computation | loop fusion | flops 2949120 | bytes 4423680 | tf_op jit(solution)/shard_map/convert_element_type | solution.py:342
  46.8 5.9 %all-to-all-start.2 = ((bf16[16,40,1152]{2,1,0:T(8,128)(2,1)}), bf16[16,40,1152]{2,1,0:T(8,128)(2,1)}, u32[]{:S(2)}, u32[]{:S(2)}) async-start(bf16[16,40,1152]{2,1,0:T(8,128)(2,1)} %add_convert_fusion), calls=%async_computation.2 | async-start | bytes 2949120 | tf_op jit(solution)/shard_map/all_to_all | solution.py:344
  52.7 3.3 %copy-done.1 = bf16[1152,3456]{1,0:T(8,128)(2,1)S(1)} copy-done((bf16[1152,3456]{1,0:T(8,128)(2,1)S(1)}, bf16[1152,3456]{1,0:T(8,128)(2,1)}, u32[]{:S(2)}) %copy-start.1) | copy-done | bytes 7962648
  56.0 1.7 %copy-done.2 = bf16[1152,1152]{1,0:T(8,128)(2,1)S(1)} copy-done((bf16[1152,1152]{1,0:T(8,128)(2,1)S(1)}, bf16[1152,1152]{1,0:T(8,128)(2,1)}, u32[]{:S(2)}) %copy-start.2) | copy-done | bytes 2654232
  57.7 1.5 %copy-done.4 = bf16[256,3456]{1,0:T(8,128)(2,1)S(1)} copy-done((bf16[256,3456]{1,0:T(8,128)(2,1)S(1)}, bf16[256,3456]{1,0:T(8,128)(2,1)}, u32[]{:S(2)}) %copy-start.4) | copy-done | bytes 1769496
  59.2 1.1 copy-done.6
  60.3 1.1 copy-done.8
  61.3 12.9 %backward.1 = bf16[32,16,1152]{2,1,0:T(8,128)(2,1)} custom-call(s32[1,32]{1,0:T(1,128)S(1)} %copy-done.10, s32[1,4]{1,0:T(1,128)S(1)} %copy-done.11, s32[2]{0:T(128)S(1)} %pad_add_fusion.place_ref, bf16[32,16,1152]{2,1,0:T(8,128)(2,1)S(1)} %all-to-all-done.tokens_ref, f32[3,4,1152]{2,1,0:T(4,128)S(1)} %bitcast.10, bf16[1152,3456]{1,0:T(8,128)(2,1)S(1)} %copy-done.1, ...), custom_call_target="tpu_custom_call" | custom-call | flops 4076863488 | bytes 16777216 | tf_op jit(solution)/shard_map/backward/pallas_call | solution.py:265
  74.2 7.4 %all-to-all-start.1 = ((bf16[32,16,1152]{2,1,0:T(8,128)(2,1)}), bf16[32,16,1152]{2,1,0:T(8,128)(2,1)S(1)}, u32[]{:S(2)}, u32[]{:S(2)}) async-start(bf16[32,16,1152]{2,1,0:T(8,128)(2,1)} %backward.1), calls=%async_computation.1 | async-start | bytes 2359296 | tf_op jit(solution)/shard_map/all_to_all | solution.py:353
  81.7 1.6 %reduce_sum.12.own_ref = bf16[40,1152]{1,0:T(8,128)(2,1)S(1)} reduce(bf16[16,40,1152]{2,1,0:T(8,128)(2,1)} %all-to-all-done.2, bf16[]{:T(256)} %constant.21.clone.1), dimensions={0}, to_apply=%region_0.1 | reduce | flops 691200 | bytes 1566722 | tf_op jit(solution)/shard_map/reduce_sum | solution.py:348
  83.3 5.9 %collective-permute-start.7 = (bf16[40,1152]{1,0:T(8,128)(2,1)S(1)}, bf16[40,1152]{1,0:T(8,128)(2,1)S(1)}, u32[]{:S(2)}, u32[]{:S(2)}) collective-permute-start(bf16[40,1152]{1,0:T(8,128)(2,1)S(1)} %reduce_sum.12.own_ref), channel_id=1, source_target_pairs={{0,224},{32,0},{64,32},{96,64},{128,96},{160,128},{192,160},{224,1... | collective-permute-start | bytes 276488 | tf_op jit(solution)/shard_map/ppermute | solution.py:350
  89.2 1.5 %collective-permute-start.6 = (bf16[40,1152]{1,0:T(8,128)(2,1)S(1)}, bf16[40,1152]{1,0:T(8,128)(2,1)S(1)}, u32[]{:S(2)}, u32[]{:S(2)}) collective-permute-start(bf16[40,1152]{1,0:T(8,128)(2,1)S(1)} %reduce_sum.12.own_ref), channel_id=1, source_target_pairs={{0,192},{32,224},{64,0},{96,32},{128,64},{160,96},{192,128},{224,1... | collective-permute-start | bytes 276488 | tf_op jit(solution)/shard_map/ppermute | solution.py:350
  90.7 0.4 collective-permute-start.5
  91.1 5.0 %collective-permute-start.4 = (bf16[40,1152]{1,0:T(8,128)(2,1)S(1)}, bf16[40,1152]{1,0:T(8,128)(2,1)S(1)}, u32[]{:S(2)}, u32[]{:S(2)}) collective-permute-start(bf16[40,1152]{1,0:T(8,128)(2,1)S(1)} %reduce_sum.12.own_ref), channel_id=1, source_target_pairs={{0,128},{32,160},{64,192},{96,224},{128,0},{160,32},{192,64},{224,... | collective-permute-start | bytes 276488 | tf_op jit(solution)/shard_map/ppermute | solution.py:350
  96.2 2.4 %collective-permute-start.2 = (bf16[40,1152]{1,0:T(8,128)(2,1)S(1)}, bf16[40,1152]{1,0:T(8,128)(2,1)S(1)}, u32[]{:S(2)}, u32[]{:S(2)}) collective-permute-start(bf16[40,1152]{1,0:T(8,128)(2,1)S(1)} %reduce_sum.12.own_ref), channel_id=1, source_target_pairs={{0,64},{32,96},{64,128},{96,160},{128,192},{160,224},{192,0},{224,... | collective-permute-start | bytes 276488 | tf_op jit(solution)/shard_map/ppermute | solution.py:350
  98.6 1.9 %collective-permute-start.1 = (bf16[40,1152]{1,0:T(8,128)(2,1)S(1)}, bf16[40,1152]{1,0:T(8,128)(2,1)S(1)}, u32[]{:S(2)}, u32[]{:S(2)}) collective-permute-start(bf16[40,1152]{1,0:T(8,128)(2,1)S(1)} %reduce_sum.12.own_ref), channel_id=1, source_target_pairs={{0,32},{32,64},{64,96},{96,128},{128,160},{160,192},{192,224},{224... | collective-permute-start | bytes 276488 | tf_op jit(solution)/shard_map/ppermute | solution.py:350
  100.5 4.8 %collective-permute-done.5.refs_4_ = bf16[40,1152]{1,0:T(8,128)(2,1)S(1)} collective-permute-done((bf16[40,1152]{1,0:T(8,128)(2,1)S(1)}, bf16[40,1152]{1,0:T(8,128)(2,1)S(1)}, u32[]{:S(2)}, u32[]{:S(2)}) %collective-permute-start.5) | collective-permute-done | bytes 92192 | tf_op jit(solution)/shard_map/ppermute | solution.py:350
  105.3 4.1 %collective-permute-done.3.refs_2_ = bf16[40,1152]{1,0:T(8,128)(2,1)S(1)} collective-permute-done((bf16[40,1152]{1,0:T(8,128)(2,1)S(1)}, bf16[40,1152]{1,0:T(8,128)(2,1)S(1)}, u32[]{:S(2)}, u32[]{:S(2)}) %collective-permute-start.3) | collective-permute-done | bytes 92192 | tf_op jit(solution)/shard_map/ppermute | solution.py:350
  109.4 2.6 %collective-permute-done.2.refs_1_ = bf16[40,1152]{1,0:T(8,128)(2,1)S(1)} collective-permute-done((bf16[40,1152]{1,0:T(8,128)(2,1)S(1)}, bf16[40,1152]{1,0:T(8,128)(2,1)S(1)}, u32[]{:S(2)}, u32[]{:S(2)}) %collective-permute-start.2) | collective-permute-done | bytes 92192 | tf_op jit(solution)/shard_map/ppermute | solution.py:350
  112.0 0.8 collective-permute-done.1.refs_0_
  112.8 1.2 %finish.1 = (bf16[256,1152]{1,0:T(8,128)(2,1)}, bf16[256,1152]{1,0:T(8,128)(2,1)}, f32[36,1152]{1,0:T(8,128)}) custom-call(bf16[32,16,1152]{2,1,0:T(8,128)(2,1)S(1)} %all-to-all-done.1.returned_ref, bf16[40,1152]{1,0:T(8,128)(2,1)S(1)} %reduce_sum.12.own_ref, bf16[40,1152]{1,0:T(8,128)(2,1)S(1)} %collective-permute-done.1.refs_0_, ...), custom_call_target="tpu_custom_call" | custom-call | bytes 4194304 | tf_op jit(solution)/shard_map/finish/pallas_call | solution.py:307
  (21 shorter events, 0.0 us)
Async XLA Ops:
  3.0 25.3 %copy-start.9 = (f32[1,4,3,1152]{3,1,2,0:T(4,128)S(1)}, f32[1,4,3,1152]{3,1,2,0:T(4,128)}, u32[]{:S(2)}) copy-start(f32[1,4,3,1152]{3,1,2,0:T(4,128)} %param.11) | copy-start | bytes 165892
  3.0 25.3 %copy-start.10 = (s32[1,32]{1,0:T(1,128)S(1)}, s32[1,32]{1,0:T(1,128)}, u32[]{:S(2)}) copy-start(s32[1,32]{1,0:T(1,128)} %clip_ref.3) | copy-start | bytes 388
  3.0 25.3 %copy-start.11 = (s32[1,4]{1,0:T(1,128)S(1)}, s32[1,4]{1,0:T(1,128)}, u32[]{:S(2)}) copy-start(s32[1,4]{1,0:T(1,128)} %count_ref.3) | copy-start | bytes 52
  3.0 25.3 %all-to-all-start = ((bf16[32,16,1152]{2,1,0:T(8,128)(2,1)}), bf16[32,16,1152]{2,1,0:T(8,128)(2,1)S(1)}, u32[]{:S(2)}, u32[]{:S(2)}) async-start(bf16[32,16,1152]{2,1,0:T(8,128)(2,1)} %pad_maximum_fusion), calls=%async_computation | async-start | bytes 2359296 | tf_op jit(solution)/shard_map/all_to_all | solution.py:336
  28.3 3.3 %copy-start = (bf16[1152,3456]{1,0:T(8,128)(2,1)S(1)}, bf16[1152,3456]{1,0:T(8,128)(2,1)}, u32[]{:S(2)}) copy-start(bf16[1152,3456]{1,0:T(8,128)(2,1)} %wqkv_ref.3) | copy-start | bytes 23887876
  39.2 1.2 %copy-start.3 = (bf16[256,3456]{1,0:T(8,128)(2,1)}, bf16[256,3456]{1,0:T(8,128)(2,1)S(1)}, u32[]{:S(2)}) copy-start(bf16[256,3456]{1,0:T(8,128)(2,1)S(1)} %get-tuple-element.12.qkv_ref) | copy-start | bytes 5308420
  40.5 0.8 copy-start.5
  41.3 0.8 copy-start.7
  42.1 3.3 %collective-permute-start = (bf16[16,40,1152]{2,1,0:T(8,128)(2,1)S(1)}, bf16[16,40,1152]{2,1,0:T(8,128)(2,1)S(1)}, u32[]{:S(2)}, u32[]{:S(2)}) collective-permute-start(bf16[16,40,1152]{2,1,0:T(8,128)(2,1)S(1)} %get-tuple-element.17), channel_id=1, source_target_pairs={{0,1},{1,0},{2,3},{3,2},{4,5},{5,4},{6,7},{7,6},{8,9},{9,8},{10,11... | collective-permute-start | bytes 4423688 | tf_op jit(solution)/shard_map/ppermute | solution.py:341
  46.8 27.4 %all-to-all-start.2 = ((bf16[16,40,1152]{2,1,0:T(8,128)(2,1)}), bf16[16,40,1152]{2,1,0:T(8,128)(2,1)}, u32[]{:S(2)}, u32[]{:S(2)}) async-start(bf16[16,40,1152]{2,1,0:T(8,128)(2,1)} %add_convert_fusion), calls=%async_computation.2 | async-start | bytes 2949120 | tf_op jit(solution)/shard_map/all_to_all | solution.py:344
  52.7 3.3 %copy-start.1 = (bf16[1152,3456]{1,0:T(8,128)(2,1)S(1)}, bf16[1152,3456]{1,0:T(8,128)(2,1)}, u32[]{:S(2)}) copy-start(bf16[1152,3456]{1,0:T(8,128)(2,1)} %wqkv_ref.3) | copy-start | bytes 23887876
  56.0 1.7 %copy-start.2 = (bf16[1152,1152]{1,0:T(8,128)(2,1)S(1)}, bf16[1152,1152]{1,0:T(8,128)(2,1)}, u32[]{:S(2)}) copy-start(bf16[1152,1152]{1,0:T(8,128)(2,1)} %wout_ref.1) | copy-start | bytes 7962628
  57.7 1.5 %copy-start.4 = (bf16[256,3456]{1,0:T(8,128)(2,1)S(1)}, bf16[256,3456]{1,0:T(8,128)(2,1)}, u32[]{:S(2)}) copy-start(bf16[256,3456]{1,0:T(8,128)(2,1)} %copy-done.3) | copy-start | bytes 5308420
  59.2 1.1 copy-start.6
  60.3 1.1 copy-start.8
  74.2 26.3 %all-to-all-start.1 = ((bf16[32,16,1152]{2,1,0:T(8,128)(2,1)}), bf16[32,16,1152]{2,1,0:T(8,128)(2,1)S(1)}, u32[]{:S(2)}, u32[]{:S(2)}) async-start(bf16[32,16,1152]{2,1,0:T(8,128)(2,1)} %backward.1), calls=%async_computation.1 | async-start | bytes 2359296 | tf_op jit(solution)/shard_map/all_to_all | solution.py:353
  83.3 12.9 %collective-permute-start.7 = (bf16[40,1152]{1,0:T(8,128)(2,1)S(1)}, bf16[40,1152]{1,0:T(8,128)(2,1)S(1)}, u32[]{:S(2)}, u32[]{:S(2)}) collective-permute-start(bf16[40,1152]{1,0:T(8,128)(2,1)S(1)} %reduce_sum.12.own_ref), channel_id=1, source_target_pairs={{0,224},{32,0},{64,32},{96,64},{128,96},{160,128},{192,160},{224,1... | collective-permute-start | bytes 276488 | tf_op jit(solution)/shard_map/ppermute | solution.py:350
  89.2 9.4 %collective-permute-start.6 = (bf16[40,1152]{1,0:T(8,128)(2,1)S(1)}, bf16[40,1152]{1,0:T(8,128)(2,1)S(1)}, u32[]{:S(2)}, u32[]{:S(2)}) collective-permute-start(bf16[40,1152]{1,0:T(8,128)(2,1)S(1)} %reduce_sum.12.own_ref), channel_id=1, source_target_pairs={{0,192},{32,224},{64,0},{96,32},{128,64},{160,96},{192,128},{224,1... | collective-permute-start | bytes 276488 | tf_op jit(solution)/shard_map/ppermute | solution.py:350
  90.7 14.6 %collective-permute-start.5 = (bf16[40,1152]{1,0:T(8,128)(2,1)S(1)}, bf16[40,1152]{1,0:T(8,128)(2,1)S(1)}, u32[]{:S(2)}, u32[]{:S(2)}) collective-permute-start(bf16[40,1152]{1,0:T(8,128)(2,1)S(1)} %reduce_sum.12.own_ref), channel_id=1, source_target_pairs={{0,160},{32,192},{64,224},{96,0},{128,32},{160,64},{192,96},{224,1... | collective-permute-start | bytes 276488 | tf_op jit(solution)/shard_map/ppermute | solution.py:350
  91.1 14.2 %collective-permute-start.4 = (bf16[40,1152]{1,0:T(8,128)(2,1)S(1)}, bf16[40,1152]{1,0:T(8,128)(2,1)S(1)}, u32[]{:S(2)}, u32[]{:S(2)}) collective-permute-start(bf16[40,1152]{1,0:T(8,128)(2,1)S(1)} %reduce_sum.12.own_ref), channel_id=1, source_target_pairs={{0,128},{32,160},{64,192},{96,224},{128,0},{160,32},{192,64},{224,... | collective-permute-start | bytes 276488 | tf_op jit(solution)/shard_map/ppermute | solution.py:350
  96.1 13.3 %collective-permute-start.3 = (bf16[40,1152]{1,0:T(8,128)(2,1)S(1)}, bf16[40,1152]{1,0:T(8,128)(2,1)S(1)}, u32[]{:S(2)}, u32[]{:S(2)}) collective-permute-start(bf16[40,1152]{1,0:T(8,128)(2,1)S(1)} %reduce_sum.12.own_ref), channel_id=1, source_target_pairs={{0,96},{32,128},{64,160},{96,192},{128,224},{160,0},{192,32},{224,... | collective-permute-start | bytes 276488 | tf_op jit(solution)/shard_map/ppermute | solution.py:350
  96.2 15.8 %collective-permute-start.2 = (bf16[40,1152]{1,0:T(8,128)(2,1)S(1)}, bf16[40,1152]{1,0:T(8,128)(2,1)S(1)}, u32[]{:S(2)}, u32[]{:S(2)}) collective-permute-start(bf16[40,1152]{1,0:T(8,128)(2,1)S(1)} %reduce_sum.12.own_ref), channel_id=1, source_target_pairs={{0,64},{32,96},{64,128},{96,160},{128,192},{160,224},{192,0},{224,... | collective-permute-start | bytes 276488 | tf_op jit(solution)/shard_map/ppermute | solution.py:350
  98.6 14.2 %collective-permute-start.1 = (bf16[40,1152]{1,0:T(8,128)(2,1)S(1)}, bf16[40,1152]{1,0:T(8,128)(2,1)S(1)}, u32[]{:S(2)}, u32[]{:S(2)}) collective-permute-start(bf16[40,1152]{1,0:T(8,128)(2,1)S(1)} %reduce_sum.12.own_ref), channel_id=1, source_target_pairs={{0,32},{32,64},{64,96},{96,128},{128,160},{160,192},{192,224},{224... | collective-permute-start | bytes 276488 | tf_op jit(solution)/shard_map/ppermute | solution.py:350

commit v3 on v2

--- a/solution.py
+++ b/solution.py
@@ -8,6 +8,7 @@
 HEADS = 16
 LANES = 128
 CHUNK = 384
+SHARE_ROWS = 40
 MIB = 1024 * 1024
 
 NN = (((1,), (0,)), ((), ()))
@@ -57,10 +58,10 @@
 
 
 def forward_kernel(
-    clip_ref, count_ref, place_ref,
-    tokens_ref, mod_ref, wqkv_ref,
-    qkv_ref, prob_ref, att_ref, gdy_ref, keep_ref, send_ref,
-    xmod_ref, same_ref, sum_ref,
+    clip_ref, count_ref, place_ref, tokens_ref, mod_ref, wqkv_hbm,
+    qkv_hbm, prob_hbm, att_hbm, gdy_hbm, keep_ref, send_ref,
+    wqkv_ref, qkv_ref, prob_ref, att_ref, gdy_ref, xmod_ref, same_ref, turned_ref, share_ref,
+    load_sems, store_sems,
 ):
     frames, both, model = tokens_ref.shape
     patches = both // 2
@@ -68,6 +69,15 @@
     head_dim = model // HEADS
     base = place_ref[0]
     core = place_ref[1]
+
+    loads = []
+    for step, start in enumerate(range(0, 3 * model, CHUNK)):
+        columns = slice(start, start + CHUNK)
+        load = pltpu.make_async_copy(
+            wqkv_hbm.at[:, columns], wqkv_ref.at[:, columns], load_sems.at[step]
+        )
+        load.start()
+        loads.append(load)
 
     def pair_step(step, carry):
         xmods, gdys = [], []
@@ -89,6 +99,15 @@
 
     lax.fori_loop(0, frames // 2, pair_step, 0, unroll=4)
 
+    stores = []
+
+    def store_out(source_ref, target_hbm):
+        store = pltpu.make_async_copy(source_ref, target_hbm, store_sems.at[len(stores)])
+        store.start()
+        stores.append(store)
+
+    store_out(gdy_ref, gdy_hbm)
+
     starts = []
     for clip in range(1, mod_ref.shape[1]):
         start = jnp.int32(0)
@@ -107,11 +126,30 @@
     key_f = key_of(lax.broadcasted_iota(jnp.int32, (1, rows), 1))
     same_ref[...] = (key_e == key_f).astype(jnp.float32)
 
+    chips, held = share_ref.shape[1] // SHARE_ROWS, SHARE_ROWS
+    share = model // (2 * chips)
+    for start in range(0, model, LANES):
+        turned_ref[start : start + LANES, :] = gdy_ref[:, start : start + LANES].astype(
+            jnp.float32
+        ).T
+    turned_ref[model:, :] = jnp.zeros((turned_ref.shape[0] - model, rows), jnp.float32)
+    for side in range(2):
+        for chip in range(0, chips, 2):
+            pieces = []
+            for k in range(2):
+                start = (2 * (chip + k) + side) * share
+                pieces.append(turned_ref[start : start + held, :])
+            share_ref[side, chip * held : (chip + 2) * held, :] = jnp.concatenate(
+                pieces, axis=0
+            ).astype(jnp.bfloat16)
+
     xmod = xmod_ref[...]
-    for start in range(0, 3 * model, CHUNK):
+    for step, start in enumerate(range(0, 3 * model, CHUNK)):
+        loads[step].wait()
         qkv_ref[:, start : start + CHUNK] = dot(
             xmod, wqkv_ref[:, start : start + CHUNK], NN
         ).astype(jnp.bfloat16)
+    store_out(qkv_ref, qkv_hbm)
 
     def store_att(low, value):
         att_ref[:, low : low + LANES] = value.astype(jnp.bfloat16)
@@ -128,28 +166,24 @@
         prob_ref[head] = prob
         add_tiles(parts, low, dot(prob, value, TN))
         flush_tiles(parts, last, store_att)
-
-    att = att_ref[...]
-    for start in range(0, model, LANES):
-        sum_ref[start : start + LANES, :] = dot(gdy_ref[:, start : start + LANES], att, TN)
-    chips, held, _ = keep_ref.shape
-    share = model // (2 * chips)
-    for side in range(2):
-
-        def store_share(target_ref, side=side):
-            for chip in range(chips):
-                start = (2 * chip + side) * share
-                target_ref[chip] = sum_ref[start : start + held, :].astype(jnp.bfloat16)
-
-        pl.when(core == side)(lambda: store_share(keep_ref))
-        pl.when(core != side)(lambda: store_share(send_ref))
+    store_out(att_ref, att_hbm)
+    store_out(prob_ref, prob_hbm)
+
+    for target_ref, side in ((send_ref, 1 - core), (keep_ref, core)):
+        for start in range(0, model, CHUNK):
+            target_ref[:, start : start + CHUNK] = dot(
+                share_ref[side], att_ref[:, start : start + CHUNK], NN
+            ).astype(jnp.bfloat16)
+    for store in stores:
+        store.wait()
 
 
 def backward_kernel(
-    clip_ref, count_ref, place_ref,
-    tokens_ref, mod_ref, wqkv_ref, wout_ref, qkv_ref, prob_ref, att_ref, gdy_ref,
+    clip_ref, count_ref, place_ref, tokens_ref, mod_ref,
+    gdy_hbm, wout_hbm, att_hbm, qkv_hbm, prob_hbm, wqkv_hbm,
     out_ref,
-    datt_ref, dqkv_ref, proj_ref, dxmod_ref,
+    gdy_ref, wout_ref, att_ref, qkv_ref, prob_ref, wqkv_ref,
+    datt_ref, dqkv_ref, proj_ref, dxmod_ref, sems,
 ):
     frames, both, model = tokens_ref.shape
     patches = both // 2
@@ -157,14 +191,28 @@
     att_scale = head_dim ** (-0.5)
     base = place_ref[0]
 
+    loads = []
+    for source_hbm, target_ref in (
+        (gdy_hbm, gdy_ref), (wout_hbm, wout_ref), (att_hbm, att_ref),
+        (qkv_hbm, qkv_ref), (prob_hbm, prob_ref), (wqkv_hbm, wqkv_ref),
+    ):
+        load = pltpu.make_async_copy(source_hbm, target_ref, sems.at[len(loads)])
+        load.start()
+        loads.append(load)
+
+    loads[0].wait()
+    loads[1].wait()
     gdy = gdy_ref[...]
-    att = att_ref[...]
     for start in range(0, model, CHUNK):
         datt_ref[:, start : start + CHUNK] = dot(
             gdy, wout_ref[start : start + CHUNK, :], NT
         ).astype(jnp.bfloat16)
+    loads[2].wait()
+    att = att_ref[...]
     for start in range(0, model, CHUNK):
         proj_ref[:, start : start + CHUNK] = dot(att, wout_ref[:, start : start + CHUNK], NN)
+    loads[3].wait()
+    loads[4].wait()
 
     def store_at(offset, factor):
         def store(low, value):
@@ -191,6 +239,7 @@
         flush_tiles(parts_k, last, store_at(model, att_scale))
         flush_tiles(parts_v, last, store_at(2 * model, 1.0))
 
+    loads[5].wait()
     dqkv = dqkv_ref[...]
     for start in range(0, model, CHUNK):
         dxmod_ref[:, start : start + CHUNK] = dot(dqkv, wqkv_ref[start : start + CHUNK, :], NT)
@@ -227,28 +276,32 @@
     return pl.BlockSpec(memory_space=pltpu.VMEM)
 
 
-def run_forward(frame_clip, clip_patches, place, tokens, modulation, qkv_weight, chips, held):
+def hbm():
+    return pl.BlockSpec(memory_space=pltpu.HBM)
+
+
+def run_forward(frame_clip, clip_patches, place, tokens, modulation, qkv_weight, chips):
     frames, both, model = tokens.shape
     rows = frames * both // 2
     low = jnp.bfloat16
+    sizes = ((rows, 3 * model), (HEADS, rows, rows), (rows, model), (rows, model))
     return pl.pallas_call(
         forward_kernel,
-        out_shape=(
-            jax.ShapeDtypeStruct((rows, 3 * model), low),
-            jax.ShapeDtypeStruct((HEADS, rows, rows), low),
-            jax.ShapeDtypeStruct((rows, model), low),
-            jax.ShapeDtypeStruct((rows, model), low),
-            jax.ShapeDtypeStruct((chips, held, model), low),
-            jax.ShapeDtypeStruct((chips, held, model), low),
-        ),
-        in_specs=[smem()] * 3 + [vmem()] * 3,
-        out_specs=(vmem(),) * 6,
-        scratch_shapes=[
+        out_shape=tuple(jax.ShapeDtypeStruct(size, low) for size in sizes)
+        + (jax.ShapeDtypeStruct((chips * SHARE_ROWS, model), low),) * 2,
+        in_specs=[smem()] * 3 + [vmem()] * 2 + [hbm()],
+        out_specs=(hbm(),) * 4 + (vmem(),) * 2,
+        scratch_shapes=[pltpu.VMEM((model, 3 * model), low)]
+        + [pltpu.VMEM(size, low) for size in sizes]
+        + [
             pltpu.VMEM((rows, model), low),
             pltpu.VMEM((rows, rows), jnp.float32),
-            pltpu.VMEM((model + 16, model), jnp.float32),
+            pltpu.VMEM((model + 16, rows), jnp.float32),
+            pltpu.VMEM((2, chips * SHARE_ROWS, rows), low),
+            pltpu.SemaphoreType.DMA((3 * model // CHUNK,)),
+            pltpu.SemaphoreType.DMA((4,)),
         ],
-        compiler_params=pltpu.CompilerParams(vmem_limit_bytes=30 * MIB),
+        compiler_params=pltpu.CompilerParams(vmem_limit_bytes=32 * MIB),
         cost_estimate=pl.CostEstimate(
             flops=2 * rows * model * 4 * model, bytes_accessed=12 * MIB, transcendentals=0
         ),
@@ -257,32 +310,80 @@
 
 
 def run_backward(
-    frame_clip, clip_patches, place, tokens, modulation, qkv_weight, out_weight, qkv, prob, att, gdy
+    frame_clip, clip_patches, place, tokens, modulation, gdy, out_weight, att, qkv, prob, qkv_weight
 ):
     frames, both, model = tokens.shape
     rows = frames * both // 2
     low = jnp.bfloat16
+    loaded = (gdy, out_weight, att, qkv, prob, qkv_weight)
     return pl.pallas_call(
         backward_kernel,
         out_shape=jax.ShapeDtypeStruct((frames, both, model), low),
-        in_specs=[smem()] * 3 + [vmem()] * 8,
+        in_specs=[smem()] * 3 + [vmem()] * 2 + [hbm()] * len(loaded),
         out_specs=vmem(),
-        scratch_shapes=[
+        scratch_shapes=[pltpu.VMEM(array.shape, low) for array in loaded]
+        + [
             pltpu.VMEM((rows, model), low),
             pltpu.VMEM((rows, 3 * model), low),
             pltpu.VMEM((rows, model), jnp.float32),
             pltpu.VMEM((rows, model), jnp.float32),
+            pltpu.SemaphoreType.DMA((len(loaded),)),
         ],
-        compiler_params=pltpu.CompilerParams(vmem_limit_bytes=30 * MIB),
+        compiler_params=pltpu.CompilerParams(vmem_limit_bytes=32 * MIB),
         cost_estimate=pl.CostEstimate(
             flops=2 * rows * model * 6 * model, bytes_accessed=16 * MIB, transcendentals=0
         ),
         name="backward",
-    )(frame_clip, clip_patches, place, tokens, modulation, qkv_weight, out_weight, qkv, prob, att, gdy)
-
-
-def finish_kernel(returned_ref, own_ref, *refs):
-    other_refs, (block_ref, latent_ref, grad_ref) = refs[:-3], refs[-3:]
+    )(frame_clip, clip_patches, place, tokens, modulation, *loaded)
+
+
+def pack_kernel(latent_ref, cotangent_ref, out_ref):
+    both = out_ref.shape[1]
+    patches = both // 2
+    for step in range(out_ref.shape[0] // 2):
+        where = slice(step * both, (step + 1) * both)
+        latent = latent_ref[where, :].astype(jnp.float32)
+        cotangent = cotangent_ref[where, :].astype(jnp.float32)
+        for k in range(2):
+            half = slice(k * patches, (k + 1) * patches)
+            out_ref[2 * step + k] = jnp.concatenate([latent[half], cotangent[half]], axis=0).astype(
+                jnp.bfloat16
+            )
+
+
+def run_pack(latents, cotangent, seq):
+    rows, model = latents.shape
+    return pl.pallas_call(
+        pack_kernel,
+        out_shape=jax.ShapeDtypeStruct((seq, 2 * rows // seq, model), jnp.bfloat16),
+        in_specs=[vmem()] * 2,
+        out_specs=vmem(),
+        compiler_params=pltpu.CompilerParams(vmem_limit_bytes=12 * MIB),
+        name="pack",
+    )(latents, cotangent)
+
+
+def add_kernel(left_ref, right_ref, out_ref):
+    step_rows = 64
+    for start in range(0, left_ref.shape[0], step_rows):
+        where = slice(start, start + step_rows)
+        out_ref[where, :] = (
+            left_ref[where, :].astype(jnp.float32) + right_ref[where, :].astype(jnp.float32)
+        ).astype(jnp.bfloat16)
+
+
+def run_add(left, right):
+    return pl.pallas_call(
+        add_kernel,
+        out_shape=jax.ShapeDtypeStruct(left.shape, left.dtype),
+        in_specs=[vmem()] * 2,
+        out_specs=vmem(),
+        compiler_params=pltpu.CompilerParams(vmem_limit_bytes=12 * MIB),
+        name="add",
+    )(left, right)
+
+
+def finish_kernel(returned_ref, left_ref, right_ref, block_ref, latent_ref, grad_ref):
     groups, both, _ = returned_ref.shape
     patches = both // 2
     for step in range(groups // 2):
@@ -294,13 +395,11 @@
         latent_ref[where, :] = jnp.concatenate([part[patches:] for part in pair], axis=0).astype(
             jnp.bfloat16
         )
-    total = own_ref[...].astype(jnp.float32)
-    for other_ref in other_refs:
-        total = total + other_ref[...].astype(jnp.float32)
+    total = left_ref[...].astype(jnp.float32) + right_ref[...].astype(jnp.float32)
     grad_ref[...] = total[: grad_ref.shape[0]]
 
 
-def run_finish(returned, own, others, share):
+def run_finish(returned, left, right, share):
     groups, both, model = returned.shape
     low = jnp.bfloat16
     rows = groups * both // 2
@@ -311,12 +410,12 @@
             jax.ShapeDtypeStruct((rows, model), low),
             jax.ShapeDtypeStruct((share, model), jnp.float32),
         ),
-        in_specs=[vmem()] * (2 + len(others)),
+        in_specs=[vmem()] * 3,
         out_specs=(vmem(),) * 3,
         compiler_params=pltpu.CompilerParams(vmem_limit_bytes=12 * MIB),
         cost_estimate=pl.CostEstimate(flops=0, bytes_accessed=4 * MIB, transcendentals=0),
         name="finish",
-    )(returned, own, *others)
+    )(returned, left, right)
 
 
 def per_device(latents, cotangent, qkv_weight, out_weight, modulation, frame_clip, clip_patches):
@@ -326,33 +425,33 @@
     patches, model = latents.shape[2], latents.shape[3]
     mine = patches // seq
     share = model // seq
-    held = -(-share // 8) * 8
     index = lax.axis_index("seq")
     place = jnp.stack([index * mine, index % 2]).astype(jnp.int32)
 
-    outgoing = jnp.concatenate(
-        [latents.reshape(seq, mine, model), cotangent.reshape(seq, mine, model)], axis=1
-    )
+    outgoing = run_pack(latents.reshape(patches, model), cotangent.reshape(patches, model), seq)
     tokens = lax.all_to_all(outgoing, "seq", 0, 0, tiled=True)
     mod = modulation[0].transpose(1, 0, 2)
     qkv, prob, att, gdy, keep, send = run_forward(
-        frame_clip, clip_patches, place, tokens, mod, qkv_weight, chips, held
+        frame_clip, clip_patches, place, tokens, mod, qkv_weight, chips
     )
     other = lax.ppermute(send, "seq", [(i, i ^ 1) for i in range(seq)])
-    pair = (keep.astype(jnp.float32) + other.astype(jnp.float32)).astype(jnp.bfloat16)
+    pair = run_add(keep, other).reshape(chips, SHARE_ROWS, model)
     same_core = [[2 * chip + core for chip in range(chips)] for core in range(2)]
     terms = lax.all_to_all(pair, "seq", 0, 0, tiled=True, axis_index_groups=same_core)
     results = run_backward(
-        frame_clip, clip_patches, place, tokens, mod, qkv_weight, out_weight, qkv, prob, att, gdy
+        frame_clip, clip_patches, place, tokens, mod, gdy, out_weight, att, qkv, prob, qkv_weight
     )
-    own = jnp.sum(terms.astype(jnp.float32), axis=0).astype(jnp.bfloat16)
-    others = [
-        lax.ppermute(own, "dp", [(i, (i + step) % groups) for i in range(groups)])
-        for step in range(1, groups)
-    ]
+    total = jnp.sum(terms.astype(jnp.float32), axis=0).astype(jnp.bfloat16)
+    stride = 1
+    while True:
+        met = lax.ppermute(total, "dp", [(i, i ^ stride) for i in range(groups)])
+        stride *= 2
+        if stride >= groups:
+            break
+        total = (total.astype(jnp.float32) + met.astype(jnp.float32)).astype(jnp.bfloat16)
     returned = lax.all_to_all(results, "seq", 0, 0, tiled=True)
-    block_out, latent_grad, total = run_finish(returned, own, others, share)
-    return block_out.reshape(latents.shape), latent_grad.reshape(latents.shape), total
+    block_out, latent_grad, grad = run_finish(returned, total, met, share)
+    return block_out.reshape(latents.shape), latent_grad.reshape(latents.shape), grad
 
 
 def solution(mesh):

time: 115 us -> 127 us (1.10)
  blocking collectives: 0 us -> 25.9 us
  starting transfers between devices: 38.5 us -> 24.8 us
  Pallas kernels: 21.7 us -> 29.2 us
  waiting for transfers between devices: 32.8 us -> 28.5 us
  other arithmetic: 5.53 us -> 1.72 us
    all_to_all x0 -> x1, blocking collectives: none -> 25.9 us  [per_device(): lax.all_to_all(pair, 'seq', 0, 0, tiled=True, axis_index_groups=same_core)]
    ppermute x7 -> x3, waiting for transfers between devices: 12.3 us -> 4.51 us  [per_device(): met = lax.ppermute(total, 'dp', [(i, i ^ stride) for i in range(groups)])]
    all_to_all x1 -> x0, starting transfers between devices: 5.87 us -> none  [per_device(): lax.all_to_all(pair, 'seq', 0, 0, tiled=True, axis_index_groups=same_core)]
    ppermute x7 -> x3, starting transfers between devices: 17.2 us -> 11.8 us  [per_device(): met = lax.ppermute(total, 'dp', [(i, i ^ stride) for i in range(groups)])]
    pallas_call x1 -> x3, Pallas kernels: 7.64 us -> 13 us  [the longest x1 11.5 us: run_forward(): pl.pallas_call(forward_kernel, out_shape=tuple((jax.ShapeDtypeStruct(size...]
    all_to_all x1, waiting for transfers between devices: 0.01 us -> 3.46 us  [per_device(): returned = lax.all_to_all(results, 'seq', 0, 0, tiled=True)]
    concatenate x1 -> x0, other arithmetic: 2.37 us -> none  [per_device(): jnp.concatenate([latents.reshape(seq, mine, model), cotangent.reshape(seq...]
    all_to_all x1, starting transfers between devices: 7.43 us -> 5.06 us  [per_device(): returned = lax.all_to_all(results, 'seq', 0, 0, tiled=True)]
  transfers between devices with their start and end apart: 11 -> 6, of which waited for: 6 -> 4; matrix products, arithmetic and copies ran while one was open for 1% -> 0% of each run, Pallas kernels for 11% -> 12%
where the time goes in v3:
time: 127 us; the launch traced here: 125 us
  Pallas kernels  29.2 us (23%)
  waiting for transfers between devices  28.5 us (22%)
  blocking collectives  25.9 us (20%)
  starting transfers between devices  24.8 us (20%)
  local copies, waits for them, and re-layouts  14 us (11%)
  other arithmetic  1.72 us (1%)
    all_to_all x1, blocking collectives, per_device(): lax.all_to_all(pair, 'seq', 0, 0, tiled=True, axis_index_groups=same_core)  25.9 us
    all_to_all x1, waiting for transfers between devices, per_device(): tokens = lax.all_to_all(outgoing, 'seq', 0, 0, tiled=True)  17.4 us
    pallas_call x1, Pallas kernels, run_backward(): pl.pallas_call(backward_kernel, out_shape=jax.ShapeDtypeStruct((frames, b...  15.1 us
    unnamed x28, local copies, waits for them, and re-layouts  14 us
    ppermute x3, starting transfers between devices, per_device(): met = lax.ppermute(total, 'dp', [(i, i ^ stride) for i in range(groups)])  11.8 us
    pallas_call x1, Pallas kernels, run_forward(): pl.pallas_call(forward_kernel, out_shape=tuple((jax.ShapeDtypeStruct(size...  11.5 us
    all_to_all x1, starting transfers between devices, per_device(): tokens = lax.all_to_all(outgoing, 'seq', 0, 0, tiled=True)  7.75 us
    all_to_all x1, starting transfers between devices, per_device(): returned = lax.all_to_all(results, 'seq', 0, 0, tiled=True)  5.06 us
  transfers between devices with their start and end apart: 6, of which 4 were waited for; matrix products, arithmetic and copies ran while one was open for 0% of the time, Pallas kernels for 12%

profile of v3, /device:TPU:2, one launch (start us, length us, event | category | flops | bytes accessed | tf_op | source)
XLA Modules:
  0.0 125.0 jit_solution(15095922386436114389)
XLA Ops:
  0.6 1.1 copy-done.9
  1.7 1.1 copy-done.10
  2.8 1.1 pack.1
  3.9 7.8 %all-to-all-start = ((bf16[32,16,1152]{2,1,0:T(8,128)(2,1)}), bf16[32,16,1152]{2,1,0:T(8,128)(2,1)S(1)}, u32[]{:S(2)}, u32[]{:S(2)}) async-start(bf16[32,16,1152]{2,1,0:T(8,128)(2,1)} %pack.1), calls=%async_computation | async-start | bytes 2359296 | tf_op jit(solution)/shard_map/all_to_all | solution.py:432
  11.7 0.1 pad_add_fusion.place_ref
  11.7 17.4 %all-to-all-done.tokens_ref = bf16[32,16,1152]{2,1,0:T(8,128)(2,1)S(1)} async-done(((bf16[32,16,1152]{2,1,0:T(8,128)(2,1)}), bf16[32,16,1152]{2,1,0:T(8,128)(2,1)S(1)}, u32[]{:S(2)}, u32[]{:S(2)}) %all-to-all-start) | async-done | bytes 1179680 | tf_op jit(solution)/shard_map/all_to_all | solution.py:432
  29.2 0.0 copy-done.11
  29.2 0.0 copy-start
  29.2 3.3 %copy-done = bf16[1152,3456]{1,0:T(8,128)(2,1)S(1)} copy-done((bf16[1152,3456]{1,0:T(8,128)(2,1)S(1)}, bf16[1152,3456]{1,0:T(8,128)(2,1)}, u32[]{:S(2)}) %copy-start) | copy-done | bytes 7962648
  32.4 11.5 %forward.1 = (bf16[256,3456]{1,0:T(8,128)(2,1)S(1)}, bf16[16,256,256]{2,1,0:T(8,128)(2,1)S(1)}, bf16[256,1152]{1,0:T(8,128)(2,1)S(1)}, bf16[256,1152]{1,0:T(8,12...) custom-call(s32[1,32]{1,0:T(1,128)S(1)} %copy-done.12, s32[1,4]{1,0:T(1,128)S(1)} %copy-done.13, ...), custom_call_target="tpu_custom_call" | custom-call | flops 2717908992 | bytes 12582912 | tf_op jit(solution)/shard_map/forward/pallas_call | solution.py:288
  44.0 0.0 copy-start.5
  44.0 0.0 copy-start.7
  44.0 0.2 collective-permute-start
  44.3 3.1 %collective-permute-done.right_ref = bf16[640,1152]{1,0:T(8,128)(2,1)S(1)} collective-permute-done((bf16[640,1152]{1,0:T(8,128)(2,1)S(1)}, bf16[640,1152]{1,0:T(8,128)(2,1)S(1)}, u32[]{:S(2)}, u32[]{:S(2)}) %collective-permute-start) | collective-permute-done | bytes 1474592 | tf_op jit(solution)/shard_map/ppermute | solution.py:437
  47.4 0.3 add.18
  47.8 25.9 %all_to_all.15 = bf16[16,40,1152]{2,1,0:T(8,128)(2,1)} all-to-all(bf16[16,40,1152]{2,1,0:T(8,128)(2,1)S(1)} %bitcast.10), channel_id=1, replica_groups={{0,2,4,6,8,10,12,14,16,18,20,22,24,26,28,30},{1,3,5,7,9,11,13,15,17,19,..., dimensions={0} | all-to-all | bytes 2949120 | tf_op jit(solution)/shard_map/all_to_all | solution.py:440
  73.7 1.6 %reduce_sum.12 = bf16[40,1152]{1,0:T(8,128)(2,1)S(1)} reduce(bf16[16,40,1152]{2,1,0:T(8,128)(2,1)} %all_to_all.15, bf16[]{:T(256)} %constant.21.clone.1), dimensions={0}, to_apply=%region_0.1 | reduce | flops 691200 | bytes 1566722 | tf_op jit(solution)/shard_map/reduce_sum | solution.py:444
  75.3 2.2 %collective-permute-start.1 = (bf16[40,1152]{1,0:T(8,128)(2,1)S(1)}, bf16[40,1152]{1,0:T(8,128)(2,1)S(1)}, u32[]{:S(2)}, u32[]{:S(2)}) collective-permute-start(bf16[40,1152]{1,0:T(8,128)(2,1)S(1)} %reduce_sum.12), channel_id=1, source_target_pairs={{0,32},{32,0},{64,96},{96,64},{128,160},{160,128},{192,224},{224,1... | collective-permute-start | bytes 276488 | tf_op jit(solution)/shard_map/ppermute | solution.py:447
  77.5 3.3 %copy-done.1 = bf16[1152,3456]{1,0:T(8,128)(2,1)S(1)} copy-done((bf16[1152,3456]{1,0:T(8,128)(2,1)S(1)}, bf16[1152,3456]{1,0:T(8,128)(2,1)}, u32[]{:S(2)}) %copy-start.1) | copy-done | bytes 7962648
  80.7 1.7 %copy-done.2 = bf16[1152,1152]{1,0:T(8,128)(2,1)S(1)} copy-done((bf16[1152,1152]{1,0:T(8,128)(2,1)S(1)}, bf16[1152,1152]{1,0:T(8,128)(2,1)}, u32[]{:S(2)}) %copy-start.2) | copy-done | bytes 2654232
  82.5 1.5 %copy-done.4 = bf16[256,3456]{1,0:T(8,128)(2,1)S(1)} copy-done((bf16[256,3456]{1,0:T(8,128)(2,1)S(1)}, bf16[256,3456]{1,0:T(8,128)(2,1)}, u32[]{:S(2)}) %copy-start.4) | copy-done | bytes 1769496
  84.0 1.1 copy-done.6
  85.0 1.1 copy-done.8
  86.1 15.1 %backward.1 = bf16[32,16,1152]{2,1,0:T(8,128)(2,1)} custom-call(s32[1,32]{1,0:T(1,128)S(1)} %copy-done.12, s32[1,4]{1,0:T(1,128)S(1)} %copy-done.13, s32[2]{0:T(128)S(1)} %pad_add_fusion.place_ref, bf16[32,16,1152]{2,1,0:T(8,128)(2,1)S(1)} %all-to-all-done.tokens_ref, f32[3,4,1152]{2,1,0:T(4,128)S(1)} %bitcast.14, bf16[256,1152]{1,0:T(8,128)(2,1)S(1)} %copy-done.8, ...), custom_call_target="tpu_custom_call" | custom-call | flops 4076863488 | bytes 16777216 | tf_op jit(solution)/shard_map/backward/pallas_call | solution.py:319
  101.2 5.1 %all-to-all-start.1 = ((bf16[32,16,1152]{2,1,0:T(8,128)(2,1)}), bf16[32,16,1152]{2,1,0:T(8,128)(2,1)S(1)}, u32[]{:S(2)}, u32[]{:S(2)}) async-start(bf16[32,16,1152]{2,1,0:T(8,128)(2,1)} %backward.1), calls=%async_computation.1 | async-start | bytes 2359296 | tf_op jit(solution)/shard_map/all_to_all | solution.py:452
  106.2 0.0 collective-permute-done.1
  106.3 3.4 %collective-permute-start.2 = (bf16[40,1152]{1,0:T(8,128)(2,1)S(1)}, bf16[40,1152]{1,0:T(8,128)(2,1)S(1)}, u32[]{:S(2)}, u32[]{:S(2)}) collective-permute-start(bf16[40,1152]{1,0:T(8,128)(2,1)S(1)} %add_convert_fusion.1), channel_id=1, source_target_pairs={{0,64},{32,96},{64,0},{96,32},{128,192},{160,224},{192,128},{224,1... | collective-permute-start | bytes 276488 | tf_op jit(solution)/shard_map/ppermute | solution.py:447
  109.6 4.5 %collective-permute-done.2 = bf16[40,1152]{1,0:T(8,128)(2,1)S(1)} collective-permute-done((bf16[40,1152]{1,0:T(8,128)(2,1)S(1)}, bf16[40,1152]{1,0:T(8,128)(2,1)S(1)}, u32[]{:S(2)}, u32[]{:S(2)}) %collective-permute-start.2) | collective-permute-done | bytes 92192 | tf_op jit(solution)/shard_map/ppermute | solution.py:447
  114.2 6.2 %collective-permute-start.3 = (bf16[40,1152]{1,0:T(8,128)(2,1)S(1)}, bf16[40,1152]{1,0:T(8,128)(2,1)S(1)}, u32[]{:S(2)}, u32[]{:S(2)}) collective-permute-start(bf16[40,1152]{1,0:T(8,128)(2,1)S(1)} %add_convert_fusion.left_ref), channel_id=1, source_target_pairs={{0,128},{32,160},{64,192},{96,224},{128,0},{160,32},{192,64},{224,... | collective-permute-start | bytes 276488 | tf_op jit(solution)/shard_map/ppermute | solution.py:447
  120.4 3.5 %all-to-all-done.1.returned_ref = bf16[32,16,1152]{2,1,0:T(8,128)(2,1)S(1)} async-done(((bf16[32,16,1152]{2,1,0:T(8,128)(2,1)}), bf16[32,16,1152]{2,1,0:T(8,128)(2,1)S(1)}, u32[]{:S(2)}, u32[]{:S(2)}) %all-to-all-start.1) | async-done | bytes 1179680 | tf_op jit(solution)/shard_map/all_to_all | solution.py:452
  123.9 0.0 collective-permute-done.3.right_ref
  123.9 1.2 finish.1
  (18 shorter events, 0.1 us)
Async XLA Ops:
  0.6 1.1 copy-start.9
  1.7 1.1 copy-start.10
  3.9 25.3 %copy-start.11 = (f32[1,4,3,1152]{3,1,2,0:T(4,128)S(1)}, f32[1,4,3,1152]{3,1,2,0:T(4,128)}, u32[]{:S(2)}) copy-start(f32[1,4,3,1152]{3,1,2,0:T(4,128)} %param.11) | copy-start | bytes 165892
  3.9 25.3 %copy-start.12 = (s32[1,32]{1,0:T(1,128)S(1)}, s32[1,32]{1,0:T(1,128)}, u32[]{:S(2)}) copy-start(s32[1,32]{1,0:T(1,128)} %clip_ref.3) | copy-start | bytes 388
  3.9 25.3 %copy-start.13 = (s32[1,4]{1,0:T(1,128)S(1)}, s32[1,4]{1,0:T(1,128)}, u32[]{:S(2)}) copy-start(s32[1,4]{1,0:T(1,128)} %count_ref.3) | copy-start | bytes 52
  3.9 25.3 %all-to-all-start = ((bf16[32,16,1152]{2,1,0:T(8,128)(2,1)}), bf16[32,16,1152]{2,1,0:T(8,128)(2,1)S(1)}, u32[]{:S(2)}, u32[]{:S(2)}) async-start(bf16[32,16,1152]{2,1,0:T(8,128)(2,1)} %pack.1), calls=%async_computation | async-start | bytes 2359296 | tf_op jit(solution)/shard_map/all_to_all | solution.py:432
  29.2 3.3 %copy-start = (bf16[1152,3456]{1,0:T(8,128)(2,1)S(1)}, bf16[1152,3456]{1,0:T(8,128)(2,1)}, u32[]{:S(2)}) copy-start(bf16[1152,3456]{1,0:T(8,128)(2,1)} %wqkv_hbm.3) | copy-start | bytes 23887876
  44.0 3.7 %copy-start.3 = (bf16[256,3456]{1,0:T(8,128)(2,1)}, bf16[256,3456]{1,0:T(8,128)(2,1)S(1)}, u32[]{:S(2)}) copy-start(bf16[256,3456]{1,0:T(8,128)(2,1)S(1)} %get-tuple-element.14.qkv_hbm) | copy-start | bytes 5308420
  44.0 3.7 %copy-start.5 = (bf16[256,1152]{1,0:T(8,128)(2,1)}, bf16[256,1152]{1,0:T(8,128)(2,1)S(1)}, u32[]{:S(2)}) copy-start(bf16[256,1152]{1,0:T(8,128)(2,1)S(1)} %get-tuple-element.13.att_hbm) | copy-start | bytes 1769476
  44.0 3.7 %copy-start.7 = (bf16[256,1152]{1,0:T(8,128)(2,1)}, bf16[256,1152]{1,0:T(8,128)(2,1)S(1)}, u32[]{:S(2)}) copy-start(bf16[256,1152]{1,0:T(8,128)(2,1)S(1)} %get-tuple-element.12.gdy_hbm) | copy-start | bytes 1769476
  44.0 3.4 %collective-permute-start = (bf16[640,1152]{1,0:T(8,128)(2,1)S(1)}, bf16[640,1152]{1,0:T(8,128)(2,1)S(1)}, u32[]{:S(2)}, u32[]{:S(2)}) collective-permute-start(bf16[640,1152]{1,0:T(8,128)(2,1)S(1)} %get-tuple-element.17), channel_id=1, source_target_pairs={{0,1},{1,0},{2,3},{3,2},{4,5},{5,4},{6,7},{7,6},{8,9},{9,8},{10,11... | collective-permute-start | bytes 4423688 | tf_op jit(solution)/shard_map/ppermute | solution.py:437
  75.3 31.0 %collective-permute-start.1 = (bf16[40,1152]{1,0:T(8,128)(2,1)S(1)}, bf16[40,1152]{1,0:T(8,128)(2,1)S(1)}, u32[]{:S(2)}, u32[]{:S(2)}) collective-permute-start(bf16[40,1152]{1,0:T(8,128)(2,1)S(1)} %reduce_sum.12), channel_id=1, source_target_pairs={{0,32},{32,0},{64,96},{96,64},{128,160},{160,128},{192,224},{224,1... | collective-permute-start | bytes 276488 | tf_op jit(solution)/shard_map/ppermute | solution.py:447
  77.5 3.3 %copy-start.1 = (bf16[1152,3456]{1,0:T(8,128)(2,1)S(1)}, bf16[1152,3456]{1,0:T(8,128)(2,1)}, u32[]{:S(2)}) copy-start(bf16[1152,3456]{1,0:T(8,128)(2,1)} %wqkv_hbm.3) | copy-start | bytes 23887876
  80.7 1.7 %copy-start.2 = (bf16[1152,1152]{1,0:T(8,128)(2,1)S(1)}, bf16[1152,1152]{1,0:T(8,128)(2,1)}, u32[]{:S(2)}) copy-start(bf16[1152,1152]{1,0:T(8,128)(2,1)} %wout_hbm.1) | copy-start | bytes 7962628
  82.5 1.5 %copy-start.4 = (bf16[256,3456]{1,0:T(8,128)(2,1)S(1)}, bf16[256,3456]{1,0:T(8,128)(2,1)}, u32[]{:S(2)}) copy-start(bf16[256,3456]{1,0:T(8,128)(2,1)} %copy-done.3) | copy-start | bytes 5308420
  83.9 1.1 copy-start.6
  85.0 1.1 copy-start.8
  101.2 22.7 %all-to-all-start.1 = ((bf16[32,16,1152]{2,1,0:T(8,128)(2,1)}), bf16[32,16,1152]{2,1,0:T(8,128)(2,1)S(1)}, u32[]{:S(2)}, u32[]{:S(2)}) async-start(bf16[32,16,1152]{2,1,0:T(8,128)(2,1)} %backward.1), calls=%async_computation.1 | async-start | bytes 2359296 | tf_op jit(solution)/shard_map/all_to_all | solution.py:452
  106.3 7.9 %collective-permute-start.2 = (bf16[40,1152]{1,0:T(8,128)(2,1)S(1)}, bf16[40,1152]{1,0:T(8,128)(2,1)S(1)}, u32[]{:S(2)}, u32[]{:S(2)}) collective-permute-start(bf16[40,1152]{1,0:T(8,128)(2,1)S(1)} %add_convert_fusion.1), channel_id=1, source_target_pairs={{0,64},{32,96},{64,0},{96,32},{128,192},{160,224},{192,128},{224,1... | collective-permute-start | bytes 276488 | tf_op jit(solution)/shard_map/ppermute | solution.py:447
  114.2 9.7 %collective-permute-start.3 = (bf16[40,1152]{1,0:T(8,128)(2,1)S(1)}, bf16[40,1152]{1,0:T(8,128)(2,1)S(1)}, u32[]{:S(2)}, u32[]{:S(2)}) collective-permute-start(bf16[40,1152]{1,0:T(8,128)(2,1)S(1)} %add_convert_fusion.left_ref), channel_id=1, source_target_pairs={{0,128},{32,160},{64,192},{96,224},{128,0},{160,32},{192,64},{224,... | collective-permute-start | bytes 276488 | tf_op jit(solution)/shard_map/ppermute | solution.py:447

commit v4 on v3

--- a/solution.py
+++ b/solution.py
@@ -70,14 +70,27 @@
     base = place_ref[0]
     core = place_ref[1]
 
-    loads = []
-    for step, start in enumerate(range(0, 3 * model, CHUNK)):
-        columns = slice(start, start + CHUNK)
-        load = pltpu.make_async_copy(
-            wqkv_hbm.at[:, columns], wqkv_ref.at[:, columns], load_sems.at[step]
-        )
-        load.start()
-        loads.append(load)
+    parts_n = model // CHUNK
+    columns = [
+        [slice(kind * model + part * CHUNK, kind * model + (part + 1) * CHUNK) for kind in range(3)]
+        for part in range(parts_n)
+    ]
+    loads = [
+        [
+            pltpu.make_async_copy(
+                wqkv_hbm.at[:, where], wqkv_ref.at[:, where], load_sems.at[part, kind]
+            )
+            for kind, where in enumerate(columns[part])
+        ]
+        for part in range(parts_n)
+    ]
+
+    def start_loads(part):
+        if part < parts_n:
+            for load in loads[part]:
+                load.start()
+
+    start_loads(0)
 
     def pair_step(step, carry):
         xmods, gdys = [], []
@@ -98,6 +111,7 @@
         return carry
 
     lax.fori_loop(0, frames // 2, pair_step, 0, unroll=4)
+    start_loads(1)
 
     stores = []
 
@@ -143,31 +157,35 @@
                 pieces, axis=0
             ).astype(jnp.bfloat16)
 
-    xmod = xmod_ref[...]
-    for step, start in enumerate(range(0, 3 * model, CHUNK)):
-        loads[step].wait()
-        qkv_ref[:, start : start + CHUNK] = dot(
-            xmod, wqkv_ref[:, start : start + CHUNK], NN
-        ).astype(jnp.bfloat16)
-    store_out(qkv_ref, qkv_hbm)
-
     def store_att(low, value):
         att_ref[:, low : low + LANES] = value.astype(jnp.bfloat16)
 
+    xmod = xmod_ref[...]
     parts = {}
-    for head in range(HEADS):
-        first, last, low, high = head_span(head, head_dim)
-        mask = head_mask(first, last, low, high)
-        query = qkv_ref[:, low:high] * mask
-        key = qkv_ref[:, model + low : model + high]
-        value = qkv_ref[:, 2 * model + low : 2 * model + high] * mask
-        expo = jnp.exp(dot(key, query, NT) * head_dim ** (-0.5)) * same_ref[...]
-        prob = (expo * (1.0 / jnp.sum(expo, axis=0, keepdims=True))).astype(jnp.bfloat16)
-        prob_ref[head] = prob
-        add_tiles(parts, low, dot(prob, value, TN))
-        flush_tiles(parts, last, store_att)
+    head = 0
+    for part in range(parts_n):
+        for load in loads[part]:
+            load.wait()
+        start_loads(part + 2)
+        for where in columns[part]:
+            qkv_ref[:, where] = dot(xmod, wqkv_ref[:, where], NN).astype(jnp.bfloat16)
+        if part == parts_n - 1:
+            store_out(qkv_ref, qkv_hbm)
+        first_head = head
+        while head < HEADS and (head + 1) * head_dim <= (part + 1) * CHUNK:
+            first, last, low, high = head_span(head, head_dim)
+            mask = head_mask(first, last, low, high)
+            query = qkv_ref[:, low:high] * mask
+            key = qkv_ref[:, model + low : model + high]
+            value = qkv_ref[:, 2 * model + low : 2 * model + high] * mask
+            expo = jnp.exp(dot(key, query, NT) * head_dim ** (-0.5)) * same_ref[...]
+            prob = (expo * (1.0 / jnp.sum(expo, axis=0, keepdims=True))).astype(jnp.bfloat16)
+            prob_ref[head] = prob
+            add_tiles(parts, low, dot(prob, value, TN))
+            flush_tiles(parts, last, store_att)
+            head += 1
+        store_out(prob_ref.at[first_head:head], prob_hbm.at[first_head:head])
     store_out(att_ref, att_hbm)
-    store_out(prob_ref, prob_hbm)
 
     for target_ref, side in ((send_ref, 1 - core), (keep_ref, core)):
         for start in range(0, model, CHUNK):
@@ -298,10 +316,10 @@
             pltpu.VMEM((rows, rows), jnp.float32),
             pltpu.VMEM((model + 16, rows), jnp.float32),
             pltpu.VMEM((2, chips * SHARE_ROWS, rows), low),
-            pltpu.SemaphoreType.DMA((3 * model // CHUNK,)),
-            pltpu.SemaphoreType.DMA((4,)),
+            pltpu.SemaphoreType.DMA((model // CHUNK, 3)),
+            pltpu.SemaphoreType.DMA((3 + model // CHUNK,)),
         ],
-        compiler_params=pltpu.CompilerParams(vmem_limit_bytes=32 * MIB),
+        compiler_params=pltpu.CompilerParams(vmem_limit_bytes=58 * MIB),
         cost_estimate=pl.CostEstimate(
             flops=2 * rows * model * 4 * model, bytes_accessed=12 * MIB, transcendentals=0
         ),
@@ -329,7 +347,7 @@
             pltpu.VMEM((rows, model), jnp.float32),
             pltpu.SemaphoreType.DMA((len(loaded),)),
         ],
-        compiler_params=pltpu.CompilerParams(vmem_limit_bytes=32 * MIB),
+        compiler_params=pltpu.CompilerParams(vmem_limit_bytes=58 * MIB),
         cost_estimate=pl.CostEstimate(
             flops=2 * rows * model * 6 * model, bytes_accessed=16 * MIB, transcendentals=0
         ),
@@ -337,28 +355,44 @@
     )(frame_clip, clip_patches, place, tokens, modulation, *loaded)
 
 
-def pack_kernel(latent_ref, cotangent_ref, out_ref):
+def pack_kernel(latent_hbm, cotangent_hbm, out_ref, latent_ref, cotangent_ref, sems):
     both = out_ref.shape[1]
     patches = both // 2
-    for step in range(out_ref.shape[0] // 2):
-        where = slice(step * both, (step + 1) * both)
-        latent = latent_ref[where, :].astype(jnp.float32)
-        cotangent = cotangent_ref[where, :].astype(jnp.float32)
-        for k in range(2):
-            half = slice(k * patches, (k + 1) * patches)
-            out_ref[2 * step + k] = jnp.concatenate([latent[half], cotangent[half]], axis=0).astype(
-                jnp.bfloat16
-            )
+    parts = sems.shape[1]
+    rows = latent_ref.shape[0] // parts
+    loads = []
+    for part in range(parts):
+        where = slice(part * rows, (part + 1) * rows)
+        for k, (source, target) in enumerate(
+            ((latent_hbm, latent_ref), (cotangent_hbm, cotangent_ref))
+        ):
+            load = pltpu.make_async_copy(source.at[where, :], target.at[where, :], sems.at[k, part])
+            load.start()
+            loads.append(load)
+    for part in range(parts):
+        loads[2 * part].wait()
+        loads[2 * part + 1].wait()
+        for start in range(part * rows, (part + 1) * rows, both):
+            where = slice(start, start + both)
+            latent = latent_ref[where, :].astype(jnp.float32)
+            cotangent = cotangent_ref[where, :].astype(jnp.float32)
+            for k in range(2):
+                half = slice(k * patches, (k + 1) * patches)
+                out_ref[start // patches + k] = jnp.concatenate(
+                    [latent[half], cotangent[half]], axis=0
+                ).astype(jnp.bfloat16)
 
 
 def run_pack(latents, cotangent, seq):
     rows, model = latents.shape
+    low = jnp.bfloat16
     return pl.pallas_call(
         pack_kernel,
-        out_shape=jax.ShapeDtypeStruct((seq, 2 * rows // seq, model), jnp.bfloat16),
-        in_specs=[vmem()] * 2,
+        out_shape=jax.ShapeDtypeStruct((seq, 2 * rows // seq, model), low),
+        in_specs=[hbm()] * 2,
         out_specs=vmem(),
-        compiler_params=pltpu.CompilerParams(vmem_limit_bytes=12 * MIB),
+        scratch_shapes=[pltpu.VMEM((rows, model), low)] * 2 + [pltpu.SemaphoreType.DMA((2, 4))],
+        compiler_params=pltpu.CompilerParams(vmem_limit_bytes=60 * MIB),
         name="pack",
     )(latents, cotangent)
 
@@ -381,6 +415,28 @@
         compiler_params=pltpu.CompilerParams(vmem_limit_bytes=12 * MIB),
         name="add",
     )(left, right)
+
+
+def sum_kernel(terms_ref, after_ref, out_ref):
+    del after_ref
+    step_rows = 8
+    for start in range(0, out_ref.shape[0], step_rows):
+        where = slice(start, start + step_rows)
+        total = terms_ref[0, where, :].astype(jnp.float32)
+        for term in range(1, terms_ref.shape[0]):
+            total = total + terms_ref[term, where, :].astype(jnp.float32)
+        out_ref[where, :] = total
+
+
+def run_sum(terms, after):
+    return pl.pallas_call(
+        sum_kernel,
+        out_shape=jax.ShapeDtypeStruct(terms.shape[1:], jnp.float32),
+        in_specs=[vmem(), pl.BlockSpec(memory_space=pl.ANY)],
+        out_specs=vmem(),
+        compiler_params=pltpu.CompilerParams(vmem_limit_bytes=12 * MIB),
+        name="sum",
+    )(terms, after)
 
 
 def finish_kernel(returned_ref, left_ref, right_ref, block_ref, latent_ref, grad_ref):
@@ -441,7 +497,7 @@
     results = run_backward(
         frame_clip, clip_patches, place, tokens, mod, gdy, out_weight, att, qkv, prob, qkv_weight
     )
-    total = jnp.sum(terms.astype(jnp.float32), axis=0).astype(jnp.bfloat16)
+    total = run_sum(terms, results).astype(jnp.bfloat16)
     stride = 1
     while True:
         met = lax.ppermute(total, "dp", [(i, i ^ stride) for i in range(groups)])

time: 127 us -> 104 us (0.82)
  blocking collectives: 25.9 us -> 0 us
  local copies, waits for them, and re-layouts: 14 us -> 2.39 us
  starting transfers between devices: 24.8 us -> 31.9 us
  waiting for transfers between devices: 28.5 us -> 33.2 us
  Pallas kernels: 29.2 us -> 33.3 us
    all_to_all x1 -> x0, blocking collectives: 25.9 us -> none  [per_device(): lax.all_to_all(pair, 'seq', 0, 0, tiled=True, axis_index_groups=same_core)]
    unnamed x28 -> x4, local copies, waits for them, and re-layouts: 14 us -> 2.39 us
    all_to_all x0 -> x1, starting transfers between devices: none -> 5.23 us  [per_device(): lax.all_to_all(pair, 'seq', 0, 0, tiled=True, axis_index_groups=same_core)]
    all_to_all x0 -> x1, waiting for transfers between devices: none -> 4.98 us  [per_device(): lax.all_to_all(pair, 'seq', 0, 0, tiled=True, axis_index_groups=same_core)]
    all_to_all x1, starting transfers between devices: 5.06 us -> 7.2 us  [per_device(): returned = lax.all_to_all(results, 'seq', 0, 0, tiled=True)]
    reduce_sum x1 -> x0, other arithmetic: 1.59 us -> none  [per_device(): total = jnp.sum(terms.astype(jnp.float32), axis=0).astype(jnp.bfloat16)]
    pallas_call x1, Pallas kernels: 1.13 us -> 2.45 us  [run_pack(): pl.pallas_call(pack_kernel, out_shape=jax.ShapeDtypeStruct((seq, 2 * rows...]
  transfers between devices with their start and end apart: 6 -> 7, of which waited for: 4 -> 5; matrix products, arithmetic and copies ran while one was open for 0% -> 1% of each run, Pallas kernels for 12% -> 16%
where the time goes in v4:
time: 104 us; the launch traced here: 102 us
  Pallas kernels  33.3 us (32%)
  waiting for transfers between devices  33.2 us (32%)
  starting transfers between devices  31.9 us (31%)
  local copies, waits for them, and re-layouts  2.39 us (2%)
    all_to_all x1, waiting for transfers between devices, per_device(): tokens = lax.all_to_all(outgoing, 'seq', 0, 0, tiled=True)  16.9 us
    pallas_call x1, Pallas kernels, run_backward(): pl.pallas_call(backward_kernel, out_shape=jax.ShapeDtypeStruct((frames, b...  16.1 us
    pallas_call x1, Pallas kernels, run_forward(): pl.pallas_call(forward_kernel, out_shape=tuple((jax.ShapeDtypeStruct(size...  12 us
    ppermute x3, starting transfers between devices, per_device(): met = lax.ppermute(total, 'dp', [(i, i ^ stride) for i in range(groups)])  11.6 us
    all_to_all x1, starting transfers between devices, per_device(): tokens = lax.all_to_all(outgoing, 'seq', 0, 0, tiled=True)  7.63 us
    all_to_all x1, starting transfers between devices, per_device(): returned = lax.all_to_all(results, 'seq', 0, 0, tiled=True)  7.2 us
    all_to_all x1, starting transfers between devices, per_device(): lax.all_to_all(pair, 'seq', 0, 0, tiled=True, axis_index_groups=same_core)  5.23 us
    all_to_all x1, waiting for transfers between devices, per_device(): lax.all_to_all(pair, 'seq', 0, 0, tiled=True, axis_index_groups=same_core)  4.98 us
  transfers between devices with their start and end apart: 7, of which 5 were waited for; matrix products, arithmetic and copies ran while one was open for 1% of the time, Pallas kernels for 16%

profile of v4, /device:TPU:2, one launch (start us, length us, event | category | flops | bytes accessed | tf_op | source)
XLA Modules:
  0.0 102.2 jit_solution(11633443952586452761)
XLA Ops:
  0.6 2.5 %pack.1 = bf16[32,16,1152]{2,1,0:T(8,128)(2,1)} custom-call(bf16[256,1152]{1,0:T(8,128)(2,1)} %bitcast.10, bf16[256,1152]{1,0:T(8,128)(2,1)} %bitcast.11), custom_call_target="tpu_custom_call" | custom-call | tf_op jit(solution)/shard_map/pack/pallas_call | solution.py:389
  3.1 7.6 %all-to-all-start = ((bf16[32,16,1152]{2,1,0:T(8,128)(2,1)}), bf16[32,16,1152]{2,1,0:T(8,128)(2,1)S(1)}, u32[]{:S(2)}, u32[]{:S(2)}) async-start(bf16[32,16,1152]{2,1,0:T(8,128)(2,1)} %pack.1), calls=%async_computation | async-start | bytes 2359296 | tf_op jit(solution)/shard_map/all_to_all | solution.py:488
  10.7 0.6 pad_add_fusion.place_ref
  11.3 16.9 %all-to-all-done.tokens_ref = bf16[32,16,1152]{2,1,0:T(8,128)(2,1)S(1)} async-done(((bf16[32,16,1152]{2,1,0:T(8,128)(2,1)}), bf16[32,16,1152]{2,1,0:T(8,128)(2,1)S(1)}, u32[]{:S(2)}, u32[]{:S(2)}) %all-to-all-start) | async-done | bytes 1179680 | tf_op jit(solution)/shard_map/all_to_all | solution.py:488
  28.2 0.0 copy-start.1
  28.2 1.0 copy-done.1
  29.3 12.0 %forward.1 = (bf16[256,3456]{1,0:T(8,128)(2,1)}, bf16[16,256,256]{2,1,0:T(8,128)(2,1)}, bf16[256,1152]{1,0:T(8,128)(2,1)}, bf16[256,1152]{1,0:T(8,128)(2,1)}, bf...) custom-call(s32[1,32]{1,0:T(1,128)} %clip_ref.3, s32[1,4]{1,0:T(1,128)} %count_ref.3, s32[2]{0:T(128)} %pad_add_fusion.place_ref, ...), custom_call_target="tpu_custom_call" | custom-call | flops 2717908992 | bytes 12582912 | tf_op jit(solution)/shard_map/forward/pallas_call | solution.py:306
  41.2 0.2 collective-permute-start
  41.5 3.3 %collective-permute-done.right_ref = bf16[640,1152]{1,0:T(8,128)(2,1)S(1)} collective-permute-done((bf16[640,1152]{1,0:T(8,128)(2,1)}, bf16[640,1152]{1,0:T(8,128)(2,1)S(1)}, u32[]{:S(2)}, u32[]{:S(2)}) %collective-permute-start) | collective-permute-done | bytes 1474592 | tf_op jit(solution)/shard_map/ppermute | solution.py:493
  44.8 0.0 copy-start
  44.8 1.4 %copy-done = bf16[640,1152]{1,0:T(8,128)(2,1)S(1)} copy-done((bf16[640,1152]{1,0:T(8,128)(2,1)S(1)}, bf16[640,1152]{1,0:T(8,128)(2,1)}, u32[]{:S(2)}) %copy-start) | copy-done | bytes 1474584
  46.2 1.4 %add.18 = bf16[640,1152]{1,0:T(8,128)(2,1)} custom-call(bf16[640,1152]{1,0:T(8,128)(2,1)S(1)} %copy-done, bf16[640,1152]{1,0:T(8,128)(2,1)S(1)} %collective-permute-done.right_ref), custom_call_target="tpu_custom_call" | custom-call | tf_op jit(solution)/shard_map/add/pallas_call | solution.py:410
  47.6 5.2 %all-to-all-start.2 = ((bf16[16,40,1152]{2,1,0:T(8,128)(2,1)}), bf16[16,40,1152]{2,1,0:T(8,128)(2,1)S(1)}, u32[]{:S(2)}, u32[]{:S(2)}) async-start(bf16[16,40,1152]{2,1,0:T(8,128)(2,1)} %bitcast.7), calls=%async_computation.2 | async-start | bytes 2949120 | tf_op jit(solution)/shard_map/all_to_all | solution.py:496
  52.8 16.1 %backward.1.after_ref = bf16[32,16,1152]{2,1,0:T(8,128)(2,1)} custom-call(s32[1,32]{1,0:T(1,128)} %clip_ref.3, s32[1,4]{1,0:T(1,128)} %count_ref.3, s32[2]{0:T(128)} %pad_add_fusion.place_ref, bf16[32,16,1152]{2,1,0:T(8,128)(2,1)} %copy-done.1, f32[3,4,1152]{2,1,0:T(4,128)} %bitcast.13, bf16[256,1152]{1,0:T(8,128)(2,1)} %get-tuple-element.12.gdy_hbm, ...), custom_call_target="tpu_custom_call" | custom-call | flops 4076863488 | bytes 16777216 | tf_op jit(solution)/shard_map/backward/pallas_call | solution.py:337
  69.0 5.0 %all-to-all-done.2.terms_ref = bf16[16,40,1152]{2,1,0:T(8,128)(2,1)S(1)} async-done(((bf16[16,40,1152]{2,1,0:T(8,128)(2,1)}), bf16[16,40,1152]{2,1,0:T(8,128)(2,1)S(1)}, u32[]{:S(2)}, u32[]{:S(2)}) %all-to-all-start.2) | async-done | bytes 1474592 | tf_op jit(solution)/shard_map/all_to_all | solution.py:496
  74.0 0.2 sum.1
  74.2 2.0 %collective-permute-start.1 = (bf16[40,1152]{1,0:T(8,128)(2,1)S(1)}, bf16[40,1152]{1,0:T(8,128)(2,1)S(1)}, u32[]{:S(2)}, u32[]{:S(2)}) collective-permute-start(bf16[40,1152]{1,0:T(8,128)(2,1)S(1)} %convert_element_type.21), channel_id=1, source_target_pairs={{0,32},{32,0},{64,96},{96,64},{128,160},{160,128},{192,224},{224,1... | collective-permute-start | bytes 276488 | tf_op jit(solution)/shard_map/ppermute | solution.py:503
  76.2 7.2 %all-to-all-start.1 = ((bf16[32,16,1152]{2,1,0:T(8,128)(2,1)}), bf16[32,16,1152]{2,1,0:T(8,128)(2,1)S(1)}, u32[]{:S(2)}, u32[]{:S(2)}) async-start(bf16[32,16,1152]{2,1,0:T(8,128)(2,1)} %backward.1.after_ref), calls=%async_computation.1 | async-start | bytes 2359296 | tf_op jit(solution)/shard_map/all_to_all | solution.py:508
  83.4 0.0 collective-permute-done.1
  83.4 3.4 %collective-permute-start.2 = (bf16[40,1152]{1,0:T(8,128)(2,1)S(1)}, bf16[40,1152]{1,0:T(8,128)(2,1)S(1)}, u32[]{:S(2)}, u32[]{:S(2)}) collective-permute-start(bf16[40,1152]{1,0:T(8,128)(2,1)S(1)} %add_convert_fusion.1), channel_id=1, source_target_pairs={{0,64},{32,96},{64,0},{96,32},{128,192},{160,224},{192,128},{224,1... | collective-permute-start | bytes 276488 | tf_op jit(solution)/shard_map/ppermute | solution.py:503
  86.8 4.5 %collective-permute-done.2 = bf16[40,1152]{1,0:T(8,128)(2,1)S(1)} collective-permute-done((bf16[40,1152]{1,0:T(8,128)(2,1)S(1)}, bf16[40,1152]{1,0:T(8,128)(2,1)S(1)}, u32[]{:S(2)}, u32[]{:S(2)}) %collective-permute-start.2) | collective-permute-done | bytes 92192 | tf_op jit(solution)/shard_map/ppermute | solution.py:503
  91.3 6.2 %collective-permute-start.3 = (bf16[40,1152]{1,0:T(8,128)(2,1)S(1)}, bf16[40,1152]{1,0:T(8,128)(2,1)S(1)}, u32[]{:S(2)}, u32[]{:S(2)}) collective-permute-start(bf16[40,1152]{1,0:T(8,128)(2,1)S(1)} %add_convert_fusion.left_ref), channel_id=1, source_target_pairs={{0,128},{32,160},{64,192},{96,224},{128,0},{160,32},{192,64},{224,... | collective-permute-start | bytes 276488 | tf_op jit(solution)/shard_map/ppermute | solution.py:503
  97.6 3.5 %all-to-all-done.1.returned_ref = bf16[32,16,1152]{2,1,0:T(8,128)(2,1)S(1)} async-done(((bf16[32,16,1152]{2,1,0:T(8,128)(2,1)}), bf16[32,16,1152]{2,1,0:T(8,128)(2,1)S(1)}, u32[]{:S(2)}, u32[]{:S(2)}) %all-to-all-start.1) | async-done | bytes 1179680 | tf_op jit(solution)/shard_map/all_to_all | solution.py:508
  101.0 0.0 collective-permute-done.3.right_ref
  101.0 1.2 %finish.1 = (bf16[256,1152]{1,0:T(8,128)(2,1)}, bf16[256,1152]{1,0:T(8,128)(2,1)}, f32[36,1152]{1,0:T(8,128)}) custom-call(bf16[32,16,1152]{2,1,0:T(8,128)(2,1)S(1)} %all-to-all-done.1.returned_ref, bf16[40,1152]{1,0:T(8,128)(2,1)S(1)} %add_convert_fusion.left_ref, bf16[40,1152]{1,0:T(8,128)(2,1)S(1)} %collective-permute-done.3.right_ref), custom_call_target="tpu_custom_call" | custom-call | bytes 4194304 | tf_op jit(solution)/shard_map/finish/pallas_call | solution.py:462
  (3 shorter events, 0.1 us)
Async XLA Ops:
  3.1 25.2 %all-to-all-start = ((bf16[32,16,1152]{2,1,0:T(8,128)(2,1)}), bf16[32,16,1152]{2,1,0:T(8,128)(2,1)S(1)}, u32[]{:S(2)}, u32[]{:S(2)}) async-start(bf16[32,16,1152]{2,1,0:T(8,128)(2,1)} %pack.1), calls=%async_computation | async-start | bytes 2359296 | tf_op jit(solution)/shard_map/all_to_all | solution.py:488
  28.2 1.0 copy-start.1
  41.2 3.6 %collective-permute-start = (bf16[640,1152]{1,0:T(8,128)(2,1)}, bf16[640,1152]{1,0:T(8,128)(2,1)S(1)}, u32[]{:S(2)}, u32[]{:S(2)}) collective-permute-start(bf16[640,1152]{1,0:T(8,128)(2,1)} %get-tuple-element.17), channel_id=1, source_target_pairs={{0,1},{1,0},{2,3},{3,2},{4,5},{5,4},{6,7},{7,6},{8,9},{9,8},{10,11... | collective-permute-start | bytes 4423688 | tf_op jit(solution)/shard_map/ppermute | solution.py:493
  44.8 1.4 %copy-start = (bf16[640,1152]{1,0:T(8,128)(2,1)S(1)}, bf16[640,1152]{1,0:T(8,128)(2,1)}, u32[]{:S(2)}) copy-start(bf16[640,1152]{1,0:T(8,128)(2,1)} %get-tuple-element.16.left_ref) | copy-start | bytes 4423684
  47.6 26.4 %all-to-all-start.2 = ((bf16[16,40,1152]{2,1,0:T(8,128)(2,1)}), bf16[16,40,1152]{2,1,0:T(8,128)(2,1)S(1)}, u32[]{:S(2)}, u32[]{:S(2)}) async-start(bf16[16,40,1152]{2,1,0:T(8,128)(2,1)} %bitcast.7), calls=%async_computation.2 | async-start | bytes 2949120 | tf_op jit(solution)/shard_map/all_to_all | solution.py:496
  74.2 9.2 %collective-permute-start.1 = (bf16[40,1152]{1,0:T(8,128)(2,1)S(1)}, bf16[40,1152]{1,0:T(8,128)(2,1)S(1)}, u32[]{:S(2)}, u32[]{:S(2)}) collective-permute-start(bf16[40,1152]{1,0:T(8,128)(2,1)S(1)} %convert_element_type.21), channel_id=1, source_target_pairs={{0,32},{32,0},{64,96},{96,64},{128,160},{160,128},{192,224},{224,1... | collective-permute-start | bytes 276488 | tf_op jit(solution)/shard_map/ppermute | solution.py:503
  76.2 24.8 %all-to-all-start.1 = ((bf16[32,16,1152]{2,1,0:T(8,128)(2,1)}), bf16[32,16,1152]{2,1,0:T(8,128)(2,1)S(1)}, u32[]{:S(2)}, u32[]{:S(2)}) async-start(bf16[32,16,1152]{2,1,0:T(8,128)(2,1)} %backward.1.after_ref), calls=%async_computation.1 | async-start | bytes 2359296 | tf_op jit(solution)/shard_map/all_to_all | solution.py:508
  83.4 7.9 %collective-permute-start.2 = (bf16[40,1152]{1,0:T(8,128)(2,1)S(1)}, bf16[40,1152]{1,0:T(8,128)(2,1)S(1)}, u32[]{:S(2)}, u32[]{:S(2)}) collective-permute-start(bf16[40,1152]{1,0:T(8,128)(2,1)S(1)} %add_convert_fusion.1), channel_id=1, source_target_pairs={{0,64},{32,96},{64,0},{96,32},{128,192},{160,224},{192,128},{224,1... | collective-permute-start | bytes 276488 | tf_op jit(solution)/shard_map/ppermute | solution.py:503
  91.3 9.7 %collective-permute-start.3 = (bf16[40,1152]{1,0:T(8,128)(2,1)S(1)}, bf16[40,1152]{1,0:T(8,128)(2,1)S(1)}, u32[]{:S(2)}, u32[]{:S(2)}) collective-permute-start(bf16[40,1152]{1,0:T(8,128)(2,1)S(1)} %add_convert_fusion.left_ref), channel_id=1, source_target_pairs={{0,128},{32,160},{64,192},{96,224},{128,0},{160,32},{192,64},{224,... | collective-permute-start | bytes 276488 | tf_op jit(solution)/shard_map/ppermute | solution.py:503

commit v5 on v4

--- a/solution.py
+++ b/solution.py
@@ -58,10 +58,9 @@
 
 
 def forward_kernel(
-    clip_ref, count_ref, place_ref, tokens_ref, mod_ref, wqkv_hbm,
-    qkv_hbm, prob_hbm, att_hbm, gdy_hbm, keep_ref, send_ref,
-    wqkv_ref, qkv_ref, prob_ref, att_ref, gdy_ref, xmod_ref, same_ref, turned_ref, share_ref,
-    load_sems, store_sems,
+    clip_ref, count_ref, place_ref, tokens_ref, mod_ref, wqkv_ref,
+    qkv_ref, prob_ref, att_ref, gdy_ref, keep_ref, send_ref,
+    xmod_ref, same_ref, turned_ref, share_ref,
 ):
     frames, both, model = tokens_ref.shape
     patches = both // 2
@@ -69,28 +68,6 @@
     head_dim = model // HEADS
     base = place_ref[0]
     core = place_ref[1]
-
-    parts_n = model // CHUNK
-    columns = [
-        [slice(kind * model + part * CHUNK, kind * model + (part + 1) * CHUNK) for kind in range(3)]
-        for part in range(parts_n)
-    ]
-    loads = [
-        [
-            pltpu.make_async_copy(
-                wqkv_hbm.at[:, where], wqkv_ref.at[:, where], load_sems.at[part, kind]
-            )
-            for kind, where in enumerate(columns[part])
-        ]
-        for part in range(parts_n)
-    ]
-
-    def start_loads(part):
-        if part < parts_n:
-            for load in loads[part]:
-                load.start()
-
-    start_loads(0)
 
     def pair_step(step, carry):
         xmods, gdys = [], []
@@ -111,16 +88,6 @@
         return carry
 
     lax.fori_loop(0, frames // 2, pair_step, 0, unroll=4)
-    start_loads(1)
-
-    stores = []
-
-    def store_out(source_ref, target_hbm):
-        store = pltpu.make_async_copy(source_ref, target_hbm, store_sems.at[len(stores)])
-        store.start()
-        stores.append(store)
-
-    store_out(gdy_ref, gdy_hbm)
 
     starts = []
     for clip in range(1, mod_ref.shape[1]):
@@ -163,15 +130,11 @@
     xmod = xmod_ref[...]
     parts = {}
     head = 0
-    for part in range(parts_n):
-        for load in loads[part]:
-            load.wait()
-        start_loads(part + 2)
-        for where in columns[part]:
+    for part in range(model // CHUNK):
+        for kind in range(3):
+            start = kind * model + part * CHUNK
+            where = slice(start, start + CHUNK)
             qkv_ref[:, where] = dot(xmod, wqkv_ref[:, where], NN).astype(jnp.bfloat16)
-        if part == parts_n - 1:
-            store_out(qkv_ref, qkv_hbm)
-        first_head = head
         while head < HEADS and (head + 1) * head_dim <= (part + 1) * CHUNK:
             first, last, low, high = head_span(head, head_dim)
             mask = head_mask(first, last, low, high)
@@ -184,53 +147,35 @@
             add_tiles(parts, low, dot(prob, value, TN))
             flush_tiles(parts, last, store_att)
             head += 1
-        store_out(prob_ref.at[first_head:head], prob_hbm.at[first_head:head])
-    store_out(att_ref, att_hbm)
 
     for target_ref, side in ((send_ref, 1 - core), (keep_ref, core)):
         for start in range(0, model, CHUNK):
             target_ref[:, start : start + CHUNK] = dot(
                 share_ref[side], att_ref[:, start : start + CHUNK], NN
             ).astype(jnp.bfloat16)
-    for store in stores:
-        store.wait()
 
 
 def backward_kernel(
     clip_ref, count_ref, place_ref, tokens_ref, mod_ref,
-    gdy_hbm, wout_hbm, att_hbm, qkv_hbm, prob_hbm, wqkv_hbm,
+    gdy_ref, wout_ref, att_ref, qkv_ref, prob_ref, wqkv_ref, after_ref,
     out_ref,
-    gdy_ref, wout_ref, att_ref, qkv_ref, prob_ref, wqkv_ref,
-    datt_ref, dqkv_ref, proj_ref, dxmod_ref, sems,
+    datt_ref, dqkv_ref, proj_ref, dxmod_ref,
 ):
+    del after_ref
     frames, both, model = tokens_ref.shape
     patches = both // 2
     head_dim = model // HEADS
     att_scale = head_dim ** (-0.5)
     base = place_ref[0]
 
-    loads = []
-    for source_hbm, target_ref in (
-        (gdy_hbm, gdy_ref), (wout_hbm, wout_ref), (att_hbm, att_ref),
-        (qkv_hbm, qkv_ref), (prob_hbm, prob_ref), (wqkv_hbm, wqkv_ref),
-    ):
-        load = pltpu.make_async_copy(source_hbm, target_ref, sems.at[len(loads)])
-        load.start()
-        loads.append(load)
-
-    loads[0].wait()
-    loads[1].wait()
     gdy = gdy_ref[...]
     for start in range(0, model, CHUNK):
         datt_ref[:, start : start + CHUNK] = dot(
             gdy, wout_ref[start : start + CHUNK, :], NT
         ).astype(jnp.bfloat16)
-    loads[2].wait()
     att = att_ref[...]
     for start in range(0, model, CHUNK):
         proj_ref[:, start : start + CHUNK] = dot(att, wout_ref[:, start : start + CHUNK], NN)
-    loads[3].wait()
-    loads[4].wait()
 
     def store_at(offset, factor):
         def store(low, value):
@@ -257,7 +202,6 @@
         flush_tiles(parts_k, last, store_at(model, att_scale))
         flush_tiles(parts_v, last, store_at(2 * model, 1.0))
 
-    loads[5].wait()
     dqkv = dqkv_ref[...]
     for start in range(0, model, CHUNK):
         dxmod_ref[:, start : start + CHUNK] = dot(dqkv, wqkv_ref[start : start + CHUNK, :], NT)
@@ -298,61 +242,87 @@
     return pl.BlockSpec(memory_space=pltpu.HBM)
 
 
+def in_hbm(array):
+    return pltpu.with_memory_space_constraint(array, pltpu.HBM)
+
+
+def in_vmem(array):
+    return pltpu.with_memory_space_constraint(array, pltpu.VMEM)
+
+
 def run_forward(frame_clip, clip_patches, place, tokens, modulation, qkv_weight, chips):
     frames, both, model = tokens.shape
     rows = frames * both // 2
     low = jnp.bfloat16
     sizes = ((rows, 3 * model), (HEADS, rows, rows), (rows, model), (rows, model))
+    sizes += ((chips * SHARE_ROWS, model),) * 2
     return pl.pallas_call(
         forward_kernel,
-        out_shape=tuple(jax.ShapeDtypeStruct(size, low) for size in sizes)
-        + (jax.ShapeDtypeStruct((chips * SHARE_ROWS, model), low),) * 2,
-        in_specs=[smem()] * 3 + [vmem()] * 2 + [hbm()],
-        out_specs=(hbm(),) * 4 + (vmem(),) * 2,
-        scratch_shapes=[pltpu.VMEM((model, 3 * model), low)]
-        + [pltpu.VMEM(size, low) for size in sizes]
-        + [
+        out_shape=tuple(pltpu.VMEM(size, low) for size in sizes),
+        in_specs=[smem()] * 3 + [vmem()] * 3,
+        out_specs=(vmem(),) * 6,
+        scratch_shapes=[
             pltpu.VMEM((rows, model), low),
             pltpu.VMEM((rows, rows), jnp.float32),
             pltpu.VMEM((model + 16, rows), jnp.float32),
             pltpu.VMEM((2, chips * SHARE_ROWS, rows), low),
-            pltpu.SemaphoreType.DMA((model // CHUNK, 3)),
-            pltpu.SemaphoreType.DMA((3 + model // CHUNK,)),
         ],
-        compiler_params=pltpu.CompilerParams(vmem_limit_bytes=58 * MIB),
+        compiler_params=pltpu.CompilerParams(vmem_limit_bytes=20 * MIB),
         cost_estimate=pl.CostEstimate(
             flops=2 * rows * model * 4 * model, bytes_accessed=12 * MIB, transcendentals=0
         ),
         name="forward",
-    )(frame_clip, clip_patches, place, tokens, modulation, qkv_weight)
-
-
-def run_backward(
-    frame_clip, clip_patches, place, tokens, modulation, gdy, out_weight, att, qkv, prob, qkv_weight
-):
+    )(frame_clip, clip_patches, place, in_vmem(tokens), modulation, in_vmem(qkv_weight))
+
+
+def run_backward(frame_clip, clip_patches, place, tokens, modulation, saved, after):
     frames, both, model = tokens.shape
     rows = frames * both // 2
     low = jnp.bfloat16
-    loaded = (gdy, out_weight, att, qkv, prob, qkv_weight)
     return pl.pallas_call(
         backward_kernel,
-        out_shape=jax.ShapeDtypeStruct((frames, both, model), low),
-        in_specs=[smem()] * 3 + [vmem()] * 2 + [hbm()] * len(loaded),
+        out_shape=pltpu.VMEM((frames, both, model), low),
+        in_specs=[smem()] * 3 + [vmem()] * (2 + len(saved)) + [pl.BlockSpec(memory_space=pl.ANY)],
         out_specs=vmem(),
-        scratch_shapes=[pltpu.VMEM(array.shape, low) for array in loaded]
-        + [
+        scratch_shapes=[
             pltpu.VMEM((rows, model), low),
             pltpu.VMEM((rows, 3 * model), low),
             pltpu.VMEM((rows, model), jnp.float32),
             pltpu.VMEM((rows, model), jnp.float32),
-            pltpu.SemaphoreType.DMA((len(loaded),)),
         ],
-        compiler_params=pltpu.CompilerParams(vmem_limit_bytes=58 * MIB),
+        compiler_params=pltpu.CompilerParams(vmem_limit_bytes=20 * MIB),
         cost_estimate=pl.CostEstimate(
             flops=2 * rows * model * 6 * model, bytes_accessed=16 * MIB, transcendentals=0
         ),
         name="backward",
-    )(frame_clip, clip_patches, place, tokens, modulation, *loaded)
+    )(
+        frame_clip, clip_patches, place, in_vmem(tokens), modulation, *map(in_vmem, saved), after
+    )
+
+
+def load_kernel(*refs):
+    count = len(refs) // 2
+    sems = refs[-1]
+    loads = [
+        pltpu.make_async_copy(refs[k], refs[count + k], sems.at[k]) for k in range(count)
+    ]
+    for load in loads:
+        load.start()
+    for load in loads:
+        load.wait()
+
+
+def run_load(*weights):
+    return pl.pallas_call(
+        load_kernel,
+        out_shape=tuple(pltpu.VMEM(weight.shape, weight.dtype) for weight in weights),
+        in_specs=[hbm()] * len(weights),
+        out_specs=(vmem(),) * len(weights),
+        scratch_shapes=[pltpu.SemaphoreType.DMA((len(weights),))],
+        compiler_params=pltpu.CompilerParams(vmem_limit_bytes=20 * MIB),
+        cost_estimate=pl.CostEstimate(flops=0, bytes_accessed=22 * MIB, transcendentals=0),
+        name="load",
+    )(*map(in_hbm, weights))
 
 
 def pack_kernel(latent_hbm, cotangent_hbm, out_ref, latent_ref, cotangent_ref, sems):
@@ -388,13 +358,13 @@
     low = jnp.bfloat16
     return pl.pallas_call(
         pack_kernel,
-        out_shape=jax.ShapeDtypeStruct((seq, 2 * rows // seq, model), low),
+        out_shape=pltpu.VMEM((seq, 2 * rows // seq, model), low),
         in_specs=[hbm()] * 2,
         out_specs=vmem(),
         scratch_shapes=[pltpu.VMEM((rows, model), low)] * 2 + [pltpu.SemaphoreType.DMA((2, 4))],
-        compiler_params=pltpu.CompilerParams(vmem_limit_bytes=60 * MIB),
+        compiler_params=pltpu.CompilerParams(vmem_limit_bytes=12 * MIB),
         name="pack",
-    )(latents, cotangent)
+    )(in_hbm(latents), in_hbm(cotangent))
 
 
 def add_kernel(left_ref, right_ref, out_ref):
@@ -409,12 +379,12 @@
 def run_add(left, right):
     return pl.pallas_call(
         add_kernel,
-        out_shape=jax.ShapeDtypeStruct(left.shape, left.dtype),
+        out_shape=pltpu.VMEM(left.shape, left.dtype),
         in_specs=[vmem()] * 2,
         out_specs=vmem(),
         compiler_params=pltpu.CompilerParams(vmem_limit_bytes=12 * MIB),
         name="add",
-    )(left, right)
+    )(in_vmem(left), in_vmem(right))
 
 
 def sum_kernel(terms_ref, after_ref, out_ref):
@@ -487,6 +457,7 @@
     outgoing = run_pack(latents.reshape(patches, model), cotangent.reshape(patches, model), seq)
     tokens = lax.all_to_all(outgoing, "seq", 0, 0, tiled=True)
     mod = modulation[0].transpose(1, 0, 2)
+    qkv_weight, out_weight = run_load(qkv_weight, out_weight)
     qkv, prob, att, gdy, keep, send = run_forward(
         frame_clip, clip_patches, place, tokens, mod, qkv_weight, chips
     )
@@ -494,9 +465,8 @@
     pair = run_add(keep, other).reshape(chips, SHARE_ROWS, model)
     same_core = [[2 * chip + core for chip in range(chips)] for core in range(2)]
     terms = lax.all_to_all(pair, "seq", 0, 0, tiled=True, axis_index_groups=same_core)
-    results = run_backward(
-        frame_clip, clip_patches, place, tokens, mod, gdy, out_weight, att, qkv, prob, qkv_weight
-    )
+    saved = (gdy, out_weight, att, qkv, prob, qkv_weight)
+    results = run_backward(frame_clip, clip_patches, place, tokens, mod, saved, pair)
     total = run_sum(terms, results).astype(jnp.bfloat16)
     stride = 1
     while True:

time: 104 us -> 103 us (level)
  local copies, waits for them, and re-layouts: 2.39 us -> 17.9 us
  waiting for transfers between devices: 33.2 us -> 19.6 us
  Pallas kernels: 33.3 us -> 30.4 us
    unnamed x4 -> x28, local copies, waits for them, and re-layouts: 2.39 us -> 17.9 us
    all_to_all x1, waiting for transfers between devices: 16.9 us -> 8.65 us  [per_device(): tokens = lax.all_to_all(outgoing, 'seq', 0, 0, tiled=True)]
    all_to_all x1, waiting for transfers between devices: 4.98 us -> 0.01 us  [per_device(): lax.all_to_all(pair, 'seq', 0, 0, tiled=True, axis_index_groups=same_core)]
    pallas_call x4 -> x5, Pallas kernels: 32 us -> 29 us  [the longest x1 12.9 us: run_backward(): pl.pallas_call(backward_kernel, out_shape=pltpu.VMEM((frames, both, model...]
  transfers between devices with their start and end apart: 7 -> 7, of which waited for: 5 -> 4; matrix products, arithmetic and copies ran while one was open for 1% -> 0% of each run, Pallas kernels for 16% -> 17%
where the time goes in v5:
time: 103 us; the launch traced here: 101 us
  starting transfers between devices  32 us (31%)
  Pallas kernels  30.4 us (30%)
  waiting for transfers between devices  19.6 us (19%)
  local copies, waits for them, and re-layouts  17.9 us (17%)
    unnamed x28, local copies, waits for them, and re-layouts  17.9 us
    pallas_call x1, Pallas kernels, run_backward(): pl.pallas_call(backward_kernel, out_shape=pltpu.VMEM((frames, both, model...  12.9 us
    ppermute x3, starting transfers between devices, per_device(): met = lax.ppermute(total, 'dp', [(i, i ^ stride) for i in range(groups)])  11.6 us
    all_to_all x1, waiting for transfers between devices, per_device(): tokens = lax.all_to_all(outgoing, 'seq', 0, 0, tiled=True)  8.65 us
    pallas_call x1, Pallas kernels, run_forward(): pl.pallas_call(forward_kernel, out_shape=tuple((pltpu.VMEM(size, low) for...  8.08 us
    all_to_all x1, starting transfers between devices, per_device(): tokens = lax.all_to_all(outgoing, 'seq', 0, 0, tiled=True)  7.63 us
    all_to_all x1, starting transfers between devices, per_device(): returned = lax.all_to_all(results, 'seq', 0, 0, tiled=True)  7.43 us
    all_to_all x1, starting transfers between devices, per_device(): lax.all_to_all(pair, 'seq', 0, 0, tiled=True, axis_index_groups=same_core)  5.23 us
  transfers between devices with their start and end apart: 7, of which 4 were waited for; matrix products, arithmetic and copies ran while one was open for 0% of the time, Pallas kernels for 17%

profile of v5, /device:TPU:2, one launch (start us, length us, event | category | flops | bytes accessed | tf_op | source)
XLA Modules:
  0.0 100.8 jit_solution(11091374385292703098)
XLA Ops:
  0.6 2.4 %pack.1 = bf16[32,16,1152]{2,1,0:T(8,128)(2,1)} custom-call(bf16[256,1152]{1,0:T(8,128)(2,1)} %bitcast.12, bf16[256,1152]{1,0:T(8,128)(2,1)} %bitcast.13), custom_call_target="tpu_custom_call" | custom-call | tf_op jit(solution)/shard_map/pack/pallas_call | solution.py:359
  3.1 7.6 %all-to-all-start = ((bf16[32,16,1152]{2,1,0:T(8,128)(2,1)}), bf16[32,16,1152]{2,1,0:T(8,128)(2,1)S(1)}, u32[]{:S(2)}, u32[]{:S(2)}) async-start(bf16[32,16,1152]{2,1,0:T(8,128)(2,1)} %pack.1), calls=%async_computation | async-start | bytes 2359296 | tf_op jit(solution)/shard_map/all_to_all | solution.py:458
  10.7 0.0 copy-start.11
  10.7 0.0 copy-start.12
  10.8 0.0 copy-start.13
  10.8 4.1 %load.1 = (bf16[1152,3456]{1,0:T(8,128)(2,1)S(1)}, bf16[1152,1152]{1,0:T(8,128)(2,1)S(1)}) custom-call(bf16[1152,3456]{1,0:T(8,128)(2,1)} %refs_0_.1, bf16[1152,1152]{1,0:T(8,128)(2,1)} %refs_1_.1), custom_call_target="tpu_custom_call" | custom-call | bytes 23068672 | tf_op jit(solution)/shard_map/load/pallas_call | solution.py:316
  14.8 3.1 %copy-done = bf16[1152,3456]{1,0:T(8,128)(2,1)} copy-done((bf16[1152,3456]{1,0:T(8,128)(2,1)}, bf16[1152,3456]{1,0:T(8,128)(2,1)S(1)}, u32[]{:S(2)}) %copy-start) | copy-done | bytes 7962648
  17.9 1.6 %copy-done.3 = bf16[1152,1152]{1,0:T(8,128)(2,1)} copy-done((bf16[1152,1152]{1,0:T(8,128)(2,1)}, bf16[1152,1152]{1,0:T(8,128)(2,1)S(1)}, u32[]{:S(2)}) %copy-start.3) | copy-done | bytes 2654232
  19.5 0.1 pad_add_fusion.place_ref
  19.6 8.6 %all-to-all-done.tokens_ref = bf16[32,16,1152]{2,1,0:T(8,128)(2,1)S(1)} async-done(((bf16[32,16,1152]{2,1,0:T(8,128)(2,1)}), bf16[32,16,1152]{2,1,0:T(8,128)(2,1)S(1)}, u32[]{:S(2)}, u32[]{:S(2)}) %all-to-all-start) | async-done | bytes 1179680 | tf_op jit(solution)/shard_map/all_to_all | solution.py:458
  28.3 3.3 %copy-done.1 = bf16[1152,3456]{1,0:T(8,128)(2,1)S(1)} copy-done((bf16[1152,3456]{1,0:T(8,128)(2,1)S(1)}, bf16[1152,3456]{1,0:T(8,128)(2,1)}, u32[]{:S(2)}) %copy-start.1) | copy-done | bytes 7962648
  31.5 8.1 %forward.1 = (bf16[256,3456]{1,0:T(8,128)(2,1)S(1)}, bf16[16,256,256]{2,1,0:T(8,128)(2,1)S(1)}, bf16[256,1152]{1,0:T(8,128)(2,1)S(1)}, bf16[256,1152]{1,0:T(8,12...) custom-call(s32[1,32]{1,0:T(1,128)S(1)} %copy-done.12, s32[1,4]{1,0:T(1,128)S(1)} %copy-done.13, ...), custom_call_target="tpu_custom_call" | custom-call | flops 2717908992 | bytes 12582912 | tf_op jit(solution)/shard_map/forward/pallas_call | solution.py:259
  39.6 0.0 copy-start.9
  39.6 0.8 copy-done.9
  40.4 0.1 collective-permute-start
  40.6 3.1 %collective-permute-done.right_ref = bf16[640,1152]{1,0:T(8,128)(2,1)S(1)} collective-permute-done((bf16[640,1152]{1,0:T(8,128)(2,1)S(1)}, bf16[640,1152]{1,0:T(8,128)(2,1)S(1)}, u32[]{:S(2)}, u32[]{:S(2)}) %collective-permute-start) | collective-permute-done | bytes 1474592 | tf_op jit(solution)/shard_map/ppermute | solution.py:464
  43.7 1.5 %add.18 = bf16[640,1152]{1,0:T(8,128)(2,1)} custom-call(bf16[640,1152]{1,0:T(8,128)(2,1)S(1)} %get-tuple-element.20.left_ref, bf16[640,1152]{1,0:T(8,128)(2,1)S(1)} %collective-permute-done.right_ref), custom_call_target="tpu_custom_call" | custom-call | tf_op jit(solution)/shard_map/add/pallas_call | solution.py:380
  45.2 5.2 %all-to-all-start.2 = ((bf16[16,40,1152]{2,1,0:T(8,128)(2,1)}), bf16[16,40,1152]{2,1,0:T(8,128)(2,1)S(1)}, u32[]{:S(2)}, u32[]{:S(2)}) async-start(bf16[16,40,1152]{2,1,0:T(8,128)(2,1)} %bitcast.7.after_ref), calls=%async_computation.2 | async-start | bytes 2949120 | tf_op jit(solution)/shard_map/all_to_all | solution.py:467
  50.4 3.3 %copy-done.2 = bf16[1152,3456]{1,0:T(8,128)(2,1)S(1)} copy-done((bf16[1152,3456]{1,0:T(8,128)(2,1)S(1)}, bf16[1152,3456]{1,0:T(8,128)(2,1)}, u32[]{:S(2)}) %copy-start.2) | copy-done | bytes 7962648
  53.7 1.7 %copy-done.4 = bf16[1152,1152]{1,0:T(8,128)(2,1)S(1)} copy-done((bf16[1152,1152]{1,0:T(8,128)(2,1)S(1)}, bf16[1152,1152]{1,0:T(8,128)(2,1)}, u32[]{:S(2)}) %copy-start.4) | copy-done | bytes 2654232
  55.4 1.6 %copy-done.6 = bf16[16,256,256]{2,1,0:T(8,128)(2,1)S(1)} copy-done((bf16[16,256,256]{2,1,0:T(8,128)(2,1)S(1)}, bf16[16,256,256]{2,1,0:T(8,128)(2,1)}, u32[]{:S(2)}) %copy-start.6) | copy-done | bytes 2097176
  57.0 1.5 %copy-done.8 = bf16[256,3456]{1,0:T(8,128)(2,1)S(1)} copy-done((bf16[256,3456]{1,0:T(8,128)(2,1)S(1)}, bf16[256,3456]{1,0:T(8,128)(2,1)}, u32[]{:S(2)}) %copy-start.8) | copy-done | bytes 1769496
  58.5 1.1 %copy-done.10 = bf16[256,1152]{1,0:T(8,128)(2,1)S(1)} copy-done((bf16[256,1152]{1,0:T(8,128)(2,1)S(1)}, bf16[256,1152]{1,0:T(8,128)(2,1)}, u32[]{:S(2)}) %copy-start.10) | copy-done | bytes 589848
  59.6 12.9 %backward.1.after_ref = bf16[32,16,1152]{2,1,0:T(8,128)(2,1)} custom-call(s32[1,32]{1,0:T(1,128)S(1)} %copy-done.12, s32[1,4]{1,0:T(1,128)S(1)} %copy-done.13, s32[2]{0:T(128)S(1)} %pad_add_fusion.place_ref, bf16[32,16,1152]{2,1,0:T(8,128)(2,1)S(1)} %all-to-all-done.tokens_ref, f32[3,4,1152]{2,1,0:T(4,128)S(1)} %bitcast.11, ...), custom_call_target="tpu_custom_call" | custom-call | flops 4076863488 | bytes 16777216 | tf_op jit(solution)/shard_map/backward/pallas_call | solution.py:282
  72.5 0.2 sum.1
  72.7 2.0 %collective-permute-start.1 = (bf16[40,1152]{1,0:T(8,128)(2,1)S(1)}, bf16[40,1152]{1,0:T(8,128)(2,1)S(1)}, u32[]{:S(2)}, u32[]{:S(2)}) collective-permute-start(bf16[40,1152]{1,0:T(8,128)(2,1)S(1)} %convert_element_type.21), channel_id=1, source_target_pairs={{0,32},{32,0},{64,96},{96,64},{128,160},{160,128},{192,224},{224,1... | collective-permute-start | bytes 276488 | tf_op jit(solution)/shard_map/ppermute | solution.py:473
  74.7 7.4 %all-to-all-start.1 = ((bf16[32,16,1152]{2,1,0:T(8,128)(2,1)}), bf16[32,16,1152]{2,1,0:T(8,128)(2,1)S(1)}, u32[]{:S(2)}, u32[]{:S(2)}) async-start(bf16[32,16,1152]{2,1,0:T(8,128)(2,1)} %backward.1.after_ref), calls=%async_computation.1 | async-start | bytes 2359296 | tf_op jit(solution)/shard_map/all_to_all | solution.py:478
  82.2 3.4 %collective-permute-start.2 = (bf16[40,1152]{1,0:T(8,128)(2,1)S(1)}, bf16[40,1152]{1,0:T(8,128)(2,1)S(1)}, u32[]{:S(2)}, u32[]{:S(2)}) collective-permute-start(bf16[40,1152]{1,0:T(8,128)(2,1)S(1)} %add_convert_fusion.1), channel_id=1, source_target_pairs={{0,64},{32,96},{64,0},{96,32},{128,192},{160,224},{192,128},{224,1... | collective-permute-start | bytes 276488 | tf_op jit(solution)/shard_map/ppermute | solution.py:473
  85.5 4.5 %collective-permute-done.2 = bf16[40,1152]{1,0:T(8,128)(2,1)S(1)} collective-permute-done((bf16[40,1152]{1,0:T(8,128)(2,1)S(1)}, bf16[40,1152]{1,0:T(8,128)(2,1)S(1)}, u32[]{:S(2)}, u32[]{:S(2)}) %collective-permute-start.2) | collective-permute-done | bytes 92192 | tf_op jit(solution)/shard_map/ppermute | solution.py:473
  90.1 6.2 %collective-permute-start.3 = (bf16[40,1152]{1,0:T(8,128)(2,1)S(1)}, bf16[40,1152]{1,0:T(8,128)(2,1)S(1)}, u32[]{:S(2)}, u32[]{:S(2)}) collective-permute-start(bf16[40,1152]{1,0:T(8,128)(2,1)S(1)} %add_convert_fusion.left_ref), channel_id=1, source_target_pairs={{0,128},{32,160},{64,192},{96,224},{128,0},{160,32},{192,64},{224,... | collective-permute-start | bytes 276488 | tf_op jit(solution)/shard_map/ppermute | solution.py:473
  96.3 3.4 %all-to-all-done.1.returned_ref = bf16[32,16,1152]{2,1,0:T(8,128)(2,1)S(1)} async-done(((bf16[32,16,1152]{2,1,0:T(8,128)(2,1)}), bf16[32,16,1152]{2,1,0:T(8,128)(2,1)S(1)}, u32[]{:S(2)}, u32[]{:S(2)}) %all-to-all-start.1) | async-done | bytes 1179680 | tf_op jit(solution)/shard_map/all_to_all | solution.py:478
  99.7 1.2 %finish.1 = (bf16[256,1152]{1,0:T(8,128)(2,1)}, bf16[256,1152]{1,0:T(8,128)(2,1)}, f32[36,1152]{1,0:T(8,128)}) custom-call(bf16[32,16,1152]{2,1,0:T(8,128)(2,1)S(1)} %all-to-all-done.1.returned_ref, bf16[40,1152]{1,0:T(8,128)(2,1)S(1)} %add_convert_fusion.left_ref, bf16[40,1152]{1,0:T(8,128)(2,1)S(1)} %collective-permute-done.3.right_ref), custom_call_target="tpu_custom_call" | custom-call | bytes 4194304 | tf_op jit(solution)/shard_map/finish/pallas_call | solution.py:432
  (21 shorter events, 0.1 us)
Async XLA Ops:
  3.1 25.2 %all-to-all-start = ((bf16[32,16,1152]{2,1,0:T(8,128)(2,1)}), bf16[32,16,1152]{2,1,0:T(8,128)(2,1)S(1)}, u32[]{:S(2)}, u32[]{:S(2)}) async-start(bf16[32,16,1152]{2,1,0:T(8,128)(2,1)} %pack.1), calls=%async_computation | async-start | bytes 2359296 | tf_op jit(solution)/shard_map/all_to_all | solution.py:458
  10.7 17.5 %copy-start.11 = (f32[1,4,3,1152]{3,1,2,0:T(4,128)S(1)}, f32[1,4,3,1152]{3,1,2,0:T(4,128)}, u32[]{:S(2)}) copy-start(f32[1,4,3,1152]{3,1,2,0:T(4,128)} %param.11) | copy-start | bytes 165892
  10.7 17.5 %copy-start.12 = (s32[1,32]{1,0:T(1,128)S(1)}, s32[1,32]{1,0:T(1,128)}, u32[]{:S(2)}) copy-start(s32[1,32]{1,0:T(1,128)} %clip_ref.3) | copy-start | bytes 388
  10.8 17.5 %copy-start.13 = (s32[1,4]{1,0:T(1,128)S(1)}, s32[1,4]{1,0:T(1,128)}, u32[]{:S(2)}) copy-start(s32[1,4]{1,0:T(1,128)} %count_ref.3) | copy-start | bytes 52
  14.8 3.1 %copy-start = (bf16[1152,3456]{1,0:T(8,128)(2,1)}, bf16[1152,3456]{1,0:T(8,128)(2,1)S(1)}, u32[]{:S(2)}) copy-start(bf16[1152,3456]{1,0:T(8,128)(2,1)S(1)} %get-tuple-element.14.wqkv_ref) | copy-start | bytes 23887876
  17.9 1.6 %copy-start.3 = (bf16[1152,1152]{1,0:T(8,128)(2,1)}, bf16[1152,1152]{1,0:T(8,128)(2,1)S(1)}, u32[]{:S(2)}) copy-start(bf16[1152,1152]{1,0:T(8,128)(2,1)S(1)} %get-tuple-element.16.wout_ref) | copy-start | bytes 7962628
  28.2 3.3 %copy-start.1 = (bf16[1152,3456]{1,0:T(8,128)(2,1)S(1)}, bf16[1152,3456]{1,0:T(8,128)(2,1)}, u32[]{:S(2)}) copy-start(bf16[1152,3456]{1,0:T(8,128)(2,1)} %copy-done) | copy-start | bytes 23887876
  39.6 0.8 copy-start.9
  40.4 4.8 %copy-start.5 = (bf16[16,256,256]{2,1,0:T(8,128)(2,1)}, bf16[16,256,256]{2,1,0:T(8,128)(2,1)S(1)}, u32[]{:S(2)}) copy-start(bf16[16,256,256]{2,1,0:T(8,128)(2,1)S(1)} %get-tuple-element.19.prob_ref) | copy-start | bytes 6291460
  40.4 4.8 %copy-start.7 = (bf16[256,3456]{1,0:T(8,128)(2,1)}, bf16[256,3456]{1,0:T(8,128)(2,1)S(1)}, u32[]{:S(2)}) copy-start(bf16[256,3456]{1,0:T(8,128)(2,1)S(1)} %get-tuple-element.18.qkv_ref) | copy-start | bytes 5308420
  40.4 3.3 %collective-permute-start = (bf16[640,1152]{1,0:T(8,128)(2,1)S(1)}, bf16[640,1152]{1,0:T(8,128)(2,1)S(1)}, u32[]{:S(2)}, u32[]{:S(2)}) collective-permute-start(bf16[640,1152]{1,0:T(8,128)(2,1)S(1)} %get-tuple-element.21), channel_id=1, source_target_pairs={{0,1},{1,0},{2,3},{3,2},{4,5},{5,4},{6,7},{7,6},{8,9},{9,8},{10,11... | collective-permute-start | bytes 4423688 | tf_op jit(solution)/shard_map/ppermute | solution.py:464
  45.2 27.3 %all-to-all-start.2 = ((bf16[16,40,1152]{2,1,0:T(8,128)(2,1)}), bf16[16,40,1152]{2,1,0:T(8,128)(2,1)S(1)}, u32[]{:S(2)}, u32[]{:S(2)}) async-start(bf16[16,40,1152]{2,1,0:T(8,128)(2,1)} %bitcast.7.after_ref), calls=%async_computation.2 | async-start | bytes 2949120 | tf_op jit(solution)/shard_map/all_to_all | solution.py:467
  50.4 3.3 %copy-start.2 = (bf16[1152,3456]{1,0:T(8,128)(2,1)S(1)}, bf16[1152,3456]{1,0:T(8,128)(2,1)}, u32[]{:S(2)}) copy-start(bf16[1152,3456]{1,0:T(8,128)(2,1)} %copy-done) | copy-start | bytes 23887876
  53.7 1.7 %copy-start.4 = (bf16[1152,1152]{1,0:T(8,128)(2,1)S(1)}, bf16[1152,1152]{1,0:T(8,128)(2,1)}, u32[]{:S(2)}) copy-start(bf16[1152,1152]{1,0:T(8,128)(2,1)} %copy-done.3) | copy-start | bytes 7962628
  55.4 1.6 %copy-start.6 = (bf16[16,256,256]{2,1,0:T(8,128)(2,1)S(1)}, bf16[16,256,256]{2,1,0:T(8,128)(2,1)}, u32[]{:S(2)}) copy-start(bf16[16,256,256]{2,1,0:T(8,128)(2,1)} %copy-done.5) | copy-start | bytes 6291460
  57.0 1.5 %copy-start.8 = (bf16[256,3456]{1,0:T(8,128)(2,1)S(1)}, bf16[256,3456]{1,0:T(8,128)(2,1)}, u32[]{:S(2)}) copy-start(bf16[256,3456]{1,0:T(8,128)(2,1)} %copy-done.7) | copy-start | bytes 5308420
  58.5 1.1 %copy-start.10 = (bf16[256,1152]{1,0:T(8,128)(2,1)S(1)}, bf16[256,1152]{1,0:T(8,128)(2,1)}, u32[]{:S(2)}) copy-start(bf16[256,1152]{1,0:T(8,128)(2,1)} %copy-done.9) | copy-start | bytes 1769476
  72.7 9.4 %collective-permute-start.1 = (bf16[40,1152]{1,0:T(8,128)(2,1)S(1)}, bf16[40,1152]{1,0:T(8,128)(2,1)S(1)}, u32[]{:S(2)}, u32[]{:S(2)}) collective-permute-start(bf16[40,1152]{1,0:T(8,128)(2,1)S(1)} %convert_element_type.21), channel_id=1, source_target_pairs={{0,32},{32,0},{64,96},{96,64},{128,160},{160,128},{192,224},{224,1... | collective-permute-start | bytes 276488 | tf_op jit(solution)/shard_map/ppermute | solution.py:473
  74.7 25.0 %all-to-all-start.1 = ((bf16[32,16,1152]{2,1,0:T(8,128)(2,1)}), bf16[32,16,1152]{2,1,0:T(8,128)(2,1)S(1)}, u32[]{:S(2)}, u32[]{:S(2)}) async-start(bf16[32,16,1152]{2,1,0:T(8,128)(2,1)} %backward.1.after_ref), calls=%async_computation.1 | async-start | bytes 2359296 | tf_op jit(solution)/shard_map/all_to_all | solution.py:478
  82.2 7.9 %collective-permute-start.2 = (bf16[40,1152]{1,0:T(8,128)(2,1)S(1)}, bf16[40,1152]{1,0:T(8,128)(2,1)S(1)}, u32[]{:S(2)}, u32[]{:S(2)}) collective-permute-start(bf16[40,1152]{1,0:T(8,128)(2,1)S(1)} %add_convert_fusion.1), channel_id=1, source_target_pairs={{0,64},{32,96},{64,0},{96,32},{128,192},{160,224},{192,128},{224,1... | collective-permute-start | bytes 276488 | tf_op jit(solution)/shard_map/ppermute | solution.py:473
  90.1 9.6 %collective-permute-start.3 = (bf16[40,1152]{1,0:T(8,128)(2,1)S(1)}, bf16[40,1152]{1,0:T(8,128)(2,1)S(1)}, u32[]{:S(2)}, u32[]{:S(2)}) collective-permute-start(bf16[40,1152]{1,0:T(8,128)(2,1)S(1)} %add_convert_fusion.left_ref), channel_id=1, source_target_pairs={{0,128},{32,160},{64,192},{96,224},{128,0},{160,32},{192,64},{224,... | collective-permute-start | bytes 276488 | tf_op jit(solution)/shard_map/ppermute | solution.py:473

commit v6 on v4

--- a/solution.py
+++ b/solution.py
@@ -59,9 +59,8 @@
 
 def forward_kernel(
     clip_ref, count_ref, place_ref, tokens_ref, mod_ref, wqkv_hbm,
-    qkv_hbm, prob_hbm, att_hbm, gdy_hbm, keep_ref, send_ref,
-    wqkv_ref, qkv_ref, prob_ref, att_ref, gdy_ref, xmod_ref, same_ref, turned_ref, share_ref,
-    load_sems, store_sems,
+    qkv_ref, prob_ref, att_ref, gdy_ref, share_ref, send_ref,
+    wqkv_ref, xmod_ref, same_ref, turned_ref, load_sems,
 ):
     frames, both, model = tokens_ref.shape
     patches = both // 2
@@ -110,17 +109,8 @@
         gdy_ref[where, :] = jnp.concatenate(gdys, axis=0).astype(jnp.bfloat16)
         return carry
 
-    lax.fori_loop(0, frames // 2, pair_step, 0, unroll=4)
+    lax.fori_loop(0, frames // 2, pair_step, 0, unroll=16)
     start_loads(1)
-
-    stores = []
-
-    def store_out(source_ref, target_hbm):
-        store = pltpu.make_async_copy(source_ref, target_hbm, store_sems.at[len(stores)])
-        store.start()
-        stores.append(store)
-
-    store_out(gdy_ref, gdy_hbm)
 
     starts = []
     for clip in range(1, mod_ref.shape[1]):
@@ -140,7 +130,8 @@
     key_f = key_of(lax.broadcasted_iota(jnp.int32, (1, rows), 1))
     same_ref[...] = (key_e == key_f).astype(jnp.float32)
 
-    chips, held = share_ref.shape[1] // SHARE_ROWS, SHARE_ROWS
+    held = SHARE_ROWS
+    chips = share_ref.shape[1] // held
     share = model // (2 * chips)
     for start in range(0, model, LANES):
         turned_ref[start : start + LANES, :] = gdy_ref[:, start : start + LANES].astype(
@@ -160,6 +151,11 @@
     def store_att(low, value):
         att_ref[:, low : low + LANES] = value.astype(jnp.bfloat16)
 
+    def score_of(head):
+        first, last, low, high = head_span(head, head_dim)
+        query = qkv_ref[:, low:high] * head_mask(first, last, low, high)
+        return dot(qkv_ref[:, model + low : model + high], query, NT)
+
     xmod = xmod_ref[...]
     parts = {}
     head = 0
@@ -169,40 +165,72 @@
         start_loads(part + 2)
         for where in columns[part]:
             qkv_ref[:, where] = dot(xmod, wqkv_ref[:, where], NN).astype(jnp.bfloat16)
-        if part == parts_n - 1:
-            store_out(qkv_ref, qkv_hbm)
-        first_head = head
+        scores = None
         while head < HEADS and (head + 1) * head_dim <= (part + 1) * CHUNK:
             first, last, low, high = head_span(head, head_dim)
             mask = head_mask(first, last, low, high)
-            query = qkv_ref[:, low:high] * mask
-            key = qkv_ref[:, model + low : model + high]
+            if scores is None:
+                scores = score_of(head)
+            last_head = (head + 2) * head_dim > (part + 1) * CHUNK
+            later = None if last_head else score_of(head + 1)
             value = qkv_ref[:, 2 * model + low : 2 * model + high] * mask
-            expo = jnp.exp(dot(key, query, NT) * head_dim ** (-0.5)) * same_ref[...]
+            expo = jnp.exp(scores * head_dim ** (-0.5)) * same_ref[...]
             prob = (expo * (1.0 / jnp.sum(expo, axis=0, keepdims=True))).astype(jnp.bfloat16)
             prob_ref[head] = prob
             add_tiles(parts, low, dot(prob, value, TN))
             flush_tiles(parts, last, store_att)
+            scores = later
             head += 1
-        store_out(prob_ref.at[first_head:head], prob_hbm.at[first_head:head])
-    store_out(att_ref, att_hbm)
-
-    for target_ref, side in ((send_ref, 1 - core), (keep_ref, core)):
-        for start in range(0, model, CHUNK):
-            target_ref[:, start : start + CHUNK] = dot(
-                share_ref[side], att_ref[:, start : start + CHUNK], NN
-            ).astype(jnp.bfloat16)
+
+    for start in range(0, model, CHUNK):
+        send_ref[:, start : start + CHUNK] = dot(
+            share_ref[1 - core], att_ref[:, start : start + CHUNK], NN
+        ).astype(jnp.bfloat16)
+
+
+def keep_kernel(place_ref, share_ref, qkv_ref, prob_ref, att_ref, gdy_ref, *refs):
+    keep_ref, targets, sems = refs[0], refs[1:-1], refs[-1]
+    stores = []
+    for source, target in zip((qkv_ref, prob_ref, att_ref, gdy_ref), targets):
+        store = pltpu.make_async_copy(source, target, sems.at[len(stores)])
+        store.start()
+        stores.append(store)
+    core = place_ref[1]
+    model = keep_ref.shape[1]
+    for start in range(0, model, CHUNK):
+        keep_ref[:, start : start + CHUNK] = dot(
+            share_ref[core], att_ref[:, start : start + CHUNK], NN
+        ).astype(jnp.bfloat16)
     for store in stores:
         store.wait()
 
 
+def run_keep(place, share, saved):
+    rows, model = share.shape[1], saved[2].shape[1]
+    low = jnp.bfloat16
+    return pl.pallas_call(
+        keep_kernel,
+        out_shape=(pltpu.VMEM((rows, model), low),)
+        + tuple(pltpu.HBM(array.shape, low) for array in saved),
+        in_specs=[smem()] + [vmem()] * (1 + len(saved)),
+        out_specs=(vmem(),) + (hbm(),) * len(saved),
+        scratch_shapes=[pltpu.SemaphoreType.DMA((len(saved),))],
+        compiler_params=pltpu.CompilerParams(vmem_limit_bytes=12 * MIB),
+        cost_estimate=pl.CostEstimate(
+            flops=2 * rows * model * share.shape[2], bytes_accessed=6 * MIB, transcendentals=0
+        ),
+        name="keep",
+    )(place, in_vmem(share), *map(in_vmem, saved))
+
+
 def backward_kernel(
     clip_ref, count_ref, place_ref, tokens_ref, mod_ref,
-    gdy_hbm, wout_hbm, att_hbm, qkv_hbm, prob_hbm, wqkv_hbm,
-    out_ref,
+    gdy_hbm, wout_hbm, att_hbm, qkv_hbm, prob_hbm, wqkv_hbm, after_ref,
+    out_hbm,
     gdy_ref, wout_ref, att_ref, qkv_ref, prob_ref, wqkv_ref,
-    datt_ref, dqkv_ref, proj_ref, dxmod_ref, sems,
+    datt_ref, dqkv_ref, proj_ref, dxmod_ref, out_ref, sems, store_sems,
 ):
+    del after_ref
     frames, both, model = tokens_ref.shape
     patches = both // 2
     head_dim = model // HEADS
@@ -283,7 +311,17 @@
         ).astype(jnp.bfloat16)
         return carry
 
-    lax.fori_loop(0, frames, frame_step, 0, unroll=8)
+    stores = []
+    part_n = store_sems.shape[0]
+    step = frames // part_n
+    for part in range(part_n):
+        lax.fori_loop(part * step, (part + 1) * step, frame_step, 0, unroll=step)
+        where = slice(part * step, (part + 1) * step)
+        store = pltpu.make_async_copy(out_ref.at[where], out_hbm.at[where], store_sems.at[part])
+        store.start()
+        stores.append(store)
+    for store in stores:
+        store.wait()
 
 
 def smem():
@@ -296,66 +334,75 @@
 
 def hbm():
     return pl.BlockSpec(memory_space=pltpu.HBM)
+
+
+def in_hbm(array):
+    return pltpu.with_memory_space_constraint(array, pltpu.HBM)
+
+
+def in_vmem(array):
+    return pltpu.with_memory_space_constraint(array, pltpu.VMEM)
 
 
 def run_forward(frame_clip, clip_patches, place, tokens, modulation, qkv_weight, chips):
     frames, both, model = tokens.shape
     rows = frames * both // 2
     low = jnp.bfloat16
+    groups = model // CHUNK
     sizes = ((rows, 3 * model), (HEADS, rows, rows), (rows, model), (rows, model))
+    sizes += ((2, chips * SHARE_ROWS, rows), (chips * SHARE_ROWS, model))
     return pl.pallas_call(
         forward_kernel,
-        out_shape=tuple(jax.ShapeDtypeStruct(size, low) for size in sizes)
-        + (jax.ShapeDtypeStruct((chips * SHARE_ROWS, model), low),) * 2,
+        out_shape=tuple(pltpu.VMEM(size, low) for size in sizes),
         in_specs=[smem()] * 3 + [vmem()] * 2 + [hbm()],
-        out_specs=(hbm(),) * 4 + (vmem(),) * 2,
-        scratch_shapes=[pltpu.VMEM((model, 3 * model), low)]
-        + [pltpu.VMEM(size, low) for size in sizes]
-        + [
+        out_specs=(vmem(),) * 6,
+        scratch_shapes=[
+            pltpu.VMEM((model, 3 * model), low),
             pltpu.VMEM((rows, model), low),
             pltpu.VMEM((rows, rows), jnp.float32),
             pltpu.VMEM((model + 16, rows), jnp.float32),
-            pltpu.VMEM((2, chips * SHARE_ROWS, rows), low),
-            pltpu.SemaphoreType.DMA((model // CHUNK, 3)),
-            pltpu.SemaphoreType.DMA((3 + model // CHUNK,)),
+            pltpu.SemaphoreType.DMA((groups, 3)),
         ],
-        compiler_params=pltpu.CompilerParams(vmem_limit_bytes=58 * MIB),
+        compiler_params=pltpu.CompilerParams(vmem_limit_bytes=36 * MIB),
         cost_estimate=pl.CostEstimate(
             flops=2 * rows * model * 4 * model, bytes_accessed=12 * MIB, transcendentals=0
         ),
         name="forward",
-    )(frame_clip, clip_patches, place, tokens, modulation, qkv_weight)
-
-
-def run_backward(
-    frame_clip, clip_patches, place, tokens, modulation, gdy, out_weight, att, qkv, prob, qkv_weight
-):
+    )(frame_clip, clip_patches, place, in_vmem(tokens), modulation, in_hbm(qkv_weight))
+
+
+def run_backward(frame_clip, clip_patches, place, tokens, modulation, saved, after):
     frames, both, model = tokens.shape
     rows = frames * both // 2
     low = jnp.bfloat16
-    loaded = (gdy, out_weight, att, qkv, prob, qkv_weight)
     return pl.pallas_call(
         backward_kernel,
-        out_shape=jax.ShapeDtypeStruct((frames, both, model), low),
-        in_specs=[smem()] * 3 + [vmem()] * 2 + [hbm()] * len(loaded),
-        out_specs=vmem(),
-        scratch_shapes=[pltpu.VMEM(array.shape, low) for array in loaded]
+        out_shape=pltpu.HBM((frames, both, model), low),
+        in_specs=[smem()] * 3 + [vmem()] * 2 + [hbm()] * (len(saved) + 1),
+        out_specs=hbm(),
+        scratch_shapes=[pltpu.VMEM(array.shape, low) for array in saved]
         + [
             pltpu.VMEM((rows, model), low),
             pltpu.VMEM((rows, 3 * model), low),
             pltpu.VMEM((rows, model), jnp.float32),
             pltpu.VMEM((rows, model), jnp.float32),
-            pltpu.SemaphoreType.DMA((len(loaded),)),
+            pltpu.VMEM((frames, both, model), low),
+            pltpu.SemaphoreType.DMA((len(saved),)),
+            pltpu.SemaphoreType.DMA((4,)),
         ],
-        compiler_params=pltpu.CompilerParams(vmem_limit_bytes=58 * MIB),
+        compiler_params=pltpu.CompilerParams(vmem_limit_bytes=36 * MIB),
         cost_estimate=pl.CostEstimate(
             flops=2 * rows * model * 6 * model, bytes_accessed=16 * MIB, transcendentals=0
         ),
         name="backward",
-    )(frame_clip, clip_patches, place, tokens, modulation, *loaded)
-
-
-def pack_kernel(latent_hbm, cotangent_hbm, out_ref, latent_ref, cotangent_ref, sems):
+    )(
+        frame_clip, clip_patches, place, in_vmem(tokens), modulation, *map(in_hbm, saved), in_hbm(after)
+    )
+
+
+def pack_kernel(
+    latent_hbm, cotangent_hbm, out_hbm, latent_ref, cotangent_ref, out_ref, sems, store_sems
+):
     both = out_ref.shape[1]
     patches = both // 2
     parts = sems.shape[1]
@@ -369,6 +416,7 @@
             load = pltpu.make_async_copy(source.at[where, :], target.at[where, :], sems.at[k, part])
             load.start()
             loads.append(load)
+    stores = []
     for part in range(parts):
         loads[2 * part].wait()
         loads[2 * part + 1].wait()
@@ -381,40 +429,62 @@
                 out_ref[start // patches + k] = jnp.concatenate(
                     [latent[half], cotangent[half]], axis=0
                 ).astype(jnp.bfloat16)
+        where = slice(part * rows // patches, (part + 1) * rows // patches)
+        store = pltpu.make_async_copy(out_ref.at[where], out_hbm.at[where], store_sems.at[part])
+        store.start()
+        stores.append(store)
+    for store in stores:
+        store.wait()
 
 
 def run_pack(latents, cotangent, seq):
     rows, model = latents.shape
     low = jnp.bfloat16
+    size = (seq, 2 * rows // seq, model)
     return pl.pallas_call(
         pack_kernel,
-        out_shape=jax.ShapeDtypeStruct((seq, 2 * rows // seq, model), low),
+        out_shape=pltpu.HBM(size, low),
         in_specs=[hbm()] * 2,
-        out_specs=vmem(),
-        scratch_shapes=[pltpu.VMEM((rows, model), low)] * 2 + [pltpu.SemaphoreType.DMA((2, 4))],
-        compiler_params=pltpu.CompilerParams(vmem_limit_bytes=60 * MIB),
+        out_specs=hbm(),
+        scratch_shapes=[pltpu.VMEM((rows, model), low)] * 2
+        + [
+            pltpu.VMEM(size, low),
+            pltpu.SemaphoreType.DMA((2, 4)),
+            pltpu.SemaphoreType.DMA((4,)),
+        ],
+        compiler_params=pltpu.CompilerParams(vmem_limit_bytes=12 * MIB),
         name="pack",
-    )(latents, cotangent)
-
-
-def add_kernel(left_ref, right_ref, out_ref):
-    step_rows = 64
-    for start in range(0, left_ref.shape[0], step_rows):
-        where = slice(start, start + step_rows)
+    )(in_hbm(latents), in_hbm(cotangent))
+
+
+def add_kernel(left_ref, right_ref, out_hbm, out_ref, store_sems):
+    parts = store_sems.shape[0]
+    rows = out_ref.shape[0] // parts
+    stores = []
+    for part in range(parts):
+        where = slice(part * rows, (part + 1) * rows)
         out_ref[where, :] = (
             left_ref[where, :].astype(jnp.float32) + right_ref[where, :].astype(jnp.float32)
         ).astype(jnp.bfloat16)
+        store = pltpu.make_async_copy(
+            out_ref.at[where, :], out_hbm.at[where, :], store_sems.at[part]
+        )
+        store.start()
+        stores.append(store)
+    for store in stores:
+        store.wait()
 
 
 def run_add(left, right):
     return pl.pallas_call(
         add_kernel,
-        out_shape=jax.ShapeDtypeStruct(left.shape, left.dtype),
+        out_shape=pltpu.HBM(left.shape, left.dtype),
         in_specs=[vmem()] * 2,
-        out_specs=vmem(),
+        out_specs=hbm(),
+        scratch_shapes=[pltpu.VMEM(left.shape, left.dtype), pltpu.SemaphoreType.DMA((5,))],
         compiler_params=pltpu.CompilerParams(vmem_limit_bytes=12 * MIB),
         name="add",
-    )(left, right)
+    )(in_vmem(left), in_vmem(right))
 
 
 def sum_kernel(terms_ref, after_ref, out_ref):
@@ -432,11 +502,11 @@
     return pl.pallas_call(
         sum_kernel,
         out_shape=jax.ShapeDtypeStruct(terms.shape[1:], jnp.float32),
-        in_specs=[vmem(), pl.BlockSpec(memory_space=pl.ANY)],
+        in_specs=[vmem(), hbm()],
         out_specs=vmem(),
         compiler_params=pltpu.CompilerParams(vmem_limit_bytes=12 * MIB),
         name="sum",
-    )(terms, after)
+    )(terms, in_hbm(after))
 
 
 def finish_kernel(returned_ref, left_ref, right_ref, block_ref, latent_ref, grad_ref):
@@ -487,16 +557,16 @@
     outgoing = run_pack(latents.reshape(patches, model), cotangent.reshape(patches, model), seq)
     tokens = lax.all_to_all(outgoing, "seq", 0, 0, tiled=True)
     mod = modulation[0].transpose(1, 0, 2)
-    qkv, prob, att, gdy, keep, send = run_forward(
+    qkv, prob, att, gdy, shares, send = run_forward(
         frame_clip, clip_patches, place, tokens, mod, qkv_weight, chips
     )
     other = lax.ppermute(send, "seq", [(i, i ^ 1) for i in range(seq)])
+    keep, qkv, prob, att, gdy = run_keep(place, shares, (qkv, prob, att, gdy))
     pair = run_add(keep, other).reshape(chips, SHARE_ROWS, model)
     same_core = [[2 * chip + core for chip in range(chips)] for core in range(2)]
     terms = lax.all_to_all(pair, "seq", 0, 0, tiled=True, axis_index_groups=same_core)
-    results = run_backward(
-        frame_clip, clip_patches, place, tokens, mod, gdy, out_weight, att, qkv, prob, qkv_weight
-    )
+    saved = (gdy, out_weight, att, qkv, prob, qkv_weight)
+    results = run_backward(frame_clip, clip_patches, place, tokens, mod, saved, pair)
     total = run_sum(terms, results).astype(jnp.bfloat16)
     stride = 1
     while True:

time: 104 us -> 98.3 us (0.945)
  local copies, waits for them, and re-layouts: 2.39 us -> 0.02 us
  Pallas kernels: 33.3 us -> 31.5 us
    ppermute x1, waiting for transfers between devices: 3.34 us -> 0.25 us  [per_device(): other = lax.ppermute(send, 'seq', [(i, i ^ 1) for i in range(seq)])]
    unnamed x4 -> x6, local copies, waits for them, and re-layouts: 2.39 us -> 0.02 us
    pallas_call x4 -> x5, Pallas kernels: 32 us -> 30.1 us  [the longest x1 14.5 us: run_backward(): pl.pallas_call(backward_kernel, out_shape=pltpu.HBM((frames, both, model)...]
    all_to_all x1, waiting for transfers between devices: 4.98 us -> 6.62 us  [per_device(): lax.all_to_all(pair, 'seq', 0, 0, tiled=True, axis_index_groups=same_core)]
  transfers between devices with their start and end apart: 7 -> 7, of which waited for: 5 -> 5; matrix products, arithmetic and copies ran while one was open for 1% -> 0% of each run, Pallas kernels for 16% -> 18%
where the time goes in v6:
time: 98.3 us; the launch traced here: 96.7 us
  waiting for transfers between devices  32.3 us (33%)
  starting transfers between devices  32 us (33%)
  Pallas kernels  31.5 us (32%)
    all_to_all x1, waiting for transfers between devices, per_device(): tokens = lax.all_to_all(outgoing, 'seq', 0, 0, tiled=True)  17.4 us
    pallas_call x1, Pallas kernels, run_backward(): pl.pallas_call(backward_kernel, out_shape=pltpu.HBM((frames, both, model)...  14.5 us
    ppermute x3, starting transfers between devices, per_device(): met = lax.ppermute(total, 'dp', [(i, i ^ stride) for i in range(groups)])  11.6 us
    pallas_call x1, Pallas kernels, run_forward(): pl.pallas_call(forward_kernel, out_shape=tuple((pltpu.VMEM(size, low) for...  9.36 us
    all_to_all x1, starting transfers between devices, per_device(): tokens = lax.all_to_all(outgoing, 'seq', 0, 0, tiled=True)  7.76 us
    all_to_all x1, starting transfers between devices, per_device(): returned = lax.all_to_all(results, 'seq', 0, 0, tiled=True)  7.2 us
    all_to_all x1, waiting for transfers between devices, per_device(): lax.all_to_all(pair, 'seq', 0, 0, tiled=True, axis_index_groups=same_core)  6.62 us
    all_to_all x1, starting transfers between devices, per_device(): lax.all_to_all(pair, 'seq', 0, 0, tiled=True, axis_index_groups=same_core)  5.24 us
  transfers between devices with their start and end apart: 7, of which 5 were waited for; matrix products, arithmetic and copies ran while one was open for 0% of the time, Pallas kernels for 18%

profile of v6, /device:TPU:2, one launch (start us, length us, event | category | flops | bytes accessed | tf_op | source)
XLA Modules:
  0.0 96.7 jit_solution(4499099757463946686)
XLA Ops:
  0.6 2.2 %pack.1 = bf16[32,16,1152]{2,1,0:T(8,128)(2,1)} custom-call(bf16[256,1152]{1,0:T(8,128)(2,1)} %bitcast.14, bf16[256,1152]{1,0:T(8,128)(2,1)} %bitcast.15), custom_call_target="tpu_custom_call" | custom-call | tf_op jit(solution)/shard_map/pack/pallas_call | solution.py:444
  2.8 0.0 copy-start
  2.8 0.0 copy-start.1
  2.8 0.0 copy-start.2
  2.9 7.8 %all-to-all-start = ((bf16[32,16,1152]{2,1,0:T(8,128)(2,1)}), bf16[32,16,1152]{2,1,0:T(8,128)(2,1)S(1)}, u32[]{:S(2)}, u32[]{:S(2)}) async-start(bf16[32,16,1152]{2,1,0:T(8,128)(2,1)} %pack.1), calls=%async_computation | async-start | bytes 2359296 | tf_op jit(solution)/shard_map/all_to_all | solution.py:558
  10.6 0.1 pad_add_fusion.place_ref
  10.7 17.4 %all-to-all-done.tokens_ref = bf16[32,16,1152]{2,1,0:T(8,128)(2,1)S(1)} async-done(((bf16[32,16,1152]{2,1,0:T(8,128)(2,1)}), bf16[32,16,1152]{2,1,0:T(8,128)(2,1)S(1)}, u32[]{:S(2)}, u32[]{:S(2)}) %all-to-all-start) | async-done | bytes 1179680 | tf_op jit(solution)/shard_map/all_to_all | solution.py:558
  28.1 0.0 copy-done
  28.1 0.0 copy-done.1
  28.2 0.0 copy-done.2
  28.2 9.4 %forward.1 = (bf16[256,3456]{1,0:T(8,128)(2,1)S(1)}, bf16[16,256,256]{2,1,0:T(8,128)(2,1)S(1)}, bf16[256,1152]{1,0:T(8,128)(2,1)S(1)}, bf16[256,1152]{1,0:T(8,12...) custom-call(s32[1,32]{1,0:T(1,128)S(1)} %copy-done.1, s32[1,4]{1,0:T(1,128)S(1)} %copy-done.2, ...), custom_call_target="tpu_custom_call" | custom-call | flops 2717908992 | bytes 12582912 | tf_op jit(solution)/shard_map/forward/pallas_call | solution.py:354
  37.5 0.2 collective-permute-start
  37.7 2.9 %keep.1 = (bf16[640,1152]{1,0:T(8,128)(2,1)S(1)}, bf16[256,3456]{1,0:T(8,128)(2,1)}, bf16[16,256,256]{2,1,0:T(8,128)(2,1)}, bf16[256,1152]{1,0:T(8,128)(2,1)}, bf16[256,1152]{1,0:T(8,128)(2,1)}) custom-call(s32[2]{0:T(128)S(1)} %pad_add_fusion.place_ref, bf16[2,640,256]{2,1,0:T(8,128)(2,1)S(1)} %get-tuple-element.17.share_ref, ...), custom_call_target="tpu_custom_call" | custom-call | flops 377487360 | bytes 6291456 | tf_op jit(solution)/shard_map/keep/pallas_call | solution.py:211
  40.6 0.3 collective-permute-done.right_ref
  40.9 1.2 %add.18 = bf16[640,1152]{1,0:T(8,128)(2,1)} custom-call(bf16[640,1152]{1,0:T(8,128)(2,1)S(1)} %get-tuple-element.26.left_ref, bf16[640,1152]{1,0:T(8,128)(2,1)S(1)} %collective-permute-done.right_ref), custom_call_target="tpu_custom_call" | custom-call | tf_op jit(solution)/shard_map/add/pallas_call | solution.py:479
  42.1 5.2 %all-to-all-start.2 = ((bf16[16,40,1152]{2,1,0:T(8,128)(2,1)}), bf16[16,40,1152]{2,1,0:T(8,128)(2,1)S(1)}, u32[]{:S(2)}, u32[]{:S(2)}) async-start(bf16[16,40,1152]{2,1,0:T(8,128)(2,1)} %bitcast.12), calls=%async_computation.2 | async-start | bytes 2949120 | tf_op jit(solution)/shard_map/all_to_all | solution.py:567
  47.3 14.5 %backward.1.after_ref = bf16[32,16,1152]{2,1,0:T(8,128)(2,1)} custom-call(s32[1,32]{1,0:T(1,128)S(1)} %copy-done.1, s32[1,4]{1,0:T(1,128)S(1)} %copy-done.2, s32[2]{0:T(128)S(1)} %pad_add_fusion.place_ref, bf16[32,16,1152]{2,1,0:T(8,128)(2,1)S(1)} %all-to-all-done.tokens_ref, f32[3,4,1152]{2,1,0:T(4,128)S(1)} %bitcast.11, ...), custom_call_target="tpu_custom_call" | custom-call | flops 4076863488 | bytes 16777216 | tf_op jit(solution)/shard_map/backward/pallas_call | solution.py:378
  61.9 6.6 %all-to-all-done.2.terms_ref = bf16[16,40,1152]{2,1,0:T(8,128)(2,1)S(1)} async-done(((bf16[16,40,1152]{2,1,0:T(8,128)(2,1)}), bf16[16,40,1152]{2,1,0:T(8,128)(2,1)S(1)}, u32[]{:S(2)}, u32[]{:S(2)}) %all-to-all-start.2) | async-done | bytes 1474592 | tf_op jit(solution)/shard_map/all_to_all | solution.py:567
  68.5 0.2 sum.1
  68.7 2.0 %collective-permute-start.1 = (bf16[40,1152]{1,0:T(8,128)(2,1)S(1)}, bf16[40,1152]{1,0:T(8,128)(2,1)S(1)}, u32[]{:S(2)}, u32[]{:S(2)}) collective-permute-start(bf16[40,1152]{1,0:T(8,128)(2,1)S(1)} %convert_element_type.21), channel_id=1, source_target_pairs={{0,32},{32,0},{64,96},{96,64},{128,160},{160,128},{192,224},{224,1... | collective-permute-start | bytes 276488 | tf_op jit(solution)/shard_map/ppermute | solution.py:573
  70.7 7.2 %all-to-all-start.1 = ((bf16[32,16,1152]{2,1,0:T(8,128)(2,1)}), bf16[32,16,1152]{2,1,0:T(8,128)(2,1)S(1)}, u32[]{:S(2)}, u32[]{:S(2)}) async-start(bf16[32,16,1152]{2,1,0:T(8,128)(2,1)} %backward.1.after_ref), calls=%async_computation.1 | async-start | bytes 2359296 | tf_op jit(solution)/shard_map/all_to_all | solution.py:578
  77.9 0.0 collective-permute-done.1
  77.9 3.4 %collective-permute-start.2 = (bf16[40,1152]{1,0:T(8,128)(2,1)S(1)}, bf16[40,1152]{1,0:T(8,128)(2,1)S(1)}, u32[]{:S(2)}, u32[]{:S(2)}) collective-permute-start(bf16[40,1152]{1,0:T(8,128)(2,1)S(1)} %add_convert_fusion.1), channel_id=1, source_target_pairs={{0,64},{32,96},{64,0},{96,32},{128,192},{160,224},{192,128},{224,1... | collective-permute-start | bytes 276488 | tf_op jit(solution)/shard_map/ppermute | solution.py:573
  81.3 4.5 %collective-permute-done.2 = bf16[40,1152]{1,0:T(8,128)(2,1)S(1)} collective-permute-done((bf16[40,1152]{1,0:T(8,128)(2,1)S(1)}, bf16[40,1152]{1,0:T(8,128)(2,1)S(1)}, u32[]{:S(2)}, u32[]{:S(2)}) %collective-permute-start.2) | collective-permute-done | bytes 92192 | tf_op jit(solution)/shard_map/ppermute | solution.py:573
  85.8 6.2 %collective-permute-start.3 = (bf16[40,1152]{1,0:T(8,128)(2,1)S(1)}, bf16[40,1152]{1,0:T(8,128)(2,1)S(1)}, u32[]{:S(2)}, u32[]{:S(2)}) collective-permute-start(bf16[40,1152]{1,0:T(8,128)(2,1)S(1)} %add_convert_fusion.left_ref), channel_id=1, source_target_pairs={{0,128},{32,160},{64,192},{96,224},{128,0},{160,32},{192,64},{224,... | collective-permute-start | bytes 276488 | tf_op jit(solution)/shard_map/ppermute | solution.py:573
  92.1 3.5 %all-to-all-done.1.returned_ref = bf16[32,16,1152]{2,1,0:T(8,128)(2,1)S(1)} async-done(((bf16[32,16,1152]{2,1,0:T(8,128)(2,1)}), bf16[32,16,1152]{2,1,0:T(8,128)(2,1)S(1)}, u32[]{:S(2)}, u32[]{:S(2)}) %all-to-all-start.1) | async-done | bytes 1179680 | tf_op jit(solution)/shard_map/all_to_all | solution.py:578
  95.5 0.0 collective-permute-done.3.right_ref
  95.5 1.2 %finish.1 = (bf16[256,1152]{1,0:T(8,128)(2,1)}, bf16[256,1152]{1,0:T(8,128)(2,1)}, f32[36,1152]{1,0:T(8,128)}) custom-call(bf16[32,16,1152]{2,1,0:T(8,128)(2,1)S(1)} %all-to-all-done.1.returned_ref, bf16[40,1152]{1,0:T(8,128)(2,1)S(1)} %add_convert_fusion.left_ref, bf16[40,1152]{1,0:T(8,128)(2,1)S(1)} %collective-permute-done.3.right_ref), custom_call_target="tpu_custom_call" | custom-call | bytes 4194304 | tf_op jit(solution)/shard_map/finish/pallas_call | solution.py:532
  (3 shorter events, 0.1 us)
Async XLA Ops:
  2.8 25.3 %copy-start = (f32[1,4,3,1152]{3,1,2,0:T(4,128)S(1)}, f32[1,4,3,1152]{3,1,2,0:T(4,128)}, u32[]{:S(2)}) copy-start(f32[1,4,3,1152]{3,1,2,0:T(4,128)} %param.11) | copy-start | bytes 165892
  2.8 25.3 %copy-start.1 = (s32[1,32]{1,0:T(1,128)S(1)}, s32[1,32]{1,0:T(1,128)}, u32[]{:S(2)}) copy-start(s32[1,32]{1,0:T(1,128)} %clip_ref.3) | copy-start | bytes 388
  2.8 25.3 %copy-start.2 = (s32[1,4]{1,0:T(1,128)S(1)}, s32[1,4]{1,0:T(1,128)}, u32[]{:S(2)}) copy-start(s32[1,4]{1,0:T(1,128)} %count_ref.3) | copy-start | bytes 52
  2.9 25.3 %all-to-all-start = ((bf16[32,16,1152]{2,1,0:T(8,128)(2,1)}), bf16[32,16,1152]{2,1,0:T(8,128)(2,1)S(1)}, u32[]{:S(2)}, u32[]{:S(2)}) async-start(bf16[32,16,1152]{2,1,0:T(8,128)(2,1)} %pack.1), calls=%async_computation | async-start | bytes 2359296 | tf_op jit(solution)/shard_map/all_to_all | solution.py:558
  37.5 3.4 %collective-permute-start = (bf16[640,1152]{1,0:T(8,128)(2,1)S(1)}, bf16[640,1152]{1,0:T(8,128)(2,1)S(1)}, u32[]{:S(2)}, u32[]{:S(2)}) collective-permute-start(bf16[640,1152]{1,0:T(8,128)(2,1)S(1)} %get-tuple-element.27), channel_id=1, source_target_pairs={{0,1},{1,0},{2,3},{3,2},{4,5},{5,4},{6,7},{7,6},{8,9},{9,8},{10,11... | collective-permute-start | bytes 4423688 | tf_op jit(solution)/shard_map/ppermute | solution.py:563
  42.1 26.4 %all-to-all-start.2 = ((bf16[16,40,1152]{2,1,0:T(8,128)(2,1)}), bf16[16,40,1152]{2,1,0:T(8,128)(2,1)S(1)}, u32[]{:S(2)}, u32[]{:S(2)}) async-start(bf16[16,40,1152]{2,1,0:T(8,128)(2,1)} %bitcast.12), calls=%async_computation.2 | async-start | bytes 2949120 | tf_op jit(solution)/shard_map/all_to_all | solution.py:567
  68.7 9.2 %collective-permute-start.1 = (bf16[40,1152]{1,0:T(8,128)(2,1)S(1)}, bf16[40,1152]{1,0:T(8,128)(2,1)S(1)}, u32[]{:S(2)}, u32[]{:S(2)}) collective-permute-start(bf16[40,1152]{1,0:T(8,128)(2,1)S(1)} %convert_element_type.21), channel_id=1, source_target_pairs={{0,32},{32,0},{64,96},{96,64},{128,160},{160,128},{192,224},{224,1... | collective-permute-start | bytes 276488 | tf_op jit(solution)/shard_map/ppermute | solution.py:573
  70.7 24.8 %all-to-all-start.1 = ((bf16[32,16,1152]{2,1,0:T(8,128)(2,1)}), bf16[32,16,1152]{2,1,0:T(8,128)(2,1)S(1)}, u32[]{:S(2)}, u32[]{:S(2)}) async-start(bf16[32,16,1152]{2,1,0:T(8,128)(2,1)} %backward.1.after_ref), calls=%async_computation.1 | async-start | bytes 2359296 | tf_op jit(solution)/shard_map/all_to_all | solution.py:578
  77.9 7.9 %collective-permute-start.2 = (bf16[40,1152]{1,0:T(8,128)(2,1)S(1)}, bf16[40,1152]{1,0:T(8,128)(2,1)S(1)}, u32[]{:S(2)}, u32[]{:S(2)}) collective-permute-start(bf16[40,1152]{1,0:T(8,128)(2,1)S(1)} %add_convert_fusion.1), channel_id=1, source_target_pairs={{0,64},{32,96},{64,0},{96,32},{128,192},{160,224},{192,128},{224,1... | collective-permute-start | bytes 276488 | tf_op jit(solution)/shard_map/ppermute | solution.py:573
  85.8 9.7 %collective-permute-start.3 = (bf16[40,1152]{1,0:T(8,128)(2,1)S(1)}, bf16[40,1152]{1,0:T(8,128)(2,1)S(1)}, u32[]{:S(2)}, u32[]{:S(2)}) collective-permute-start(bf16[40,1152]{1,0:T(8,128)(2,1)S(1)} %add_convert_fusion.left_ref), channel_id=1, source_target_pairs={{0,128},{32,160},{64,192},{96,224},{128,0},{160,32},{192,64},{224,... | collective-permute-start | bytes 276488 | tf_op jit(solution)/shard_map/ppermute | solution.py:573

commit v7 on v6

--- a/solution.py
+++ b/solution.py
@@ -7,7 +7,7 @@
 
 HEADS = 16
 LANES = 128
-CHUNK = 384
+EDGES = (0, 512, 1152)
 SHARE_ROWS = 40
 MIB = 1024 * 1024
 
@@ -18,6 +18,11 @@
 
 def dot(left, right, dims):
     return lax.dot_general(left, right, dims, preferred_element_type=jnp.float32)
+
+
+def wide_columns(width):
+    edges = list(range(0, width - 511, 512))
+    return [slice(low, high) for low, high in zip(edges, edges[1:] + [width])]
 
 
 def head_span(head, head_dim):
@@ -62,16 +67,16 @@
     qkv_ref, prob_ref, att_ref, gdy_ref, share_ref, send_ref,
     wqkv_ref, xmod_ref, same_ref, turned_ref, load_sems,
 ):
-    frames, both, model = tokens_ref.shape
-    patches = both // 2
-    rows = frames * patches
+    rows, model = xmod_ref.shape
+    frames = clip_ref.shape[1]
+    patches = rows // frames
     head_dim = model // HEADS
     base = place_ref[0]
     core = place_ref[1]
 
-    parts_n = model // CHUNK
+    parts_n = len(EDGES) - 1
     columns = [
-        [slice(kind * model + part * CHUNK, kind * model + (part + 1) * CHUNK) for kind in range(3)]
+        [slice(kind * model + EDGES[part], kind * model + EDGES[part + 1]) for kind in range(3)]
         for part in range(parts_n)
     ]
     loads = [
@@ -92,24 +97,25 @@
     start_loads(0)
 
     def pair_step(step, carry):
+        where = pl.ds(pl.multiple_of(2 * step * patches, 2 * patches), 2 * patches)
+        latent = tokens_ref[where, :model].astype(jnp.float32)
+        cotangent = tokens_ref[where, model:].astype(jnp.float32)
         xmods, gdys = [], []
         for k in range(2):
-            frame = 2 * step + k
-            clip = clip_ref[0, frame]
+            half = slice(k * patches, (k + 1) * patches)
+            clip = clip_ref[0, 2 * step + k]
             shift = mod_ref[0, pl.ds(clip, 1), :]
             scale = mod_ref[1, pl.ds(clip, 1), :]
             gate = mod_ref[2, pl.ds(clip, 1), :]
-            both_f = tokens_ref[frame].astype(jnp.float32)
-            normed, _ = normalize(both_f[:patches])
+            normed, _ = normalize(latent[half])
             xmods.append(normed * (1.0 + scale) + shift)
             valid = valid_patches(base, count_ref[0, clip], patches)
-            gdys.append(valid * gate * both_f[patches:])
-        where = pl.ds(pl.multiple_of(step * both, both), both)
+            gdys.append(valid * gate * cotangent[half])
         xmod_ref[where, :] = jnp.concatenate(xmods, axis=0).astype(jnp.bfloat16)
         gdy_ref[where, :] = jnp.concatenate(gdys, axis=0).astype(jnp.bfloat16)
         return carry
 
-    lax.fori_loop(0, frames // 2, pair_step, 0, unroll=16)
+    lax.fori_loop(0, frames // 2, pair_step, 0, unroll=4)
     start_loads(1)
 
     starts = []
@@ -166,12 +172,12 @@
         for where in columns[part]:
             qkv_ref[:, where] = dot(xmod, wqkv_ref[:, where], NN).astype(jnp.bfloat16)
         scores = None
-        while head < HEADS and (head + 1) * head_dim <= (part + 1) * CHUNK:
+        while head < HEADS and (head + 1) * head_dim <= EDGES[part + 1]:
             first, last, low, high = head_span(head, head_dim)
             mask = head_mask(first, last, low, high)
             if scores is None:
                 scores = score_of(head)
-            last_head = (head + 2) * head_dim > (part + 1) * CHUNK
+            last_head = (head + 2) * head_dim > EDGES[part + 1]
             later = None if last_head else score_of(head + 1)
             value = qkv_ref[:, 2 * model + low : 2 * model + high] * mask
             expo = jnp.exp(scores * head_dim ** (-0.5)) * same_ref[...]
@@ -182,10 +188,8 @@
             scores = later
             head += 1
 
-    for start in range(0, model, CHUNK):
-        send_ref[:, start : start + CHUNK] = dot(
-            share_ref[1 - core], att_ref[:, start : start + CHUNK], NN
-        ).astype(jnp.bfloat16)
+    for where in wide_columns(model):
+        send_ref[:, where] = dot(share_ref[1 - core], att_ref[:, where], NN).astype(jnp.bfloat16)
 
 
 def keep_kernel(place_ref, share_ref, qkv_ref, prob_ref, att_ref, gdy_ref, *refs):
@@ -197,10 +201,8 @@
         stores.append(store)
     core = place_ref[1]
     model = keep_ref.shape[1]
-    for start in range(0, model, CHUNK):
-        keep_ref[:, start : start + CHUNK] = dot(
-            share_ref[core], att_ref[:, start : start + CHUNK], NN
-        ).astype(jnp.bfloat16)
+    for where in wide_columns(model):
+        keep_ref[:, where] = dot(share_ref[core], att_ref[:, where], NN).astype(jnp.bfloat16)
     for store in stores:
         store.wait()
 
@@ -231,8 +233,9 @@
     datt_ref, dqkv_ref, proj_ref, dxmod_ref, out_ref, sems, store_sems,
 ):
     del after_ref
-    frames, both, model = tokens_ref.shape
-    patches = both // 2
+    rows, model = gdy_ref.shape
+    frames = clip_ref.shape[1]
+    patches = rows // frames
     head_dim = model // HEADS
     att_scale = head_dim ** (-0.5)
     base = place_ref[0]
@@ -249,14 +252,12 @@
     loads[0].wait()
     loads[1].wait()
     gdy = gdy_ref[...]
-    for start in range(0, model, CHUNK):
-        datt_ref[:, start : start + CHUNK] = dot(
-            gdy, wout_ref[start : start + CHUNK, :], NT
-        ).astype(jnp.bfloat16)
+    for where in wide_columns(model):
+        datt_ref[:, where] = dot(gdy, wout_ref[where, :], NT).astype(jnp.bfloat16)
     loads[2].wait()
     att = att_ref[...]
-    for start in range(0, model, CHUNK):
-        proj_ref[:, start : start + CHUNK] = dot(att, wout_ref[:, start : start + CHUNK], NN)
+    for where in wide_columns(model):
+        proj_ref[:, where] = dot(att, wout_ref[:, where], NN)
     loads[3].wait()
     loads[4].wait()
 
@@ -287,37 +288,48 @@
 
     loads[5].wait()
     dqkv = dqkv_ref[...]
-    for start in range(0, model, CHUNK):
-        dxmod_ref[:, start : start + CHUNK] = dot(dqkv, wqkv_ref[start : start + CHUNK, :], NT)
-
-    def frame_step(frame, carry):
-        clip = clip_ref[0, frame]
-        scale = mod_ref[1, pl.ds(clip, 1), :]
-        gate = mod_ref[2, pl.ds(clip, 1), :]
-        valid = valid_patches(base, count_ref[0, clip], patches)
-        where = pl.ds(pl.multiple_of(frame * patches, patches), patches)
-        both_f = tokens_ref[frame].astype(jnp.float32)
-        latent = both_f[:patches]
-        block_out = latent + valid * gate * proj_ref[where, :]
-        normed, inv_std = normalize(latent)
-        dnorm = dxmod_ref[where, :] * (1.0 + scale)
-        branch = inv_std * (
-            dnorm
-            - jnp.mean(dnorm, axis=-1, keepdims=True)
-            - normed * jnp.mean(dnorm * normed, axis=-1, keepdims=True)
+    for where in wide_columns(model):
+        dxmod_ref[:, where] = dot(dqkv, wqkv_ref[where, :], NT)
+
+    def pair_step(step, carry):
+        where = pl.ds(pl.multiple_of(2 * step * patches, 2 * patches), 2 * patches)
+        latent_pair = tokens_ref[where, :model].astype(jnp.float32)
+        cotangent = tokens_ref[where, model:].astype(jnp.float32)
+        blocks, branches = [], []
+        for k in range(2):
+            half = slice(k * patches, (k + 1) * patches)
+            clip = clip_ref[0, 2 * step + k]
+            scale = mod_ref[1, pl.ds(clip, 1), :]
+            gate = mod_ref[2, pl.ds(clip, 1), :]
+            valid = valid_patches(base, count_ref[0, clip], patches)
+            own = pl.ds(pl.multiple_of((2 * step + k) * patches, patches), patches)
+            latent = latent_pair[half]
+            blocks.append(latent + valid * gate * proj_ref[own, :])
+            normed, inv_std = normalize(latent)
+            dnorm = dxmod_ref[own, :] * (1.0 + scale)
+            branches.append(
+                inv_std
+                * (
+                    dnorm
+                    - jnp.mean(dnorm, axis=-1, keepdims=True)
+                    - normed * jnp.mean(dnorm * normed, axis=-1, keepdims=True)
+                )
+            )
+        out_ref[where, :model] = jnp.concatenate(blocks, axis=0).astype(jnp.bfloat16)
+        out_ref[where, model:] = (cotangent + jnp.concatenate(branches, axis=0)).astype(
+            jnp.bfloat16
         )
-        out_ref[frame] = jnp.concatenate(
-            [block_out, both_f[patches:] + branch], axis=0
-        ).astype(jnp.bfloat16)
         return carry
 
     stores = []
     part_n = store_sems.shape[0]
-    step = frames // part_n
+    steps = frames // (2 * part_n)
     for part in range(part_n):
-        lax.fori_loop(part * step, (part + 1) * step, frame_step, 0, unroll=step)
-        where = slice(part * step, (part + 1) * step)
-        store = pltpu.make_async_copy(out_ref.at[where], out_hbm.at[where], store_sems.at[part])
+        lax.fori_loop(part * steps, (part + 1) * steps, pair_step, 0, unroll=steps)
+        where = slice(2 * part * steps * patches, 2 * (part + 1) * steps * patches)
+        store = pltpu.make_async_copy(
+            out_ref.at[where, :], out_hbm.at[where, :], store_sems.at[part]
+        )
         store.start()
         stores.append(store)
     for store in stores:
@@ -345,10 +357,9 @@
 
 
 def run_forward(frame_clip, clip_patches, place, tokens, modulation, qkv_weight, chips):
-    frames, both, model = tokens.shape
-    rows = frames * both // 2
+    rows, model = tokens.shape[0], tokens.shape[1] // 2
     low = jnp.bfloat16
-    groups = model // CHUNK
+    groups = len(EDGES) - 1
     sizes = ((rows, 3 * model), (HEADS, rows, rows), (rows, model), (rows, model))
     sizes += ((2, chips * SHARE_ROWS, rows), (chips * SHARE_ROWS, model))
     return pl.pallas_call(
@@ -372,12 +383,11 @@
 
 
 def run_backward(frame_clip, clip_patches, place, tokens, modulation, saved, after):
-    frames, both, model = tokens.shape
-    rows = frames * both // 2
+    rows, model = tokens.shape[0], tokens.shape[1] // 2
     low = jnp.bfloat16
     return pl.pallas_call(
         backward_kernel,
-        out_shape=pltpu.HBM((frames, both, model), low),
+        out_shape=pltpu.HBM(tokens.shape, low),
         in_specs=[smem()] * 3 + [vmem()] * 2 + [hbm()] * (len(saved) + 1),
         out_specs=hbm(),
         scratch_shapes=[pltpu.VMEM(array.shape, low) for array in saved]
@@ -386,7 +396,7 @@
             pltpu.VMEM((rows, 3 * model), low),
             pltpu.VMEM((rows, model), jnp.float32),
             pltpu.VMEM((rows, model), jnp.float32),
-            pltpu.VMEM((frames, both, model), low),
+            pltpu.VMEM(tokens.shape, low),
             pltpu.SemaphoreType.DMA((len(saved),)),
             pltpu.SemaphoreType.DMA((4,)),
         ],
@@ -400,58 +410,26 @@
     )
 
 
-def pack_kernel(
-    latent_hbm, cotangent_hbm, out_hbm, latent_ref, cotangent_ref, out_ref, sems, store_sems
-):
-    both = out_ref.shape[1]
-    patches = both // 2
-    parts = sems.shape[1]
-    rows = latent_ref.shape[0] // parts
-    loads = []
-    for part in range(parts):
-        where = slice(part * rows, (part + 1) * rows)
-        for k, (source, target) in enumerate(
-            ((latent_hbm, latent_ref), (cotangent_hbm, cotangent_ref))
-        ):
-            load = pltpu.make_async_copy(source.at[where, :], target.at[where, :], sems.at[k, part])
-            load.start()
-            loads.append(load)
-    stores = []
-    for part in range(parts):
-        loads[2 * part].wait()
-        loads[2 * part + 1].wait()
-        for start in range(part * rows, (part + 1) * rows, both):
-            where = slice(start, start + both)
-            latent = latent_ref[where, :].astype(jnp.float32)
-            cotangent = cotangent_ref[where, :].astype(jnp.float32)
-            for k in range(2):
-                half = slice(k * patches, (k + 1) * patches)
-                out_ref[start // patches + k] = jnp.concatenate(
-                    [latent[half], cotangent[half]], axis=0
-                ).astype(jnp.bfloat16)
-        where = slice(part * rows // patches, (part + 1) * rows // patches)
-        store = pltpu.make_async_copy(out_ref.at[where], out_hbm.at[where], store_sems.at[part])
-        store.start()
-        stores.append(store)
-    for store in stores:
-        store.wait()
-
-
-def run_pack(latents, cotangent, seq):
+def pack_kernel(latent_hbm, cotangent_hbm, out_hbm, sems):
+    model = latent_hbm.shape[1]
+    copies = [
+        pltpu.make_async_copy(latent_hbm, out_hbm.at[:, :model], sems.at[0]),
+        pltpu.make_async_copy(cotangent_hbm, out_hbm.at[:, model:], sems.at[1]),
+    ]
+    for copy in copies:
+        copy.start()
+    for copy in copies:
+        copy.wait()
+
+
+def run_pack(latents, cotangent):
     rows, model = latents.shape
-    low = jnp.bfloat16
-    size = (seq, 2 * rows // seq, model)
     return pl.pallas_call(
         pack_kernel,
-        out_shape=pltpu.HBM(size, low),
+        out_shape=pltpu.HBM((rows, 2 * model), latents.dtype),
         in_specs=[hbm()] * 2,
         out_specs=hbm(),
-        scratch_shapes=[pltpu.VMEM((rows, model), low)] * 2
-        + [
-            pltpu.VMEM(size, low),
-            pltpu.SemaphoreType.DMA((2, 4)),
-            pltpu.SemaphoreType.DMA((4,)),
-        ],
+        scratch_shapes=[pltpu.SemaphoreType.DMA((2,))],
         compiler_params=pltpu.CompilerParams(vmem_limit_bytes=12 * MIB),
         name="pack",
     )(in_hbm(latents), in_hbm(cotangent))
@@ -509,35 +487,33 @@
     )(terms, in_hbm(after))
 
 
-def finish_kernel(returned_ref, left_ref, right_ref, block_ref, latent_ref, grad_ref):
-    groups, both, _ = returned_ref.shape
-    patches = both // 2
-    for step in range(groups // 2):
-        pair = [returned_ref[2 * step + k].astype(jnp.float32) for k in range(2)]
-        where = slice(step * both, (step + 1) * both)
-        block_ref[where, :] = jnp.concatenate([part[:patches] for part in pair], axis=0).astype(
-            jnp.bfloat16
-        )
-        latent_ref[where, :] = jnp.concatenate([part[patches:] for part in pair], axis=0).astype(
-            jnp.bfloat16
-        )
+def finish_kernel(returned_ref, left_ref, right_ref, block_hbm, latent_hbm, grad_ref, sems):
+    model = block_hbm.shape[1]
+    copies = [
+        pltpu.make_async_copy(returned_ref.at[:, :model], block_hbm, sems.at[0]),
+        pltpu.make_async_copy(returned_ref.at[:, model:], latent_hbm, sems.at[1]),
+    ]
+    for copy in copies:
+        copy.start()
     total = left_ref[...].astype(jnp.float32) + right_ref[...].astype(jnp.float32)
     grad_ref[...] = total[: grad_ref.shape[0]]
+    for copy in copies:
+        copy.wait()
 
 
 def run_finish(returned, left, right, share):
-    groups, both, model = returned.shape
+    rows, model = returned.shape[0], returned.shape[1] // 2
     low = jnp.bfloat16
-    rows = groups * both // 2
     return pl.pallas_call(
         finish_kernel,
         out_shape=(
-            jax.ShapeDtypeStruct((rows, model), low),
-            jax.ShapeDtypeStruct((rows, model), low),
+            pltpu.HBM((rows, model), low),
+            pltpu.HBM((rows, model), low),
             jax.ShapeDtypeStruct((share, model), jnp.float32),
         ),
         in_specs=[vmem()] * 3,
-        out_specs=(vmem(),) * 3,
+        out_specs=(hbm(), hbm(), vmem()),
+        scratch_shapes=[pltpu.SemaphoreType.DMA((2,))],
         compiler_params=pltpu.CompilerParams(vmem_limit_bytes=12 * MIB),
         cost_estimate=pl.CostEstimate(flops=0, bytes_accessed=4 * MIB, transcendentals=0),
         name="finish",
@@ -554,8 +530,11 @@
     index = lax.axis_index("seq")
     place = jnp.stack([index * mine, index % 2]).astype(jnp.int32)
 
-    outgoing = run_pack(latents.reshape(patches, model), cotangent.reshape(patches, model), seq)
-    tokens = lax.all_to_all(outgoing, "seq", 0, 0, tiled=True)
+    def exchange(rows):
+        pieces = rows.reshape(seq, mine, rows.shape[1])
+        return lax.all_to_all(pieces, "seq", 0, 0, tiled=True).reshape(rows.shape)
+
+    tokens = exchange(run_pack(latents.reshape(patches, model), cotangent.reshape(patches, model)))
     mod = modulation[0].transpose(1, 0, 2)
     qkv, prob, att, gdy, shares, send = run_forward(
         frame_clip, clip_patches, place, tokens, mod, qkv_weight, chips
@@ -575,7 +554,7 @@
         if stride >= groups:
             break
         total = (total.astype(jnp.float32) + met.astype(jnp.float32)).astype(jnp.bfloat16)
-    returned = lax.all_to_all(results, "seq", 0, 0, tiled=True)
+    returned = exchange(results)
     block_out, latent_grad, grad = run_finish(returned, total, met, share)
     return block_out.reshape(latents.shape), latent_grad.reshape(latents.shape), grad
 

time: 98.3 us -> 132 us (1.34)
  Pallas kernels: 31.5 us -> 65 us
    pallas_call x3, Pallas kernels: 17.8 us -> 53 us  [the longest x1 36.9 us: run_pack(): pl.pallas_call(pack_kernel, out_shape=pltpu.HBM((rows, 2 * model), latent...]
    pallas_call x1, Pallas kernels: 9.36 us -> 7.7 us  [run_forward(): pl.pallas_call(forward_kernel, out_shape=tuple((pltpu.VMEM(size, low) for...]
  transfers between devices with their start and end apart: 7 -> 7, of which waited for: 5 -> 5; matrix products, arithmetic and copies ran while one was open for 0% -> 0% of each run, Pallas kernels for 18% -> 13%
where the time goes in v7:
time: 132 us; the launch traced here: 130 us
  Pallas kernels  65 us (49%)
  waiting for transfers between devices  32.3 us (24%)
  starting transfers between devices  32 us (24%)
    pallas_call x1, Pallas kernels, run_pack(): pl.pallas_call(pack_kernel, out_shape=pltpu.HBM((rows, 2 * model), latent...  36.9 us
    all_to_all x2, waiting for transfers between devices, exchange(): return lax.all_to_all(pieces, 'seq', 0, 0, tiled=True).reshape(rows.shape)  20.9 us
    all_to_all x2, starting transfers between devices, exchange(): return lax.all_to_all(pieces, 'seq', 0, 0, tiled=True).reshape(rows.shape)  15 us
    pallas_call x1, Pallas kernels, run_backward(): pl.pallas_call(backward_kernel, out_shape=pltpu.HBM(tokens.shape, low), i...  14.4 us
    ppermute x3, starting transfers between devices, per_device(): met = lax.ppermute(total, 'dp', [(i, i ^ stride) for i in range(groups)])  11.6 us
    pallas_call x1, Pallas kernels, run_forward(): pl.pallas_call(forward_kernel, out_shape=tuple((pltpu.VMEM(size, low) for...  7.7 us
    all_to_all x1, waiting for transfers between devices, per_device(): lax.all_to_all(pair, 'seq', 0, 0, tiled=True, axis_index_groups=same_core)  6.69 us
    all_to_all x1, starting transfers between devices, per_device(): lax.all_to_all(pair, 'seq', 0, 0, tiled=True, axis_index_groups=same_core)  5.24 us
  transfers between devices with their start and end apart: 7, of which 5 were waited for; matrix products, arithmetic and copies ran while one was open for 0% of the time, Pallas kernels for 13%

profile of v7, /device:TPU:2, one launch (start us, length us, event | category | flops | bytes accessed | tf_op | source)
XLA Modules:
  0.0 130.4 jit_solution(16761386473416993388)
XLA Ops:
  0.6 36.9 %pack.1 = bf16[256,2304]{1,0:T(8,128)(2,1)} custom-call(bf16[256,1152]{1,0:T(8,128)(2,1)} %bitcast.23, bf16[256,1152]{1,0:T(8,128)(2,1)} %bitcast.24), custom_call_target="tpu_custom_call" | custom-call | tf_op jit(solution)/shard_map/pack/pallas_call | solution.py:427
  37.5 0.0 copy-start
  37.5 0.0 copy-start.1
  37.5 0.0 copy-start.2
  37.5 7.8 %all-to-all-start = ((bf16[32,8,2304]{2,1,0:T(8,128)(2,1)}), bf16[32,8,2304]{2,1,0:T(8,128)(2,1)S(1)}, u32[]{:S(2)}, u32[]{:S(2)}) async-start(bf16[32,8,2304]{2,1,0:T(8,128)(2,1)} %bitcast.22), calls=%async_computation | async-start | bytes 2359296 | tf_op jit(solution)/shard_map/all_to_all | solution.py:535
  45.3 0.1 pad_add_fusion.place_ref
  45.4 17.4 %all-to-all-done = bf16[32,8,2304]{2,1,0:T(8,128)(2,1)S(1)} async-done(((bf16[32,8,2304]{2,1,0:T(8,128)(2,1)}), bf16[32,8,2304]{2,1,0:T(8,128)(2,1)S(1)}, u32[]{:S(2)}, u32[]{:S(2)}) %all-to-all-start) | async-done | bytes 1179680 | tf_op jit(solution)/shard_map/all_to_all | solution.py:535
  62.8 0.0 copy-done
  62.8 0.0 copy-done.1
  62.8 0.0 copy-done.2
  62.8 7.7 %forward.1 = (bf16[256,3456]{1,0:T(8,128)(2,1)S(1)}, bf16[16,256,256]{2,1,0:T(8,128)(2,1)S(1)}, bf16[256,1152]{1,0:T(8,128)(2,1)S(1)}, bf16[256,1152]{1,0:T(8,12...) custom-call(s32[1,32]{1,0:T(1,128)S(1)} %copy-done.1, s32[1,4]{1,0:T(1,128)S(1)} %copy-done.2, ...), custom_call_target="tpu_custom_call" | custom-call | flops 2717908992 | bytes 12582912 | tf_op jit(solution)/shard_map/forward/pallas_call | solution.py:365
  70.5 0.2 collective-permute-start
  70.8 2.9 %keep.1 = (bf16[640,1152]{1,0:T(8,128)(2,1)S(1)}, bf16[256,3456]{1,0:T(8,128)(2,1)}, bf16[16,256,256]{2,1,0:T(8,128)(2,1)}, bf16[256,1152]{1,0:T(8,128)(2,1)}, bf16[256,1152]{1,0:T(8,128)(2,1)}) custom-call(s32[2]{0:T(128)S(1)} %pad_add_fusion.place_ref, bf16[2,640,256]{2,1,0:T(8,128)(2,1)S(1)} %get-tuple-element.17.share_ref, ...), custom_call_target="tpu_custom_call" | custom-call | flops 377487360 | bytes 6291456 | tf_op jit(solution)/shard_map/keep/pallas_call | solution.py:213
  73.6 0.3 collective-permute-done.right_ref
  73.9 1.2 add.18
  75.1 5.2 %all-to-all-start.2 = ((bf16[16,40,1152]{2,1,0:T(8,128)(2,1)}), bf16[16,40,1152]{2,1,0:T(8,128)(2,1)S(1)}, u32[]{:S(2)}, u32[]{:S(2)}) async-start(bf16[16,40,1152]{2,1,0:T(8,128)(2,1)} %bitcast.19), calls=%async_computation.2 | async-start | bytes 2949120 | tf_op jit(solution)/shard_map/all_to_all | solution.py:546
  80.4 14.4 %backward.1.after_ref = bf16[256,2304]{1,0:T(8,128)(2,1)} custom-call(s32[1,32]{1,0:T(1,128)S(1)} %copy-done.1, s32[1,4]{1,0:T(1,128)S(1)} %copy-done.2, s32[2]{0:T(128)S(1)} %pad_add_fusion.place_ref, bf16[256,2304]{1,0:T(8,128)(2,1)S(1)} %bitcast.15, f32[3,4,1152]{2,1,0:T(4,128)S(1)} %bitcast.18, bf16[256,1152]{1,0:T(8,128)(2,1)} %get-tuple-element.22.gdy_hbm, ...), custom_call_target="tpu_custom_call" | custom-call | flops 4076863488 | bytes 16777216 | tf_op jit(solution)/shard_map/backward/pallas_call | solution.py:388
  94.8 6.7 %all-to-all-done.2.terms_ref = bf16[16,40,1152]{2,1,0:T(8,128)(2,1)S(1)} async-done(((bf16[16,40,1152]{2,1,0:T(8,128)(2,1)}), bf16[16,40,1152]{2,1,0:T(8,128)(2,1)S(1)}, u32[]{:S(2)}, u32[]{:S(2)}) %all-to-all-start.2) | async-done | bytes 1474592 | tf_op jit(solution)/shard_map/all_to_all | solution.py:546
  101.5 0.2 sum.1
  101.7 2.0 %collective-permute-start.1 = (bf16[40,1152]{1,0:T(8,128)(2,1)S(1)}, bf16[40,1152]{1,0:T(8,128)(2,1)S(1)}, u32[]{:S(2)}, u32[]{:S(2)}) collective-permute-start(bf16[40,1152]{1,0:T(8,128)(2,1)S(1)} %convert_element_type.21), channel_id=1, source_target_pairs={{0,32},{32,0},{64,96},{96,64},{128,160},{160,128},{192,224},{224,1... | collective-permute-start | bytes 276488 | tf_op jit(solution)/shard_map/ppermute | solution.py:552
  103.7 7.2 %all-to-all-start.1 = ((bf16[32,8,2304]{2,1,0:T(8,128)(2,1)}), bf16[32,8,2304]{2,1,0:T(8,128)(2,1)S(1)}, u32[]{:S(2)}, u32[]{:S(2)}) async-start(bf16[32,8,2304]{2,1,0:T(8,128)(2,1)} %bitcast.21), calls=%async_computation.1 | async-start | bytes 2359296 | tf_op jit(solution)/shard_map/all_to_all | solution.py:535
  110.9 0.0 collective-permute-done.1
  111.0 3.4 %collective-permute-start.2 = (bf16[40,1152]{1,0:T(8,128)(2,1)S(1)}, bf16[40,1152]{1,0:T(8,128)(2,1)S(1)}, u32[]{:S(2)}, u32[]{:S(2)}) collective-permute-start(bf16[40,1152]{1,0:T(8,128)(2,1)S(1)} %add_convert_fusion.1), channel_id=1, source_target_pairs={{0,64},{32,96},{64,0},{96,32},{128,192},{160,224},{192,128},{224,1... | collective-permute-start | bytes 276488 | tf_op jit(solution)/shard_map/ppermute | solution.py:552
  114.3 4.5 %collective-permute-done.2 = bf16[40,1152]{1,0:T(8,128)(2,1)S(1)} collective-permute-done((bf16[40,1152]{1,0:T(8,128)(2,1)S(1)}, bf16[40,1152]{1,0:T(8,128)(2,1)S(1)}, u32[]{:S(2)}, u32[]{:S(2)}) %collective-permute-start.2) | collective-permute-done | bytes 92192 | tf_op jit(solution)/shard_map/ppermute | solution.py:552
  118.8 6.2 %collective-permute-start.3 = (bf16[40,1152]{1,0:T(8,128)(2,1)S(1)}, bf16[40,1152]{1,0:T(8,128)(2,1)S(1)}, u32[]{:S(2)}, u32[]{:S(2)}) collective-permute-start(bf16[40,1152]{1,0:T(8,128)(2,1)S(1)} %add_convert_fusion.left_ref), channel_id=1, source_target_pairs={{0,128},{32,160},{64,192},{96,224},{128,0},{160,32},{192,64},{224,... | collective-permute-start | bytes 276488 | tf_op jit(solution)/shard_map/ppermute | solution.py:552
  125.1 3.5 %all-to-all-done.1 = bf16[32,8,2304]{2,1,0:T(8,128)(2,1)S(1)} async-done(((bf16[32,8,2304]{2,1,0:T(8,128)(2,1)}), bf16[32,8,2304]{2,1,0:T(8,128)(2,1)S(1)}, u32[]{:S(2)}, u32[]{:S(2)}) %all-to-all-start.1) | async-done | bytes 1179680 | tf_op jit(solution)/shard_map/all_to_all | solution.py:535
  128.5 0.0 collective-permute-done.3.right_ref
  128.5 1.7 %finish.1 = (bf16[256,1152]{1,0:T(8,128)(2,1)}, bf16[256,1152]{1,0:T(8,128)(2,1)}, f32[36,1152]{1,0:T(8,128)}) custom-call(bf16[256,2304]{1,0:T(8,128)(2,1)S(1)} %bitcast.16, bf16[40,1152]{1,0:T(8,128)(2,1)S(1)} %add_convert_fusion.left_ref, bf16[40,1152]{1,0:T(8,128)(2,1)S(1)} %collective-permute-done.3.right_ref), custom_call_target="tpu_custom_call" | custom-call | bytes 4194304 | tf_op jit(solution)/shard_map/finish/pallas_call | solution.py:507
  (3 shorter events, 0.1 us)
Async XLA Ops:
  37.5 25.3 %copy-start = (f32[1,4,3,1152]{3,1,2,0:T(4,128)S(1)}, f32[1,4,3,1152]{3,1,2,0:T(4,128)}, u32[]{:S(2)}) copy-start(f32[1,4,3,1152]{3,1,2,0:T(4,128)} %param.11) | copy-start | bytes 165892
  37.5 25.3 %copy-start.1 = (s32[1,32]{1,0:T(1,128)S(1)}, s32[1,32]{1,0:T(1,128)}, u32[]{:S(2)}) copy-start(s32[1,32]{1,0:T(1,128)} %clip_ref.3) | copy-start | bytes 388
  37.5 25.3 %copy-start.2 = (s32[1,4]{1,0:T(1,128)S(1)}, s32[1,4]{1,0:T(1,128)}, u32[]{:S(2)}) copy-start(s32[1,4]{1,0:T(1,128)} %count_ref.3) | copy-start | bytes 52
  37.5 25.3 %all-to-all-start = ((bf16[32,8,2304]{2,1,0:T(8,128)(2,1)}), bf16[32,8,2304]{2,1,0:T(8,128)(2,1)S(1)}, u32[]{:S(2)}, u32[]{:S(2)}) async-start(bf16[32,8,2304]{2,1,0:T(8,128)(2,1)} %bitcast.22), calls=%async_computation | async-start | bytes 2359296 | tf_op jit(solution)/shard_map/all_to_all | solution.py:535
  70.5 3.4 %collective-permute-start = (bf16[640,1152]{1,0:T(8,128)(2,1)S(1)}, bf16[640,1152]{1,0:T(8,128)(2,1)S(1)}, u32[]{:S(2)}, u32[]{:S(2)}) collective-permute-start(bf16[640,1152]{1,0:T(8,128)(2,1)S(1)} %get-tuple-element.27), channel_id=1, source_target_pairs={{0,1},{1,0},{2,3},{3,2},{4,5},{5,4},{6,7},{7,6},{8,9},{9,8},{10,11... | collective-permute-start | bytes 4423688 | tf_op jit(solution)/shard_map/ppermute | solution.py:542
  75.1 26.4 %all-to-all-start.2 = ((bf16[16,40,1152]{2,1,0:T(8,128)(2,1)}), bf16[16,40,1152]{2,1,0:T(8,128)(2,1)S(1)}, u32[]{:S(2)}, u32[]{:S(2)}) async-start(bf16[16,40,1152]{2,1,0:T(8,128)(2,1)} %bitcast.19), calls=%async_computation.2 | async-start | bytes 2949120 | tf_op jit(solution)/shard_map/all_to_all | solution.py:546
  101.7 9.2 %collective-permute-start.1 = (bf16[40,1152]{1,0:T(8,128)(2,1)S(1)}, bf16[40,1152]{1,0:T(8,128)(2,1)S(1)}, u32[]{:S(2)}, u32[]{:S(2)}) collective-permute-start(bf16[40,1152]{1,0:T(8,128)(2,1)S(1)} %convert_element_type.21), channel_id=1, source_target_pairs={{0,32},{32,0},{64,96},{96,64},{128,160},{160,128},{192,224},{224,1... | collective-permute-start | bytes 276488 | tf_op jit(solution)/shard_map/ppermute | solution.py:552
  103.7 24.8 %all-to-all-start.1 = ((bf16[32,8,2304]{2,1,0:T(8,128)(2,1)}), bf16[32,8,2304]{2,1,0:T(8,128)(2,1)S(1)}, u32[]{:S(2)}, u32[]{:S(2)}) async-start(bf16[32,8,2304]{2,1,0:T(8,128)(2,1)} %bitcast.21), calls=%async_computation.1 | async-start | bytes 2359296 | tf_op jit(solution)/shard_map/all_to_all | solution.py:535
  111.0 7.9 %collective-permute-start.2 = (bf16[40,1152]{1,0:T(8,128)(2,1)S(1)}, bf16[40,1152]{1,0:T(8,128)(2,1)S(1)}, u32[]{:S(2)}, u32[]{:S(2)}) collective-permute-start(bf16[40,1152]{1,0:T(8,128)(2,1)S(1)} %add_convert_fusion.1), channel_id=1, source_target_pairs={{0,64},{32,96},{64,0},{96,32},{128,192},{160,224},{192,128},{224,1... | collective-permute-start | bytes 276488 | tf_op jit(solution)/shard_map/ppermute | solution.py:552
  118.8 9.7 %collective-permute-start.3 = (bf16[40,1152]{1,0:T(8,128)(2,1)S(1)}, bf16[40,1152]{1,0:T(8,128)(2,1)S(1)}, u32[]{:S(2)}, u32[]{:S(2)}) collective-permute-start(bf16[40,1152]{1,0:T(8,128)(2,1)S(1)} %add_convert_fusion.left_ref), channel_id=1, source_target_pairs={{0,128},{32,160},{64,192},{96,224},{128,0},{160,32},{192,64},{224,... | collective-permute-start | bytes 276488 | tf_op jit(solution)/shard_map/ppermute | solution.py:552

commit v8 on v7

--- a/solution.py
+++ b/solution.py
@@ -8,6 +8,7 @@
 HEADS = 16
 LANES = 128
 EDGES = (0, 512, 1152)
+PARTS = 2
 SHARE_ROWS = 40
 MIB = 1024 * 1024
 
@@ -410,26 +411,45 @@
     )
 
 
-def pack_kernel(latent_hbm, cotangent_hbm, out_hbm, sems):
-    model = latent_hbm.shape[1]
-    copies = [
-        pltpu.make_async_copy(latent_hbm, out_hbm.at[:, :model], sems.at[0]),
-        pltpu.make_async_copy(cotangent_hbm, out_hbm.at[:, model:], sems.at[1]),
-    ]
-    for copy in copies:
-        copy.start()
-    for copy in copies:
-        copy.wait()
+def pack_kernel(latent_hbm, cotangent_hbm, out_hbm, both_ref, load_sems, store_sems):
+    rows, model = latent_hbm.shape
+    parts = store_sems.shape[0]
+    spans = [slice(part * rows // parts, (part + 1) * rows // parts) for part in range(parts)]
+    loads = []
+    for part, where in enumerate(spans):
+        for side, source in enumerate((latent_hbm, cotangent_hbm)):
+            columns = slice(side * model, (side + 1) * model)
+            load = pltpu.make_async_copy(
+                source.at[where, :], both_ref.at[where, columns], load_sems.at[part, side]
+            )
+            load.start()
+            loads.append(load)
+    stores = []
+    for part, where in enumerate(spans):
+        loads[2 * part].wait()
+        loads[2 * part + 1].wait()
+        store = pltpu.make_async_copy(
+            both_ref.at[where, :], out_hbm.at[where, :], store_sems.at[part]
+        )
+        store.start()
+        stores.append(store)
+    for store in stores:
+        store.wait()
 
 
 def run_pack(latents, cotangent):
     rows, model = latents.shape
+    size = (rows, 2 * model)
     return pl.pallas_call(
         pack_kernel,
-        out_shape=pltpu.HBM((rows, 2 * model), latents.dtype),
+        out_shape=pltpu.HBM(size, latents.dtype),
         in_specs=[hbm()] * 2,
         out_specs=hbm(),
-        scratch_shapes=[pltpu.SemaphoreType.DMA((2,))],
+        scratch_shapes=[
+            pltpu.VMEM(size, latents.dtype),
+            pltpu.SemaphoreType.DMA((PARTS, 2)),
+            pltpu.SemaphoreType.DMA((PARTS,)),
+        ],
         compiler_params=pltpu.CompilerParams(vmem_limit_bytes=12 * MIB),
         name="pack",
     )(in_hbm(latents), in_hbm(cotangent))
@@ -487,18 +507,12 @@
     )(terms, in_hbm(after))
 
 
-def finish_kernel(returned_ref, left_ref, right_ref, block_hbm, latent_hbm, grad_ref, sems):
-    model = block_hbm.shape[1]
-    copies = [
-        pltpu.make_async_copy(returned_ref.at[:, :model], block_hbm, sems.at[0]),
-        pltpu.make_async_copy(returned_ref.at[:, model:], latent_hbm, sems.at[1]),
-    ]
-    for copy in copies:
-        copy.start()
+def finish_kernel(returned_ref, left_ref, right_ref, block_ref, latent_ref, grad_ref):
+    model = block_ref.shape[1]
+    block_ref[...] = returned_ref[:, :model]
+    latent_ref[...] = returned_ref[:, model:]
     total = left_ref[...].astype(jnp.float32) + right_ref[...].astype(jnp.float32)
     grad_ref[...] = total[: grad_ref.shape[0]]
-    for copy in copies:
-        copy.wait()
 
 
 def run_finish(returned, left, right, share):
@@ -507,13 +521,12 @@
     return pl.pallas_call(
         finish_kernel,
         out_shape=(
-            pltpu.HBM((rows, model), low),
-            pltpu.HBM((rows, model), low),
+            jax.ShapeDtypeStruct((rows, model), low),
+            jax.ShapeDtypeStruct((rows, model), low),
             jax.ShapeDtypeStruct((share, model), jnp.float32),
         ),
         in_specs=[vmem()] * 3,
-        out_specs=(hbm(), hbm(), vmem()),
-        scratch_shapes=[pltpu.SemaphoreType.DMA((2,))],
+        out_specs=(vmem(),) * 3,
         compiler_params=pltpu.CompilerParams(vmem_limit_bytes=12 * MIB),
         cost_estimate=pl.CostEstimate(flops=0, bytes_accessed=4 * MIB, transcendentals=0),
         name="finish",

time: 132 us -> 96.6 us (0.73)
  Pallas kernels: 65 us -> 29.7 us
    pallas_call x2, Pallas kernels: 38.6 us -> 3.29 us  [the longest x1 2.14 us: run_pack(): pl.pallas_call(pack_kernel, out_shape=pltpu.HBM(size, latents.dtype), in_...]
  transfers between devices with their start and end apart: 7 -> 7, of which waited for: 5 -> 5; matrix products, arithmetic and copies ran while one was open for 0% -> 0% of each run, Pallas kernels for 13% -> 18%
where the time goes in v8:
time: 96.6 us; the launch traced here: 95 us
  waiting for transfers between devices  32.3 us (33%)
  starting transfers between devices  32 us (33%)
  Pallas kernels  29.7 us (31%)
    all_to_all x2, waiting for transfers between devices, exchange(): return lax.all_to_all(pieces, 'seq', 0, 0, tiled=True).reshape(rows.shape)  20.9 us
    all_to_all x2, starting transfers between devices, exchange(): return lax.all_to_all(pieces, 'seq', 0, 0, tiled=True).reshape(rows.shape)  15 us
    pallas_call x1, Pallas kernels, run_backward(): pl.pallas_call(backward_kernel, out_shape=pltpu.HBM(tokens.shape, low), i...  14.4 us
    ppermute x3, starting transfers between devices, per_device(): met = lax.ppermute(total, 'dp', [(i, i ^ stride) for i in range(groups)])  11.6 us
    pallas_call x1, Pallas kernels, run_forward(): pl.pallas_call(forward_kernel, out_shape=tuple((pltpu.VMEM(size, low) for...  7.7 us
    all_to_all x1, waiting for transfers between devices, per_device(): lax.all_to_all(pair, 'seq', 0, 0, tiled=True, axis_index_groups=same_core)  6.68 us
    all_to_all x1, starting transfers between devices, per_device(): lax.all_to_all(pair, 'seq', 0, 0, tiled=True, axis_index_groups=same_core)  5.24 us
    ppermute x3, waiting for transfers between devices, per_device(): met = lax.ppermute(total, 'dp', [(i, i ^ stride) for i in range(groups)])  4.5 us
  transfers between devices with their start and end apart: 7, of which 5 were waited for; matrix products, arithmetic and copies ran while one was open for 0% of the time, Pallas kernels for 18%

profile of v8, /device:TPU:2, one launch (start us, length us, event | category | flops | bytes accessed | tf_op | source)
XLA Modules:
  0.0 95.0 jit_solution(15330029571244113050)
XLA Ops:
  0.6 2.1 %pack.1 = bf16[256,2304]{1,0:T(8,128)(2,1)} custom-call(bf16[256,1152]{1,0:T(8,128)(2,1)} %bitcast.23, bf16[256,1152]{1,0:T(8,128)(2,1)} %bitcast.24), custom_call_target="tpu_custom_call" | custom-call | tf_op jit(solution)/shard_map/pack/pallas_call | solution.py:443
  2.8 0.0 copy-start
  2.8 0.0 copy-start.1
  2.8 0.0 copy-start.2
  2.8 7.8 %all-to-all-start = ((bf16[32,8,2304]{2,1,0:T(8,128)(2,1)}), bf16[32,8,2304]{2,1,0:T(8,128)(2,1)S(1)}, u32[]{:S(2)}, u32[]{:S(2)}) async-start(bf16[32,8,2304]{2,1,0:T(8,128)(2,1)} %bitcast.22), calls=%async_computation | async-start | bytes 2359296 | tf_op jit(solution)/shard_map/all_to_all | solution.py:548
  10.6 0.1 pad_add_fusion.place_ref
  10.7 17.4 %all-to-all-done = bf16[32,8,2304]{2,1,0:T(8,128)(2,1)S(1)} async-done(((bf16[32,8,2304]{2,1,0:T(8,128)(2,1)}), bf16[32,8,2304]{2,1,0:T(8,128)(2,1)S(1)}, u32[]{:S(2)}, u32[]{:S(2)}) %all-to-all-start) | async-done | bytes 1179680 | tf_op jit(solution)/shard_map/all_to_all | solution.py:548
  28.1 0.0 copy-done
  28.1 0.0 copy-done.1
  28.1 0.0 copy-done.2
  28.1 7.7 %forward.1 = (bf16[256,3456]{1,0:T(8,128)(2,1)S(1)}, bf16[16,256,256]{2,1,0:T(8,128)(2,1)S(1)}, bf16[256,1152]{1,0:T(8,128)(2,1)S(1)}, bf16[256,1152]{1,0:T(8,12...) custom-call(s32[1,32]{1,0:T(1,128)S(1)} %copy-done.1, s32[1,4]{1,0:T(1,128)S(1)} %copy-done.2, ...), custom_call_target="tpu_custom_call" | custom-call | flops 2717908992 | bytes 12582912 | tf_op jit(solution)/shard_map/forward/pallas_call | solution.py:366
  35.8 0.2 collective-permute-start
  36.1 2.9 %keep.1 = (bf16[640,1152]{1,0:T(8,128)(2,1)S(1)}, bf16[256,3456]{1,0:T(8,128)(2,1)}, bf16[16,256,256]{2,1,0:T(8,128)(2,1)}, bf16[256,1152]{1,0:T(8,128)(2,1)}, bf16[256,1152]{1,0:T(8,128)(2,1)}) custom-call(s32[2]{0:T(128)S(1)} %pad_add_fusion.place_ref, bf16[2,640,256]{2,1,0:T(8,128)(2,1)S(1)} %get-tuple-element.17.share_ref, ...), custom_call_target="tpu_custom_call" | custom-call | flops 377487360 | bytes 6291456 | tf_op jit(solution)/shard_map/keep/pallas_call | solution.py:214
  38.9 0.3 collective-permute-done.right_ref
  39.2 1.2 %add.18 = bf16[640,1152]{1,0:T(8,128)(2,1)} custom-call(bf16[640,1152]{1,0:T(8,128)(2,1)S(1)} %get-tuple-element.26.left_ref, bf16[640,1152]{1,0:T(8,128)(2,1)S(1)} %collective-permute-done.right_ref), custom_call_target="tpu_custom_call" | custom-call | tf_op jit(solution)/shard_map/add/pallas_call | solution.py:477
  40.4 5.2 %all-to-all-start.2 = ((bf16[16,40,1152]{2,1,0:T(8,128)(2,1)}), bf16[16,40,1152]{2,1,0:T(8,128)(2,1)S(1)}, u32[]{:S(2)}, u32[]{:S(2)}) async-start(bf16[16,40,1152]{2,1,0:T(8,128)(2,1)} %bitcast.19), calls=%async_computation.2 | async-start | bytes 2949120 | tf_op jit(solution)/shard_map/all_to_all | solution.py:559
  45.6 14.4 %backward.1.after_ref = bf16[256,2304]{1,0:T(8,128)(2,1)} custom-call(s32[1,32]{1,0:T(1,128)S(1)} %copy-done.1, s32[1,4]{1,0:T(1,128)S(1)} %copy-done.2, s32[2]{0:T(128)S(1)} %pad_add_fusion.place_ref, bf16[256,2304]{1,0:T(8,128)(2,1)S(1)} %bitcast.15, f32[3,4,1152]{2,1,0:T(4,128)S(1)} %bitcast.18, bf16[256,1152]{1,0:T(8,128)(2,1)} %get-tuple-element.22.gdy_hbm, ...), custom_call_target="tpu_custom_call" | custom-call | flops 4076863488 | bytes 16777216 | tf_op jit(solution)/shard_map/backward/pallas_call | solution.py:389
  60.1 6.7 %all-to-all-done.2.terms_ref = bf16[16,40,1152]{2,1,0:T(8,128)(2,1)S(1)} async-done(((bf16[16,40,1152]{2,1,0:T(8,128)(2,1)}), bf16[16,40,1152]{2,1,0:T(8,128)(2,1)S(1)}, u32[]{:S(2)}, u32[]{:S(2)}) %all-to-all-start.2) | async-done | bytes 1474592 | tf_op jit(solution)/shard_map/all_to_all | solution.py:559
  66.8 0.2 sum.1
  67.0 2.0 %collective-permute-start.1 = (bf16[40,1152]{1,0:T(8,128)(2,1)S(1)}, bf16[40,1152]{1,0:T(8,128)(2,1)S(1)}, u32[]{:S(2)}, u32[]{:S(2)}) collective-permute-start(bf16[40,1152]{1,0:T(8,128)(2,1)S(1)} %convert_element_type.21), channel_id=1, source_target_pairs={{0,32},{32,0},{64,96},{96,64},{128,160},{160,128},{192,224},{224,1... | collective-permute-start | bytes 276488 | tf_op jit(solution)/shard_map/ppermute | solution.py:565
  69.0 7.2 %all-to-all-start.1 = ((bf16[32,8,2304]{2,1,0:T(8,128)(2,1)}), bf16[32,8,2304]{2,1,0:T(8,128)(2,1)S(1)}, u32[]{:S(2)}, u32[]{:S(2)}) async-start(bf16[32,8,2304]{2,1,0:T(8,128)(2,1)} %bitcast.21), calls=%async_computation.1 | async-start | bytes 2359296 | tf_op jit(solution)/shard_map/all_to_all | solution.py:548
  76.2 0.0 collective-permute-done.1
  76.2 3.4 %collective-permute-start.2 = (bf16[40,1152]{1,0:T(8,128)(2,1)S(1)}, bf16[40,1152]{1,0:T(8,128)(2,1)S(1)}, u32[]{:S(2)}, u32[]{:S(2)}) collective-permute-start(bf16[40,1152]{1,0:T(8,128)(2,1)S(1)} %add_convert_fusion.1), channel_id=1, source_target_pairs={{0,64},{32,96},{64,0},{96,32},{128,192},{160,224},{192,128},{224,1... | collective-permute-start | bytes 276488 | tf_op jit(solution)/shard_map/ppermute | solution.py:565
  79.6 4.5 %collective-permute-done.2 = bf16[40,1152]{1,0:T(8,128)(2,1)S(1)} collective-permute-done((bf16[40,1152]{1,0:T(8,128)(2,1)S(1)}, bf16[40,1152]{1,0:T(8,128)(2,1)S(1)}, u32[]{:S(2)}, u32[]{:S(2)}) %collective-permute-start.2) | collective-permute-done | bytes 92192 | tf_op jit(solution)/shard_map/ppermute | solution.py:565
  84.1 6.2 %collective-permute-start.3 = (bf16[40,1152]{1,0:T(8,128)(2,1)S(1)}, bf16[40,1152]{1,0:T(8,128)(2,1)S(1)}, u32[]{:S(2)}, u32[]{:S(2)}) collective-permute-start(bf16[40,1152]{1,0:T(8,128)(2,1)S(1)} %add_convert_fusion.left_ref), channel_id=1, source_target_pairs={{0,128},{32,160},{64,192},{96,224},{128,0},{160,32},{192,64},{224,... | collective-permute-start | bytes 276488 | tf_op jit(solution)/shard_map/ppermute | solution.py:565
  90.4 3.5 %all-to-all-done.1 = bf16[32,8,2304]{2,1,0:T(8,128)(2,1)S(1)} async-done(((bf16[32,8,2304]{2,1,0:T(8,128)(2,1)}), bf16[32,8,2304]{2,1,0:T(8,128)(2,1)S(1)}, u32[]{:S(2)}, u32[]{:S(2)}) %all-to-all-start.1) | async-done | bytes 1179680 | tf_op jit(solution)/shard_map/all_to_all | solution.py:548
  93.8 0.0 collective-permute-done.3.right_ref
  93.8 1.2 %finish.1 = (bf16[256,1152]{1,0:T(8,128)(2,1)}, bf16[256,1152]{1,0:T(8,128)(2,1)}, f32[36,1152]{1,0:T(8,128)}) custom-call(bf16[256,2304]{1,0:T(8,128)(2,1)S(1)} %bitcast.16, bf16[40,1152]{1,0:T(8,128)(2,1)S(1)} %add_convert_fusion.left_ref, bf16[40,1152]{1,0:T(8,128)(2,1)S(1)} %collective-permute-done.3.right_ref), custom_call_target="tpu_custom_call" | custom-call | bytes 4194304 | tf_op jit(solution)/shard_map/finish/pallas_call | solution.py:521
  (3 shorter events, 0.1 us)
Async XLA Ops:
  2.8 25.3 %copy-start = (f32[1,4,3,1152]{3,1,2,0:T(4,128)S(1)}, f32[1,4,3,1152]{3,1,2,0:T(4,128)}, u32[]{:S(2)}) copy-start(f32[1,4,3,1152]{3,1,2,0:T(4,128)} %param.11) | copy-start | bytes 165892
  2.8 25.3 %copy-start.1 = (s32[1,32]{1,0:T(1,128)S(1)}, s32[1,32]{1,0:T(1,128)}, u32[]{:S(2)}) copy-start(s32[1,32]{1,0:T(1,128)} %clip_ref.3) | copy-start | bytes 388
  2.8 25.3 %copy-start.2 = (s32[1,4]{1,0:T(1,128)S(1)}, s32[1,4]{1,0:T(1,128)}, u32[]{:S(2)}) copy-start(s32[1,4]{1,0:T(1,128)} %count_ref.3) | copy-start | bytes 52
  2.8 25.3 %all-to-all-start = ((bf16[32,8,2304]{2,1,0:T(8,128)(2,1)}), bf16[32,8,2304]{2,1,0:T(8,128)(2,1)S(1)}, u32[]{:S(2)}, u32[]{:S(2)}) async-start(bf16[32,8,2304]{2,1,0:T(8,128)(2,1)} %bitcast.22), calls=%async_computation | async-start | bytes 2359296 | tf_op jit(solution)/shard_map/all_to_all | solution.py:548
  35.8 3.4 %collective-permute-start = (bf16[640,1152]{1,0:T(8,128)(2,1)S(1)}, bf16[640,1152]{1,0:T(8,128)(2,1)S(1)}, u32[]{:S(2)}, u32[]{:S(2)}) collective-permute-start(bf16[640,1152]{1,0:T(8,128)(2,1)S(1)} %get-tuple-element.27), channel_id=1, source_target_pairs={{0,1},{1,0},{2,3},{3,2},{4,5},{5,4},{6,7},{7,6},{8,9},{9,8},{10,11... | collective-permute-start | bytes 4423688 | tf_op jit(solution)/shard_map/ppermute | solution.py:555
  40.4 26.4 %all-to-all-start.2 = ((bf16[16,40,1152]{2,1,0:T(8,128)(2,1)}), bf16[16,40,1152]{2,1,0:T(8,128)(2,1)S(1)}, u32[]{:S(2)}, u32[]{:S(2)}) async-start(bf16[16,40,1152]{2,1,0:T(8,128)(2,1)} %bitcast.19), calls=%async_computation.2 | async-start | bytes 2949120 | tf_op jit(solution)/shard_map/all_to_all | solution.py:559
  67.0 9.2 %collective-permute-start.1 = (bf16[40,1152]{1,0:T(8,128)(2,1)S(1)}, bf16[40,1152]{1,0:T(8,128)(2,1)S(1)}, u32[]{:S(2)}, u32[]{:S(2)}) collective-permute-start(bf16[40,1152]{1,0:T(8,128)(2,1)S(1)} %convert_element_type.21), channel_id=1, source_target_pairs={{0,32},{32,0},{64,96},{96,64},{128,160},{160,128},{192,224},{224,1... | collective-permute-start | bytes 276488 | tf_op jit(solution)/shard_map/ppermute | solution.py:565
  69.0 24.8 %all-to-all-start.1 = ((bf16[32,8,2304]{2,1,0:T(8,128)(2,1)}), bf16[32,8,2304]{2,1,0:T(8,128)(2,1)S(1)}, u32[]{:S(2)}, u32[]{:S(2)}) async-start(bf16[32,8,2304]{2,1,0:T(8,128)(2,1)} %bitcast.21), calls=%async_computation.1 | async-start | bytes 2359296 | tf_op jit(solution)/shard_map/all_to_all | solution.py:548
  76.2 7.9 %collective-permute-start.2 = (bf16[40,1152]{1,0:T(8,128)(2,1)S(1)}, bf16[40,1152]{1,0:T(8,128)(2,1)S(1)}, u32[]{:S(2)}, u32[]{:S(2)}) collective-permute-start(bf16[40,1152]{1,0:T(8,128)(2,1)S(1)} %add_convert_fusion.1), channel_id=1, source_target_pairs={{0,64},{32,96},{64,0},{96,32},{128,192},{160,224},{192,128},{224,1... | collective-permute-start | bytes 276488 | tf_op jit(solution)/shard_map/ppermute | solution.py:565
  84.1 9.7 %collective-permute-start.3 = (bf16[40,1152]{1,0:T(8,128)(2,1)S(1)}, bf16[40,1152]{1,0:T(8,128)(2,1)S(1)}, u32[]{:S(2)}, u32[]{:S(2)}) collective-permute-start(bf16[40,1152]{1,0:T(8,128)(2,1)S(1)} %add_convert_fusion.left_ref), channel_id=1, source_target_pairs={{0,128},{32,160},{64,192},{96,224},{128,0},{160,32},{192,64},{224,... | collective-permute-start | bytes 276488 | tf_op jit(solution)/shard_map/ppermute | solution.py:565

commit v9 on v8

--- a/solution.py
+++ b/solution.py
@@ -560,13 +560,11 @@
     saved = (gdy, out_weight, att, qkv, prob, qkv_weight)
     results = run_backward(frame_clip, clip_patches, place, tokens, mod, saved, pair)
     total = run_sum(terms, results).astype(jnp.bfloat16)
-    stride = 1
-    while True:
+    strides = [groups // 2] + [1 << bit for bit in range(groups.bit_length() - 2)]
+    for stride in strides[:-1]:
         met = lax.ppermute(total, "dp", [(i, i ^ stride) for i in range(groups)])
-        stride *= 2
-        if stride >= groups:
-            break
         total = (total.astype(jnp.float32) + met.astype(jnp.float32)).astype(jnp.bfloat16)
+    met = lax.ppermute(total, "dp", [(i, i ^ strides[-1]) for i in range(groups)])
     returned = exchange(results)
     block_out, latent_grad, grad = run_finish(returned, total, met, share)
     return block_out.reshape(latents.shape), latent_grad.reshape(latents.shape), grad

time: 96.6 us -> 102 us (1.056)
  waiting for transfers between devices: 32.3 us -> 39.3 us
  starting transfers between devices: 32 us -> 30.4 us
    all_to_all x2, waiting for transfers between devices: 20.9 us -> 28.6 us  [exchange(): return lax.all_to_all(pieces, 'seq', 0, 0, tiled=True).reshape(rows.shape)]
    ppermute x3 -> x2, starting transfers between devices: 11.6 us -> 8.38 us  [per_device(): met = lax.ppermute(total, 'dp', [(i, i ^ stride) for i in range(groups)])]
    ppermute x0 -> x1, starting transfers between devices: none -> 1.56 us  [per_device(): lax.ppermute(total, 'dp', [(i, i ^ strides[-1]) for i in range(groups)])]
    ppermute x3 -> x2, waiting for transfers between devices: 4.5 us -> 3.7 us  [per_device(): met = lax.ppermute(total, 'dp', [(i, i ^ stride) for i in range(groups)])]
  transfers between devices with their start and end apart: 7 -> 7, of which waited for: 5 -> 5; matrix products, arithmetic and copies ran while one was open for 0% -> 0% of each run, Pallas kernels for 18% -> 17%
where the time goes in v9:
time: 102 us; the launch traced here: 100 us
  waiting for transfers between devices  39.3 us (39%)
  starting transfers between devices  30.4 us (30%)
  Pallas kernels  29.7 us (29%)
    all_to_all x2, waiting for transfers between devices, exchange(): return lax.all_to_all(pieces, 'seq', 0, 0, tiled=True).reshape(rows.shape)  28.6 us
    all_to_all x2, starting transfers between devices, exchange(): return lax.all_to_all(pieces, 'seq', 0, 0, tiled=True).reshape(rows.shape)  15 us
    pallas_call x1, Pallas kernels, run_backward(): pl.pallas_call(backward_kernel, out_shape=pltpu.HBM(tokens.shape, low), i...  14.4 us
    ppermute x2, starting transfers between devices, per_device(): met = lax.ppermute(total, 'dp', [(i, i ^ stride) for i in range(groups)])  8.38 us
    pallas_call x1, Pallas kernels, run_forward(): pl.pallas_call(forward_kernel, out_shape=tuple((pltpu.VMEM(size, low) for...  7.7 us
    all_to_all x1, waiting for transfers between devices, per_device(): lax.all_to_all(pair, 'seq', 0, 0, tiled=True, axis_index_groups=same_core)  6.68 us
    all_to_all x1, starting transfers between devices, per_device(): lax.all_to_all(pair, 'seq', 0, 0, tiled=True, axis_index_groups=same_core)  5.24 us
    ppermute x2, waiting for transfers between devices, per_device(): met = lax.ppermute(total, 'dp', [(i, i ^ stride) for i in range(groups)])  3.7 us
  transfers between devices with their start and end apart: 7, of which 5 were waited for; matrix products, arithmetic and copies ran while one was open for 0% of the time, Pallas kernels for 17%

profile of v9, /device:TPU:2, one launch (start us, length us, event | category | flops | bytes accessed | tf_op | source)
XLA Modules:
  0.0 100.3 jit_solution(14708848367594696279)
XLA Ops:
  0.6 2.1 %pack.1 = bf16[256,2304]{1,0:T(8,128)(2,1)} custom-call(bf16[256,1152]{1,0:T(8,128)(2,1)} %bitcast.23, bf16[256,1152]{1,0:T(8,128)(2,1)} %bitcast.24), custom_call_target="tpu_custom_call" | custom-call | tf_op jit(solution)/shard_map/pack/pallas_call | solution.py:443
  2.8 0.0 copy-start
  2.8 0.0 copy-start.1
  2.8 0.0 copy-start.2
  2.8 7.8 %all-to-all-start = ((bf16[32,8,2304]{2,1,0:T(8,128)(2,1)}), bf16[32,8,2304]{2,1,0:T(8,128)(2,1)S(1)}, u32[]{:S(2)}, u32[]{:S(2)}) async-start(bf16[32,8,2304]{2,1,0:T(8,128)(2,1)} %bitcast.22), calls=%async_computation | async-start | bytes 2359296 | tf_op jit(solution)/shard_map/all_to_all | solution.py:548
  10.6 0.1 pad_add_fusion.place_ref
  10.7 17.4 %all-to-all-done = bf16[32,8,2304]{2,1,0:T(8,128)(2,1)S(1)} async-done(((bf16[32,8,2304]{2,1,0:T(8,128)(2,1)}), bf16[32,8,2304]{2,1,0:T(8,128)(2,1)S(1)}, u32[]{:S(2)}, u32[]{:S(2)}) %all-to-all-start) | async-done | bytes 1179680 | tf_op jit(solution)/shard_map/all_to_all | solution.py:548
  28.1 0.0 copy-done
  28.1 0.0 copy-done.1
  28.1 0.0 copy-done.2
  28.1 7.7 %forward.1 = (bf16[256,3456]{1,0:T(8,128)(2,1)S(1)}, bf16[16,256,256]{2,1,0:T(8,128)(2,1)S(1)}, bf16[256,1152]{1,0:T(8,128)(2,1)S(1)}, bf16[256,1152]{1,0:T(8,12...) custom-call(s32[1,32]{1,0:T(1,128)S(1)} %copy-done.1, s32[1,4]{1,0:T(1,128)S(1)} %copy-done.2, ...), custom_call_target="tpu_custom_call" | custom-call | flops 2717908992 | bytes 12582912 | tf_op jit(solution)/shard_map/forward/pallas_call | solution.py:366
  35.8 0.2 collective-permute-start
  36.1 2.9 %keep.1 = (bf16[640,1152]{1,0:T(8,128)(2,1)S(1)}, bf16[256,3456]{1,0:T(8,128)(2,1)}, bf16[16,256,256]{2,1,0:T(8,128)(2,1)}, bf16[256,1152]{1,0:T(8,128)(2,1)}, bf16[256,1152]{1,0:T(8,128)(2,1)}) custom-call(s32[2]{0:T(128)S(1)} %pad_add_fusion.place_ref, bf16[2,640,256]{2,1,0:T(8,128)(2,1)S(1)} %get-tuple-element.17.share_ref, ...), custom_call_target="tpu_custom_call" | custom-call | flops 377487360 | bytes 6291456 | tf_op jit(solution)/shard_map/keep/pallas_call | solution.py:214
  38.9 0.3 collective-permute-done.right_ref
  39.2 1.2 %add.18 = bf16[640,1152]{1,0:T(8,128)(2,1)} custom-call(bf16[640,1152]{1,0:T(8,128)(2,1)S(1)} %get-tuple-element.26.left_ref, bf16[640,1152]{1,0:T(8,128)(2,1)S(1)} %collective-permute-done.right_ref), custom_call_target="tpu_custom_call" | custom-call | tf_op jit(solution)/shard_map/add/pallas_call | solution.py:477
  40.4 5.2 %all-to-all-start.2 = ((bf16[16,40,1152]{2,1,0:T(8,128)(2,1)}), bf16[16,40,1152]{2,1,0:T(8,128)(2,1)S(1)}, u32[]{:S(2)}, u32[]{:S(2)}) async-start(bf16[16,40,1152]{2,1,0:T(8,128)(2,1)} %bitcast.19), calls=%async_computation.2 | async-start | bytes 2949120 | tf_op jit(solution)/shard_map/all_to_all | solution.py:559
  45.6 14.4 %backward.1.after_ref = bf16[256,2304]{1,0:T(8,128)(2,1)} custom-call(s32[1,32]{1,0:T(1,128)S(1)} %copy-done.1, s32[1,4]{1,0:T(1,128)S(1)} %copy-done.2, s32[2]{0:T(128)S(1)} %pad_add_fusion.place_ref, bf16[256,2304]{1,0:T(8,128)(2,1)S(1)} %bitcast.15, f32[3,4,1152]{2,1,0:T(4,128)S(1)} %bitcast.18, bf16[256,1152]{1,0:T(8,128)(2,1)} %get-tuple-element.22.gdy_hbm, ...), custom_call_target="tpu_custom_call" | custom-call | flops 4076863488 | bytes 16777216 | tf_op jit(solution)/shard_map/backward/pallas_call | solution.py:389
  60.1 6.7 %all-to-all-done.2.terms_ref = bf16[16,40,1152]{2,1,0:T(8,128)(2,1)S(1)} async-done(((bf16[16,40,1152]{2,1,0:T(8,128)(2,1)}), bf16[16,40,1152]{2,1,0:T(8,128)(2,1)S(1)}, u32[]{:S(2)}, u32[]{:S(2)}) %all-to-all-start.2) | async-done | bytes 1474592 | tf_op jit(solution)/shard_map/all_to_all | solution.py:559
  66.8 0.2 sum.1
  67.0 7.3 %collective-permute-start.1 = (bf16[40,1152]{1,0:T(8,128)(2,1)S(1)}, bf16[40,1152]{1,0:T(8,128)(2,1)S(1)}, u32[]{:S(2)}, u32[]{:S(2)}) collective-permute-start(bf16[40,1152]{1,0:T(8,128)(2,1)S(1)} %convert_element_type.21), channel_id=1, source_target_pairs={{0,128},{32,160},{64,192},{96,224},{128,0},{160,32},{192,64},{224,... | collective-permute-start | bytes 276488 | tf_op jit(solution)/shard_map/ppermute | solution.py:565
  74.3 7.2 %all-to-all-start.1 = ((bf16[32,8,2304]{2,1,0:T(8,128)(2,1)}), bf16[32,8,2304]{2,1,0:T(8,128)(2,1)S(1)}, u32[]{:S(2)}, u32[]{:S(2)}) async-start(bf16[32,8,2304]{2,1,0:T(8,128)(2,1)} %bitcast.21), calls=%async_computation.1 | async-start | bytes 2359296 | tf_op jit(solution)/shard_map/all_to_all | solution.py:548
  81.5 0.0 collective-permute-done.1
  81.5 1.1 %collective-permute-start.2 = (bf16[40,1152]{1,0:T(8,128)(2,1)S(1)}, bf16[40,1152]{1,0:T(8,128)(2,1)S(1)}, u32[]{:S(2)}, u32[]{:S(2)}) collective-permute-start(bf16[40,1152]{1,0:T(8,128)(2,1)S(1)} %add_convert_fusion.1), channel_id=1, source_target_pairs={{0,32},{32,0},{64,96},{96,64},{128,160},{160,128},{192,224},{224,1... | collective-permute-start | bytes 276488 | tf_op jit(solution)/shard_map/ppermute | solution.py:565
  82.6 3.7 %collective-permute-done.2 = bf16[40,1152]{1,0:T(8,128)(2,1)S(1)} collective-permute-done((bf16[40,1152]{1,0:T(8,128)(2,1)S(1)}, bf16[40,1152]{1,0:T(8,128)(2,1)S(1)}, u32[]{:S(2)}, u32[]{:S(2)}) %collective-permute-start.2) | collective-permute-done | bytes 92192 | tf_op jit(solution)/shard_map/ppermute | solution.py:565
  86.3 1.6 %collective-permute-start.3 = (bf16[40,1152]{1,0:T(8,128)(2,1)S(1)}, bf16[40,1152]{1,0:T(8,128)(2,1)S(1)}, u32[]{:S(2)}, u32[]{:S(2)}) collective-permute-start(bf16[40,1152]{1,0:T(8,128)(2,1)S(1)} %add_convert_fusion.left_ref), channel_id=1, source_target_pairs={{0,64},{32,96},{64,0},{96,32},{128,192},{160,224},{192,128},{224,1... | collective-permute-start | bytes 276488 | tf_op jit(solution)/shard_map/ppermute | solution.py:567
  87.9 11.2 %all-to-all-done.1 = bf16[32,8,2304]{2,1,0:T(8,128)(2,1)S(1)} async-done(((bf16[32,8,2304]{2,1,0:T(8,128)(2,1)}), bf16[32,8,2304]{2,1,0:T(8,128)(2,1)S(1)}, u32[]{:S(2)}, u32[]{:S(2)}) %all-to-all-start.1) | async-done | bytes 1179680 | tf_op jit(solution)/shard_map/all_to_all | solution.py:548
  99.1 0.0 collective-permute-done.3.right_ref
  99.1 1.2 %finish.1 = (bf16[256,1152]{1,0:T(8,128)(2,1)}, bf16[256,1152]{1,0:T(8,128)(2,1)}, f32[36,1152]{1,0:T(8,128)}) custom-call(bf16[256,2304]{1,0:T(8,128)(2,1)S(1)} %bitcast.16, bf16[40,1152]{1,0:T(8,128)(2,1)S(1)} %add_convert_fusion.left_ref, bf16[40,1152]{1,0:T(8,128)(2,1)S(1)} %collective-permute-done.3.right_ref), custom_call_target="tpu_custom_call" | custom-call | bytes 4194304 | tf_op jit(solution)/shard_map/finish/pallas_call | solution.py:521
  (3 shorter events, 0.1 us)
Async XLA Ops:
  2.8 25.3 %copy-start = (f32[1,4,3,1152]{3,1,2,0:T(4,128)S(1)}, f32[1,4,3,1152]{3,1,2,0:T(4,128)}, u32[]{:S(2)}) copy-start(f32[1,4,3,1152]{3,1,2,0:T(4,128)} %param.11) | copy-start | bytes 165892
  2.8 25.3 %copy-start.1 = (s32[1,32]{1,0:T(1,128)S(1)}, s32[1,32]{1,0:T(1,128)}, u32[]{:S(2)}) copy-start(s32[1,32]{1,0:T(1,128)} %clip_ref.3) | copy-start | bytes 388
  2.8 25.3 %copy-start.2 = (s32[1,4]{1,0:T(1,128)S(1)}, s32[1,4]{1,0:T(1,128)}, u32[]{:S(2)}) copy-start(s32[1,4]{1,0:T(1,128)} %count_ref.3) | copy-start | bytes 52
  2.8 25.3 %all-to-all-start = ((bf16[32,8,2304]{2,1,0:T(8,128)(2,1)}), bf16[32,8,2304]{2,1,0:T(8,128)(2,1)S(1)}, u32[]{:S(2)}, u32[]{:S(2)}) async-start(bf16[32,8,2304]{2,1,0:T(8,128)(2,1)} %bitcast.22), calls=%async_computation | async-start | bytes 2359296 | tf_op jit(solution)/shard_map/all_to_all | solution.py:548
  35.8 3.4 %collective-permute-start = (bf16[640,1152]{1,0:T(8,128)(2,1)S(1)}, bf16[640,1152]{1,0:T(8,128)(2,1)S(1)}, u32[]{:S(2)}, u32[]{:S(2)}) collective-permute-start(bf16[640,1152]{1,0:T(8,128)(2,1)S(1)} %get-tuple-element.27), channel_id=1, source_target_pairs={{0,1},{1,0},{2,3},{3,2},{4,5},{5,4},{6,7},{7,6},{8,9},{9,8},{10,11... | collective-permute-start | bytes 4423688 | tf_op jit(solution)/shard_map/ppermute | solution.py:555
  40.4 26.4 %all-to-all-start.2 = ((bf16[16,40,1152]{2,1,0:T(8,128)(2,1)}), bf16[16,40,1152]{2,1,0:T(8,128)(2,1)S(1)}, u32[]{:S(2)}, u32[]{:S(2)}) async-start(bf16[16,40,1152]{2,1,0:T(8,128)(2,1)} %bitcast.19), calls=%async_computation.2 | async-start | bytes 2949120 | tf_op jit(solution)/shard_map/all_to_all | solution.py:559
  67.0 14.5 %collective-permute-start.1 = (bf16[40,1152]{1,0:T(8,128)(2,1)S(1)}, bf16[40,1152]{1,0:T(8,128)(2,1)S(1)}, u32[]{:S(2)}, u32[]{:S(2)}) collective-permute-start(bf16[40,1152]{1,0:T(8,128)(2,1)S(1)} %convert_element_type.21), channel_id=1, source_target_pairs={{0,128},{32,160},{64,192},{96,224},{128,0},{160,32},{192,64},{224,... | collective-permute-start | bytes 276488 | tf_op jit(solution)/shard_map/ppermute | solution.py:565
  74.3 24.8 %all-to-all-start.1 = ((bf16[32,8,2304]{2,1,0:T(8,128)(2,1)}), bf16[32,8,2304]{2,1,0:T(8,128)(2,1)S(1)}, u32[]{:S(2)}, u32[]{:S(2)}) async-start(bf16[32,8,2304]{2,1,0:T(8,128)(2,1)} %bitcast.21), calls=%async_computation.1 | async-start | bytes 2359296 | tf_op jit(solution)/shard_map/all_to_all | solution.py:548
  81.5 4.8 %collective-permute-start.2 = (bf16[40,1152]{1,0:T(8,128)(2,1)S(1)}, bf16[40,1152]{1,0:T(8,128)(2,1)S(1)}, u32[]{:S(2)}, u32[]{:S(2)}) collective-permute-start(bf16[40,1152]{1,0:T(8,128)(2,1)S(1)} %add_convert_fusion.1), channel_id=1, source_target_pairs={{0,32},{32,0},{64,96},{96,64},{128,160},{160,128},{192,224},{224,1... | collective-permute-start | bytes 276488 | tf_op jit(solution)/shard_map/ppermute | solution.py:565
  86.3 12.8 %collective-permute-start.3 = (bf16[40,1152]{1,0:T(8,128)(2,1)S(1)}, bf16[40,1152]{1,0:T(8,128)(2,1)S(1)}, u32[]{:S(2)}, u32[]{:S(2)}) collective-permute-start(bf16[40,1152]{1,0:T(8,128)(2,1)S(1)} %add_convert_fusion.left_ref), channel_id=1, source_target_pairs={{0,64},{32,96},{64,0},{96,32},{128,192},{160,224},{192,128},{224,1... | collective-permute-start | bytes 276488 | tf_op jit(solution)/shard_map/ppermute | solution.py:567

commit v10 on v9

--- a/solution.py
+++ b/solution.py
@@ -507,15 +507,18 @@
     )(terms, in_hbm(after))
 
 
-def finish_kernel(returned_ref, left_ref, right_ref, block_ref, latent_ref, grad_ref):
+def finish_kernel(returned_ref, own_ref, *refs):
+    other_refs, (block_ref, latent_ref, grad_ref) = refs[:-3], refs[-3:]
     model = block_ref.shape[1]
     block_ref[...] = returned_ref[:, :model]
     latent_ref[...] = returned_ref[:, model:]
-    total = left_ref[...].astype(jnp.float32) + right_ref[...].astype(jnp.float32)
+    total = own_ref[...].astype(jnp.float32)
+    for other_ref in other_refs:
+        total = total + other_ref[...].astype(jnp.float32)
     grad_ref[...] = total[: grad_ref.shape[0]]
 
 
-def run_finish(returned, left, right, share):
+def run_finish(returned, own, others, share):
     rows, model = returned.shape[0], returned.shape[1] // 2
     low = jnp.bfloat16
     return pl.pallas_call(
@@ -525,12 +528,12 @@
             jax.ShapeDtypeStruct((rows, model), low),
             jax.ShapeDtypeStruct((share, model), jnp.float32),
         ),
-        in_specs=[vmem()] * 3,
+        in_specs=[vmem()] * (2 + len(others)),
         out_specs=(vmem(),) * 3,
         compiler_params=pltpu.CompilerParams(vmem_limit_bytes=12 * MIB),
         cost_estimate=pl.CostEstimate(flops=0, bytes_accessed=4 * MIB, transcendentals=0),
         name="finish",
-    )(returned, left, right)
+    )(returned, own, *others)
 
 
 def per_device(latents, cotangent, qkv_weight, out_weight, modulation, frame_clip, clip_patches):
@@ -560,13 +563,15 @@
     saved = (gdy, out_weight, att, qkv, prob, qkv_weight)
     results = run_backward(frame_clip, clip_patches, place, tokens, mod, saved, pair)
     total = run_sum(terms, results).astype(jnp.bfloat16)
-    strides = [groups // 2] + [1 << bit for bit in range(groups.bit_length() - 2)]
-    for stride in strides[:-1]:
-        met = lax.ppermute(total, "dp", [(i, i ^ stride) for i in range(groups)])
-        total = (total.astype(jnp.float32) + met.astype(jnp.float32)).astype(jnp.bfloat16)
-    met = lax.ppermute(total, "dp", [(i, i ^ strides[-1]) for i in range(groups)])
+    half = groups // 2
+    met = lax.ppermute(total, "dp", [(i, i ^ half) for i in range(groups)])
+    total = (total.astype(jnp.float32) + met.astype(jnp.float32)).astype(jnp.bfloat16)
+    others = [
+        lax.ppermute(total, "dp", [(i, i ^ stride) for i in range(groups)])
+        for stride in range(1, half)
+    ]
     returned = exchange(results)
-    block_out, latent_grad, grad = run_finish(returned, total, met, share)
+    block_out, latent_grad, grad = run_finish(returned, total, others, share)
     return block_out.reshape(latents.shape), latent_grad.reshape(latents.shape), grad
 
 

time: 102 us -> 98.5 us (0.966)
  waiting for transfers between devices: 39.3 us -> 34.8 us
  starting transfers between devices: 30.4 us -> 32.2 us
    all_to_all x2, waiting for transfers between devices: 28.6 us -> 20 us  [exchange(): return lax.all_to_all(pieces, 'seq', 0, 0, tiled=True).reshape(rows.shape)]
    ppermute x3 -> x4, waiting for transfers between devices: 3.7 us -> 7.91 us  [the longest x3 4.83 us: per_device(): lax.ppermute(total, 'dp', [(i, i ^ stride) for i in range(groups)])]
    ppermute x3 -> x4, starting transfers between devices: 9.94 us -> 11.8 us  [the longest x1 7.28 us: per_device(): met = lax.ppermute(total, 'dp', [(i, i ^ half) for i in range(groups)])]
  transfers between devices with their start and end apart: 7 -> 8, of which waited for: 5 -> 6; matrix products, arithmetic and copies ran while one was open for 0% -> 0% of each run, Pallas kernels for 17% -> 18%
where the time goes in v10:
time: 98.5 us; the launch traced here: 97.6 us
  waiting for transfers between devices  34.8 us (35%)
  starting transfers between devices  32.2 us (33%)
  Pallas kernels  29.7 us (30%)
    all_to_all x2, waiting for transfers between devices, exchange(): return lax.all_to_all(pieces, 'seq', 0, 0, tiled=True).reshape(rows.shape)  20 us
    all_to_all x2, starting transfers between devices, exchange(): return lax.all_to_all(pieces, 'seq', 0, 0, tiled=True).reshape(rows.shape)  15 us
    pallas_call x1, Pallas kernels, run_backward(): pl.pallas_call(backward_kernel, out_shape=pltpu.HBM(tokens.shape, low), i...  14.4 us
    pallas_call x1, Pallas kernels, run_forward(): pl.pallas_call(forward_kernel, out_shape=tuple((pltpu.VMEM(size, low) for...  7.7 us
    ppermute x1, starting transfers between devices, per_device(): met = lax.ppermute(total, 'dp', [(i, i ^ half) for i in range(groups)])  7.28 us
    all_to_all x1, waiting for transfers between devices, per_device(): lax.all_to_all(pair, 'seq', 0, 0, tiled=True, axis_index_groups=same_core)  6.69 us
    all_to_all x1, starting transfers between devices, per_device(): lax.all_to_all(pair, 'seq', 0, 0, tiled=True, axis_index_groups=same_core)  5.24 us
    ppermute x3, waiting for transfers between devices, per_device(): lax.ppermute(total, 'dp', [(i, i ^ stride) for i in range(groups)])  4.83 us
  transfers between devices with their start and end apart: 8, of which 6 were waited for; matrix products, arithmetic and copies ran while one was open for 0% of the time, Pallas kernels for 18%

profile of v10, /device:TPU:2, one launch (start us, length us, event | category | flops | bytes accessed | tf_op | source)
XLA Modules:
  0.0 97.6 jit_solution(12195240373416131867)
XLA Ops:
  0.6 2.1 %pack.1 = bf16[256,2304]{1,0:T(8,128)(2,1)} custom-call(bf16[256,1152]{1,0:T(8,128)(2,1)} %bitcast.23, bf16[256,1152]{1,0:T(8,128)(2,1)} %bitcast.24), custom_call_target="tpu_custom_call" | custom-call | tf_op jit(solution)/shard_map/pack/pallas_call | solution.py:443
  2.8 0.0 copy-start
  2.8 0.0 copy-start.1
  2.8 0.0 copy-start.2
  2.8 7.8 %all-to-all-start = ((bf16[32,8,2304]{2,1,0:T(8,128)(2,1)}), bf16[32,8,2304]{2,1,0:T(8,128)(2,1)S(1)}, u32[]{:S(2)}, u32[]{:S(2)}) async-start(bf16[32,8,2304]{2,1,0:T(8,128)(2,1)} %bitcast.22), calls=%async_computation | async-start | bytes 2359296 | tf_op jit(solution)/shard_map/all_to_all | solution.py:551
  10.6 0.1 pad_add_fusion.place_ref
  10.7 17.4 %all-to-all-done = bf16[32,8,2304]{2,1,0:T(8,128)(2,1)S(1)} async-done(((bf16[32,8,2304]{2,1,0:T(8,128)(2,1)}), bf16[32,8,2304]{2,1,0:T(8,128)(2,1)S(1)}, u32[]{:S(2)}, u32[]{:S(2)}) %all-to-all-start) | async-done | bytes 1179680 | tf_op jit(solution)/shard_map/all_to_all | solution.py:551
  28.1 0.0 copy-done
  28.1 0.0 copy-done.1
  28.1 0.0 copy-done.2
  28.1 7.7 %forward.1 = (bf16[256,3456]{1,0:T(8,128)(2,1)S(1)}, bf16[16,256,256]{2,1,0:T(8,128)(2,1)S(1)}, bf16[256,1152]{1,0:T(8,128)(2,1)S(1)}, bf16[256,1152]{1,0:T(8,12...) custom-call(s32[1,32]{1,0:T(1,128)S(1)} %copy-done.1, s32[1,4]{1,0:T(1,128)S(1)} %copy-done.2, ...), custom_call_target="tpu_custom_call" | custom-call | flops 2717908992 | bytes 12582912 | tf_op jit(solution)/shard_map/forward/pallas_call | solution.py:366
  35.8 0.2 collective-permute-start
  36.0 2.9 %keep.1 = (bf16[640,1152]{1,0:T(8,128)(2,1)S(1)}, bf16[256,3456]{1,0:T(8,128)(2,1)}, bf16[16,256,256]{2,1,0:T(8,128)(2,1)}, bf16[256,1152]{1,0:T(8,128)(2,1)}, bf16[256,1152]{1,0:T(8,128)(2,1)}) custom-call(s32[2]{0:T(128)S(1)} %pad_add_fusion.place_ref, bf16[2,640,256]{2,1,0:T(8,128)(2,1)S(1)} %get-tuple-element.17.share_ref, ...), custom_call_target="tpu_custom_call" | custom-call | flops 377487360 | bytes 6291456 | tf_op jit(solution)/shard_map/keep/pallas_call | solution.py:214
  38.9 0.3 collective-permute-done.right_ref
  39.2 1.2 %add.13 = bf16[640,1152]{1,0:T(8,128)(2,1)} custom-call(bf16[640,1152]{1,0:T(8,128)(2,1)S(1)} %get-tuple-element.26.left_ref, bf16[640,1152]{1,0:T(8,128)(2,1)S(1)} %collective-permute-done.right_ref), custom_call_target="tpu_custom_call" | custom-call | tf_op jit(solution)/shard_map/add/pallas_call | solution.py:477
  40.4 5.2 %all-to-all-start.2 = ((bf16[16,40,1152]{2,1,0:T(8,128)(2,1)}), bf16[16,40,1152]{2,1,0:T(8,128)(2,1)S(1)}, u32[]{:S(2)}, u32[]{:S(2)}) async-start(bf16[16,40,1152]{2,1,0:T(8,128)(2,1)} %bitcast.19), calls=%async_computation.2 | async-start | bytes 2949120 | tf_op jit(solution)/shard_map/all_to_all | solution.py:562
  45.7 14.4 %backward.1.after_ref = bf16[256,2304]{1,0:T(8,128)(2,1)} custom-call(s32[1,32]{1,0:T(1,128)S(1)} %copy-done.1, s32[1,4]{1,0:T(1,128)S(1)} %copy-done.2, s32[2]{0:T(128)S(1)} %pad_add_fusion.place_ref, bf16[256,2304]{1,0:T(8,128)(2,1)S(1)} %bitcast.15, f32[3,4,1152]{2,1,0:T(4,128)S(1)} %bitcast.18, bf16[256,1152]{1,0:T(8,128)(2,1)} %get-tuple-element.22.gdy_hbm, ...), custom_call_target="tpu_custom_call" | custom-call | flops 4076863488 | bytes 16777216 | tf_op jit(solution)/shard_map/backward/pallas_call | solution.py:389
  60.1 6.7 %all-to-all-done.2.terms_ref = bf16[16,40,1152]{2,1,0:T(8,128)(2,1)S(1)} async-done(((bf16[16,40,1152]{2,1,0:T(8,128)(2,1)}), bf16[16,40,1152]{2,1,0:T(8,128)(2,1)S(1)}, u32[]{:S(2)}, u32[]{:S(2)}) %all-to-all-start.2) | async-done | bytes 1474592 | tf_op jit(solution)/shard_map/all_to_all | solution.py:562
  66.8 7.2 %all-to-all-start.1 = ((bf16[32,8,2304]{2,1,0:T(8,128)(2,1)}), bf16[32,8,2304]{2,1,0:T(8,128)(2,1)S(1)}, u32[]{:S(2)}, u32[]{:S(2)}) async-start(bf16[32,8,2304]{2,1,0:T(8,128)(2,1)} %bitcast.21), calls=%async_computation.1 | async-start | bytes 2359296 | tf_op jit(solution)/shard_map/all_to_all | solution.py:551
  74.0 0.2 sum.1
  74.2 7.3 %collective-permute-start.1 = (bf16[40,1152]{1,0:T(8,128)(2,1)S(1)}, bf16[40,1152]{1,0:T(8,128)(2,1)S(1)}, u32[]{:S(2)}, u32[]{:S(2)}) collective-permute-start(bf16[40,1152]{1,0:T(8,128)(2,1)S(1)} %convert_element_type.12), channel_id=1, source_target_pairs={{0,128},{32,160},{64,192},{96,224},{128,0},{160,32},{192,64},{224,... | collective-permute-start | bytes 276488 | tf_op jit(solution)/shard_map/ppermute | solution.py:567
  81.5 3.1 %collective-permute-done.1 = bf16[40,1152]{1,0:T(8,128)(2,1)S(1)} collective-permute-done((bf16[40,1152]{1,0:T(8,128)(2,1)S(1)}, bf16[40,1152]{1,0:T(8,128)(2,1)S(1)}, u32[]{:S(2)}, u32[]{:S(2)}) %collective-permute-start.1) | collective-permute-done | bytes 92192 | tf_op jit(solution)/shard_map/ppermute | solution.py:567
  84.6 3.1 %collective-permute-start.4 = (bf16[40,1152]{1,0:T(8,128)(2,1)S(1)}, bf16[40,1152]{1,0:T(8,128)(2,1)S(1)}, u32[]{:S(2)}, u32[]{:S(2)}) collective-permute-start(bf16[40,1152]{1,0:T(8,128)(2,1)S(1)} %add_convert_fusion.own_ref), channel_id=1, source_target_pairs={{0,96},{32,64},{64,32},{96,0},{128,224},{160,192},{192,160},{224,1... | collective-permute-start | bytes 276488 | tf_op jit(solution)/shard_map/ppermute | solution.py:570
  87.7 0.9 collective-permute-start.3
  88.5 0.5 collective-permute-start.2
  89.1 2.5 %all-to-all-done.1 = bf16[32,8,2304]{2,1,0:T(8,128)(2,1)S(1)} async-done(((bf16[32,8,2304]{2,1,0:T(8,128)(2,1)}), bf16[32,8,2304]{2,1,0:T(8,128)(2,1)S(1)}, u32[]{:S(2)}, u32[]{:S(2)}) %all-to-all-start.1) | async-done | bytes 1179680 | tf_op jit(solution)/shard_map/all_to_all | solution.py:551
  91.6 0.0 collective-permute-done.4.refs_2_
  91.6 4.8 %collective-permute-done.3.refs_1_ = bf16[40,1152]{1,0:T(8,128)(2,1)S(1)} collective-permute-done((bf16[40,1152]{1,0:T(8,128)(2,1)S(1)}, bf16[40,1152]{1,0:T(8,128)(2,1)S(1)}, u32[]{:S(2)}, u32[]{:S(2)}) %collective-permute-start.3) | collective-permute-done | bytes 92192 | tf_op jit(solution)/shard_map/ppermute | solution.py:570
  96.4 0.0 collective-permute-done.2.refs_0_
  96.4 1.2 %finish.1 = (bf16[256,1152]{1,0:T(8,128)(2,1)}, bf16[256,1152]{1,0:T(8,128)(2,1)}, f32[36,1152]{1,0:T(8,128)}) custom-call(bf16[256,2304]{1,0:T(8,128)(2,1)S(1)} %bitcast.16, bf16[40,1152]{1,0:T(8,128)(2,1)S(1)} %add_convert_fusion.own_ref, bf16[40,1152]{1,0:T(8,128)(2,1)S(1)} %collective-permute-done.2.refs_0_, ...), custom_call_target="tpu_custom_call" | custom-call | bytes 4194304 | tf_op jit(solution)/shard_map/finish/pallas_call | solution.py:524
  (2 shorter events, 0.0 us)
Async XLA Ops:
  2.8 25.3 %copy-start = (f32[1,4,3,1152]{3,1,2,0:T(4,128)S(1)}, f32[1,4,3,1152]{3,1,2,0:T(4,128)}, u32[]{:S(2)}) copy-start(f32[1,4,3,1152]{3,1,2,0:T(4,128)} %param.11) | copy-start | bytes 165892
  2.8 25.3 %copy-start.1 = (s32[1,32]{1,0:T(1,128)S(1)}, s32[1,32]{1,0:T(1,128)}, u32[]{:S(2)}) copy-start(s32[1,32]{1,0:T(1,128)} %clip_ref.3) | copy-start | bytes 388
  2.8 25.3 %copy-start.2 = (s32[1,4]{1,0:T(1,128)S(1)}, s32[1,4]{1,0:T(1,128)}, u32[]{:S(2)}) copy-start(s32[1,4]{1,0:T(1,128)} %count_ref.3) | copy-start | bytes 52
  2.8 25.3 %all-to-all-start = ((bf16[32,8,2304]{2,1,0:T(8,128)(2,1)}), bf16[32,8,2304]{2,1,0:T(8,128)(2,1)S(1)}, u32[]{:S(2)}, u32[]{:S(2)}) async-start(bf16[32,8,2304]{2,1,0:T(8,128)(2,1)} %bitcast.22), calls=%async_computation | async-start | bytes 2359296 | tf_op jit(solution)/shard_map/all_to_all | solution.py:551
  35.8 3.4 %collective-permute-start = (bf16[640,1152]{1,0:T(8,128)(2,1)S(1)}, bf16[640,1152]{1,0:T(8,128)(2,1)S(1)}, u32[]{:S(2)}, u32[]{:S(2)}) collective-permute-start(bf16[640,1152]{1,0:T(8,128)(2,1)S(1)} %get-tuple-element.27), channel_id=1, source_target_pairs={{0,1},{1,0},{2,3},{3,2},{4,5},{5,4},{6,7},{7,6},{8,9},{9,8},{10,11... | collective-permute-start | bytes 4423688 | tf_op jit(solution)/shard_map/ppermute | solution.py:558
  40.4 26.4 %all-to-all-start.2 = ((bf16[16,40,1152]{2,1,0:T(8,128)(2,1)}), bf16[16,40,1152]{2,1,0:T(8,128)(2,1)S(1)}, u32[]{:S(2)}, u32[]{:S(2)}) async-start(bf16[16,40,1152]{2,1,0:T(8,128)(2,1)} %bitcast.19), calls=%async_computation.2 | async-start | bytes 2949120 | tf_op jit(solution)/shard_map/all_to_all | solution.py:562
  66.8 24.8 %all-to-all-start.1 = ((bf16[32,8,2304]{2,1,0:T(8,128)(2,1)}), bf16[32,8,2304]{2,1,0:T(8,128)(2,1)S(1)}, u32[]{:S(2)}, u32[]{:S(2)}) async-start(bf16[32,8,2304]{2,1,0:T(8,128)(2,1)} %bitcast.21), calls=%async_computation.1 | async-start | bytes 2359296 | tf_op jit(solution)/shard_map/all_to_all | solution.py:551
  74.2 10.4 %collective-permute-start.1 = (bf16[40,1152]{1,0:T(8,128)(2,1)S(1)}, bf16[40,1152]{1,0:T(8,128)(2,1)S(1)}, u32[]{:S(2)}, u32[]{:S(2)}) collective-permute-start(bf16[40,1152]{1,0:T(8,128)(2,1)S(1)} %convert_element_type.12), channel_id=1, source_target_pairs={{0,128},{32,160},{64,192},{96,224},{128,0},{160,32},{192,64},{224,... | collective-permute-start | bytes 276488 | tf_op jit(solution)/shard_map/ppermute | solution.py:567
  84.6 7.0 %collective-permute-start.4 = (bf16[40,1152]{1,0:T(8,128)(2,1)S(1)}, bf16[40,1152]{1,0:T(8,128)(2,1)S(1)}, u32[]{:S(2)}, u32[]{:S(2)}) collective-permute-start(bf16[40,1152]{1,0:T(8,128)(2,1)S(1)} %add_convert_fusion.own_ref), channel_id=1, source_target_pairs={{0,96},{32,64},{64,32},{96,0},{128,224},{160,192},{192,160},{224,1... | collective-permute-start | bytes 276488 | tf_op jit(solution)/shard_map/ppermute | solution.py:570
  87.7 8.8 %collective-permute-start.3 = (bf16[40,1152]{1,0:T(8,128)(2,1)S(1)}, bf16[40,1152]{1,0:T(8,128)(2,1)S(1)}, u32[]{:S(2)}, u32[]{:S(2)}) collective-permute-start(bf16[40,1152]{1,0:T(8,128)(2,1)S(1)} %add_convert_fusion.own_ref), channel_id=1, source_target_pairs={{0,64},{32,96},{64,0},{96,32},{128,192},{160,224},{192,128},{224,1... | collective-permute-start | bytes 276488 | tf_op jit(solution)/shard_map/ppermute | solution.py:570
  88.5 7.9 %collective-permute-start.2 = (bf16[40,1152]{1,0:T(8,128)(2,1)S(1)}, bf16[40,1152]{1,0:T(8,128)(2,1)S(1)}, u32[]{:S(2)}, u32[]{:S(2)}) collective-permute-start(bf16[40,1152]{1,0:T(8,128)(2,1)S(1)} %add_convert_fusion.own_ref), channel_id=1, source_target_pairs={{0,32},{32,0},{64,96},{96,64},{128,160},{160,128},{192,224},{224,1... | collective-permute-start | bytes 276488 | tf_op jit(solution)/shard_map/ppermute | solution.py:570

commit v11 on v10

--- a/solution.py
+++ b/solution.py
@@ -563,12 +563,12 @@
     saved = (gdy, out_weight, att, qkv, prob, qkv_weight)
     results = run_backward(frame_clip, clip_patches, place, tokens, mod, saved, pair)
     total = run_sum(terms, results).astype(jnp.bfloat16)
+    met = lax.ppermute(total, "dp", [(i, i ^ 1) for i in range(groups)])
+    total = (total.astype(jnp.float32) + met.astype(jnp.float32)).astype(jnp.bfloat16)
     half = groups // 2
-    met = lax.ppermute(total, "dp", [(i, i ^ half) for i in range(groups)])
-    total = (total.astype(jnp.float32) + met.astype(jnp.float32)).astype(jnp.bfloat16)
+    strides = [stride for stride in range(2, groups, 2) if stride != half] + [half]
     others = [
-        lax.ppermute(total, "dp", [(i, i ^ stride) for i in range(groups)])
-        for stride in range(1, half)
+        lax.ppermute(total, "dp", [(i, i ^ stride) for i in range(groups)]) for stride in strides
     ]
     returned = exchange(results)
     block_out, latent_grad, grad = run_finish(returned, total, others, share)

time: 98.5 us -> 97.5 us (0.990)
  starting transfers between devices: 32.2 us -> 31 us
    ppermute x1, starting transfers between devices: 7.28 us -> 2 us  [per_device(): met = lax.ppermute(total, 'dp', [(i, i ^ 1) for i in range(groups)])]
    ppermute x3, starting transfers between devices: 4.47 us -> 8.58 us  [per_device(): lax.ppermute(total, 'dp', [(i, i ^ stride) for i in range(groups)])]
    ppermute x3, waiting for transfers between devices: 4.83 us -> 3.43 us  [per_device(): lax.ppermute(total, 'dp', [(i, i ^ stride) for i in range(groups)])]
    all_to_all x2, waiting for transfers between devices: 20 us -> 21.2 us  [exchange(): return lax.all_to_all(pieces, 'seq', 0, 0, tiled=True).reshape(rows.shape)]
  transfers between devices with their start and end apart: 8 -> 8, of which waited for: 6 -> 7; matrix products, arithmetic and copies ran while one was open for 0% -> 0% of each run, Pallas kernels for 18% -> 18%
where the time goes in v11:
time: 97.5 us; the launch traced here: 96.2 us
  waiting for transfers between devices  34.6 us (35%)
  starting transfers between devices  31 us (32%)
  Pallas kernels  29.7 us (30%)
    all_to_all x2, waiting for transfers between devices, exchange(): return lax.all_to_all(pieces, 'seq', 0, 0, tiled=True).reshape(rows.shape)  21.2 us
    all_to_all x2, starting transfers between devices, exchange(): return lax.all_to_all(pieces, 'seq', 0, 0, tiled=True).reshape(rows.shape)  15 us
    pallas_call x1, Pallas kernels, run_backward(): pl.pallas_call(backward_kernel, out_shape=pltpu.HBM(tokens.shape, low), i...  14.4 us
    ppermute x3, starting transfers between devices, per_device(): lax.ppermute(total, 'dp', [(i, i ^ stride) for i in range(groups)])  8.58 us
    pallas_call x1, Pallas kernels, run_forward(): pl.pallas_call(forward_kernel, out_shape=tuple((pltpu.VMEM(size, low) for...  7.7 us
    all_to_all x1, waiting for transfers between devices, per_device(): lax.all_to_all(pair, 'seq', 0, 0, tiled=True, axis_index_groups=same_core)  6.69 us
    all_to_all x1, starting transfers between devices, per_device(): lax.all_to_all(pair, 'seq', 0, 0, tiled=True, axis_index_groups=same_core)  5.24 us
    ppermute x3, waiting for transfers between devices, per_device(): lax.ppermute(total, 'dp', [(i, i ^ stride) for i in range(groups)])  3.43 us
  transfers between devices with their start and end apart: 8, of which 7 were waited for; matrix products, arithmetic and copies ran while one was open for 0% of the time, Pallas kernels for 18%

profile of v11, /device:TPU:2, one launch (start us, length us, event | category | flops | bytes accessed | tf_op | source)
XLA Modules:
  0.0 96.2 jit_solution(6625080532126961505)
XLA Ops:
  0.6 2.1 %pack.1 = bf16[256,2304]{1,0:T(8,128)(2,1)} custom-call(bf16[256,1152]{1,0:T(8,128)(2,1)} %bitcast.23, bf16[256,1152]{1,0:T(8,128)(2,1)} %bitcast.24), custom_call_target="tpu_custom_call" | custom-call | tf_op jit(solution)/shard_map/pack/pallas_call | solution.py:443
  2.8 0.0 copy-start
  2.8 0.0 copy-start.1
  2.8 0.0 copy-start.2
  2.8 7.8 %all-to-all-start = ((bf16[32,8,2304]{2,1,0:T(8,128)(2,1)}), bf16[32,8,2304]{2,1,0:T(8,128)(2,1)S(1)}, u32[]{:S(2)}, u32[]{:S(2)}) async-start(bf16[32,8,2304]{2,1,0:T(8,128)(2,1)} %bitcast.22), calls=%async_computation | async-start | bytes 2359296 | tf_op jit(solution)/shard_map/all_to_all | solution.py:551
  10.6 0.1 pad_add_fusion.place_ref
  10.7 17.4 %all-to-all-done = bf16[32,8,2304]{2,1,0:T(8,128)(2,1)S(1)} async-done(((bf16[32,8,2304]{2,1,0:T(8,128)(2,1)}), bf16[32,8,2304]{2,1,0:T(8,128)(2,1)S(1)}, u32[]{:S(2)}, u32[]{:S(2)}) %all-to-all-start) | async-done | bytes 1179680 | tf_op jit(solution)/shard_map/all_to_all | solution.py:551
  28.1 0.0 copy-done
  28.1 0.0 copy-done.1
  28.1 0.0 copy-done.2
  28.1 7.7 %forward.1 = (bf16[256,3456]{1,0:T(8,128)(2,1)S(1)}, bf16[16,256,256]{2,1,0:T(8,128)(2,1)S(1)}, bf16[256,1152]{1,0:T(8,128)(2,1)S(1)}, bf16[256,1152]{1,0:T(8,12...) custom-call(s32[1,32]{1,0:T(1,128)S(1)} %copy-done.1, s32[1,4]{1,0:T(1,128)S(1)} %copy-done.2, ...), custom_call_target="tpu_custom_call" | custom-call | flops 2717908992 | bytes 12582912 | tf_op jit(solution)/shard_map/forward/pallas_call | solution.py:366
  35.8 0.2 collective-permute-start
  36.0 2.9 %keep.1 = (bf16[640,1152]{1,0:T(8,128)(2,1)S(1)}, bf16[256,3456]{1,0:T(8,128)(2,1)}, bf16[16,256,256]{2,1,0:T(8,128)(2,1)}, bf16[256,1152]{1,0:T(8,128)(2,1)}, bf16[256,1152]{1,0:T(8,128)(2,1)}) custom-call(s32[2]{0:T(128)S(1)} %pad_add_fusion.place_ref, bf16[2,640,256]{2,1,0:T(8,128)(2,1)S(1)} %get-tuple-element.17.share_ref, ...), custom_call_target="tpu_custom_call" | custom-call | flops 377487360 | bytes 6291456 | tf_op jit(solution)/shard_map/keep/pallas_call | solution.py:214
  38.9 0.3 collective-permute-done.right_ref
  39.2 1.2 %add.13 = bf16[640,1152]{1,0:T(8,128)(2,1)} custom-call(bf16[640,1152]{1,0:T(8,128)(2,1)S(1)} %get-tuple-element.26.left_ref, bf16[640,1152]{1,0:T(8,128)(2,1)S(1)} %collective-permute-done.right_ref), custom_call_target="tpu_custom_call" | custom-call | tf_op jit(solution)/shard_map/add/pallas_call | solution.py:477
  40.4 5.2 %all-to-all-start.2 = ((bf16[16,40,1152]{2,1,0:T(8,128)(2,1)}), bf16[16,40,1152]{2,1,0:T(8,128)(2,1)S(1)}, u32[]{:S(2)}, u32[]{:S(2)}) async-start(bf16[16,40,1152]{2,1,0:T(8,128)(2,1)} %bitcast.19), calls=%async_computation.2 | async-start | bytes 2949120 | tf_op jit(solution)/shard_map/all_to_all | solution.py:562
  45.7 14.4 %backward.1.after_ref = bf16[256,2304]{1,0:T(8,128)(2,1)} custom-call(s32[1,32]{1,0:T(1,128)S(1)} %copy-done.1, s32[1,4]{1,0:T(1,128)S(1)} %copy-done.2, s32[2]{0:T(128)S(1)} %pad_add_fusion.place_ref, bf16[256,2304]{1,0:T(8,128)(2,1)S(1)} %bitcast.15, f32[3,4,1152]{2,1,0:T(4,128)S(1)} %bitcast.18, bf16[256,1152]{1,0:T(8,128)(2,1)} %get-tuple-element.22.gdy_hbm, ...), custom_call_target="tpu_custom_call" | custom-call | flops 4076863488 | bytes 16777216 | tf_op jit(solution)/shard_map/backward/pallas_call | solution.py:389
  60.1 6.7 %all-to-all-done.2.terms_ref = bf16[16,40,1152]{2,1,0:T(8,128)(2,1)S(1)} async-done(((bf16[16,40,1152]{2,1,0:T(8,128)(2,1)}), bf16[16,40,1152]{2,1,0:T(8,128)(2,1)S(1)}, u32[]{:S(2)}, u32[]{:S(2)}) %all-to-all-start.2) | async-done | bytes 1474592 | tf_op jit(solution)/shard_map/all_to_all | solution.py:562
  66.8 7.2 %all-to-all-start.1 = ((bf16[32,8,2304]{2,1,0:T(8,128)(2,1)}), bf16[32,8,2304]{2,1,0:T(8,128)(2,1)S(1)}, u32[]{:S(2)}, u32[]{:S(2)}) async-start(bf16[32,8,2304]{2,1,0:T(8,128)(2,1)} %bitcast.21), calls=%async_computation.1 | async-start | bytes 2359296 | tf_op jit(solution)/shard_map/all_to_all | solution.py:551
  74.0 0.2 sum.1
  74.2 2.0 %collective-permute-start.1 = (bf16[40,1152]{1,0:T(8,128)(2,1)S(1)}, bf16[40,1152]{1,0:T(8,128)(2,1)S(1)}, u32[]{:S(2)}, u32[]{:S(2)}) collective-permute-start(bf16[40,1152]{1,0:T(8,128)(2,1)S(1)} %convert_element_type.12), channel_id=1, source_target_pairs={{0,32},{32,0},{64,96},{96,64},{128,160},{160,128},{192,224},{224,1... | collective-permute-start | bytes 276488 | tf_op jit(solution)/shard_map/ppermute | solution.py:566
  76.2 3.0 %collective-permute-done.1 = bf16[40,1152]{1,0:T(8,128)(2,1)S(1)} collective-permute-done((bf16[40,1152]{1,0:T(8,128)(2,1)S(1)}, bf16[40,1152]{1,0:T(8,128)(2,1)S(1)}, u32[]{:S(2)}, u32[]{:S(2)}) %collective-permute-start.1) | collective-permute-done | bytes 92192 | tf_op jit(solution)/shard_map/ppermute | solution.py:566
  79.2 7.1 %collective-permute-start.4 = (bf16[40,1152]{1,0:T(8,128)(2,1)S(1)}, bf16[40,1152]{1,0:T(8,128)(2,1)S(1)}, u32[]{:S(2)}, u32[]{:S(2)}) collective-permute-start(bf16[40,1152]{1,0:T(8,128)(2,1)S(1)} %add_convert_fusion.own_ref), channel_id=1, source_target_pairs={{0,128},{32,160},{64,192},{96,224},{128,0},{160,32},{192,64},{224,... | collective-permute-start | bytes 276488 | tf_op jit(solution)/shard_map/ppermute | solution.py:571
  86.3 0.0 collective-permute-start.3
  86.3 1.5 %collective-permute-start.2 = (bf16[40,1152]{1,0:T(8,128)(2,1)S(1)}, bf16[40,1152]{1,0:T(8,128)(2,1)S(1)}, u32[]{:S(2)}, u32[]{:S(2)}) collective-permute-start(bf16[40,1152]{1,0:T(8,128)(2,1)S(1)} %add_convert_fusion.own_ref), channel_id=1, source_target_pairs={{0,64},{32,96},{64,0},{96,32},{128,192},{160,224},{192,128},{224,1... | collective-permute-start | bytes 276488 | tf_op jit(solution)/shard_map/ppermute | solution.py:571
  87.8 3.8 %all-to-all-done.1 = bf16[32,8,2304]{2,1,0:T(8,128)(2,1)S(1)} async-done(((bf16[32,8,2304]{2,1,0:T(8,128)(2,1)}), bf16[32,8,2304]{2,1,0:T(8,128)(2,1)S(1)}, u32[]{:S(2)}, u32[]{:S(2)}) %all-to-all-start.1) | async-done | bytes 1179680 | tf_op jit(solution)/shard_map/all_to_all | solution.py:551
  91.6 0.0 collective-permute-done.4.refs_2_
  91.6 1.9 %collective-permute-done.3.refs_1_ = bf16[40,1152]{1,0:T(8,128)(2,1)S(1)} collective-permute-done((bf16[40,1152]{1,0:T(8,128)(2,1)S(1)}, bf16[40,1152]{1,0:T(8,128)(2,1)S(1)}, u32[]{:S(2)}, u32[]{:S(2)}) %collective-permute-start.3) | collective-permute-done | bytes 92192 | tf_op jit(solution)/shard_map/ppermute | solution.py:571
  93.6 1.5 %collective-permute-done.2.refs_0_ = bf16[40,1152]{1,0:T(8,128)(2,1)S(1)} collective-permute-done((bf16[40,1152]{1,0:T(8,128)(2,1)S(1)}, bf16[40,1152]{1,0:T(8,128)(2,1)S(1)}, u32[]{:S(2)}, u32[]{:S(2)}) %collective-permute-start.2) | collective-permute-done | bytes 92192 | tf_op jit(solution)/shard_map/ppermute | solution.py:571
  95.0 1.2 %finish.1 = (bf16[256,1152]{1,0:T(8,128)(2,1)}, bf16[256,1152]{1,0:T(8,128)(2,1)}, f32[36,1152]{1,0:T(8,128)}) custom-call(bf16[256,2304]{1,0:T(8,128)(2,1)S(1)} %bitcast.16, bf16[40,1152]{1,0:T(8,128)(2,1)S(1)} %add_convert_fusion.own_ref, bf16[40,1152]{1,0:T(8,128)(2,1)S(1)} %collective-permute-done.2.refs_0_, ...), custom_call_target="tpu_custom_call" | custom-call | bytes 4194304 | tf_op jit(solution)/shard_map/finish/pallas_call | solution.py:524
  (2 shorter events, 0.0 us)
Async XLA Ops:
  2.8 25.3 %copy-start = (f32[1,4,3,1152]{3,1,2,0:T(4,128)S(1)}, f32[1,4,3,1152]{3,1,2,0:T(4,128)}, u32[]{:S(2)}) copy-start(f32[1,4,3,1152]{3,1,2,0:T(4,128)} %param.11) | copy-start | bytes 165892
  2.8 25.3 %copy-start.1 = (s32[1,32]{1,0:T(1,128)S(1)}, s32[1,32]{1,0:T(1,128)}, u32[]{:S(2)}) copy-start(s32[1,32]{1,0:T(1,128)} %clip_ref.3) | copy-start | bytes 388
  2.8 25.3 %copy-start.2 = (s32[1,4]{1,0:T(1,128)S(1)}, s32[1,4]{1,0:T(1,128)}, u32[]{:S(2)}) copy-start(s32[1,4]{1,0:T(1,128)} %count_ref.3) | copy-start | bytes 52
  2.8 25.3 %all-to-all-start = ((bf16[32,8,2304]{2,1,0:T(8,128)(2,1)}), bf16[32,8,2304]{2,1,0:T(8,128)(2,1)S(1)}, u32[]{:S(2)}, u32[]{:S(2)}) async-start(bf16[32,8,2304]{2,1,0:T(8,128)(2,1)} %bitcast.22), calls=%async_computation | async-start | bytes 2359296 | tf_op jit(solution)/shard_map/all_to_all | solution.py:551
  35.8 3.4 %collective-permute-start = (bf16[640,1152]{1,0:T(8,128)(2,1)S(1)}, bf16[640,1152]{1,0:T(8,128)(2,1)S(1)}, u32[]{:S(2)}, u32[]{:S(2)}) collective-permute-start(bf16[640,1152]{1,0:T(8,128)(2,1)S(1)} %get-tuple-element.27), channel_id=1, source_target_pairs={{0,1},{1,0},{2,3},{3,2},{4,5},{5,4},{6,7},{7,6},{8,9},{9,8},{10,11... | collective-permute-start | bytes 4423688 | tf_op jit(solution)/shard_map/ppermute | solution.py:558
  40.4 26.4 %all-to-all-start.2 = ((bf16[16,40,1152]{2,1,0:T(8,128)(2,1)}), bf16[16,40,1152]{2,1,0:T(8,128)(2,1)S(1)}, u32[]{:S(2)}, u32[]{:S(2)}) async-start(bf16[16,40,1152]{2,1,0:T(8,128)(2,1)} %bitcast.19), calls=%async_computation.2 | async-start | bytes 2949120 | tf_op jit(solution)/shard_map/all_to_all | solution.py:562
  66.8 24.8 %all-to-all-start.1 = ((bf16[32,8,2304]{2,1,0:T(8,128)(2,1)}), bf16[32,8,2304]{2,1,0:T(8,128)(2,1)S(1)}, u32[]{:S(2)}, u32[]{:S(2)}) async-start(bf16[32,8,2304]{2,1,0:T(8,128)(2,1)} %bitcast.21), calls=%async_computation.1 | async-start | bytes 2359296 | tf_op jit(solution)/shard_map/all_to_all | solution.py:551
  74.2 5.0 %collective-permute-start.1 = (bf16[40,1152]{1,0:T(8,128)(2,1)S(1)}, bf16[40,1152]{1,0:T(8,128)(2,1)S(1)}, u32[]{:S(2)}, u32[]{:S(2)}) collective-permute-start(bf16[40,1152]{1,0:T(8,128)(2,1)S(1)} %convert_element_type.12), channel_id=1, source_target_pairs={{0,32},{32,0},{64,96},{96,64},{128,160},{160,128},{192,224},{224,1... | collective-permute-start | bytes 276488 | tf_op jit(solution)/shard_map/ppermute | solution.py:566
  79.2 12.4 %collective-permute-start.4 = (bf16[40,1152]{1,0:T(8,128)(2,1)S(1)}, bf16[40,1152]{1,0:T(8,128)(2,1)S(1)}, u32[]{:S(2)}, u32[]{:S(2)}) collective-permute-start(bf16[40,1152]{1,0:T(8,128)(2,1)S(1)} %add_convert_fusion.own_ref), channel_id=1, source_target_pairs={{0,128},{32,160},{64,192},{96,224},{128,0},{160,32},{192,64},{224,... | collective-permute-start | bytes 276488 | tf_op jit(solution)/shard_map/ppermute | solution.py:571
  86.3 7.2 %collective-permute-start.3 = (bf16[40,1152]{1,0:T(8,128)(2,1)S(1)}, bf16[40,1152]{1,0:T(8,128)(2,1)S(1)}, u32[]{:S(2)}, u32[]{:S(2)}) collective-permute-start(bf16[40,1152]{1,0:T(8,128)(2,1)S(1)} %add_convert_fusion.own_ref), channel_id=1, source_target_pairs={{0,192},{32,224},{64,128},{96,160},{128,64},{160,96},{192,0},{224,... | collective-permute-start | bytes 276488 | tf_op jit(solution)/shard_map/ppermute | solution.py:571
  86.3 8.7 %collective-permute-start.2 = (bf16[40,1152]{1,0:T(8,128)(2,1)S(1)}, bf16[40,1152]{1,0:T(8,128)(2,1)S(1)}, u32[]{:S(2)}, u32[]{:S(2)}) collective-permute-start(bf16[40,1152]{1,0:T(8,128)(2,1)S(1)} %add_convert_fusion.own_ref), channel_id=1, source_target_pairs={{0,64},{32,96},{64,0},{96,32},{128,192},{160,224},{192,128},{224,1... | collective-permute-start | bytes 276488 | tf_op jit(solution)/shard_map/ppermute | solution.py:571

commit v12 on v8

--- a/solution.py
+++ b/solution.py
@@ -116,7 +116,7 @@
         gdy_ref[where, :] = jnp.concatenate(gdys, axis=0).astype(jnp.bfloat16)
         return carry
 
-    lax.fori_loop(0, frames // 2, pair_step, 0, unroll=4)
+    lax.fori_loop(0, frames // 2, pair_step, 0, unroll=8)
     start_loads(1)
 
     starts = []
@@ -479,7 +479,7 @@
         out_shape=pltpu.HBM(left.shape, left.dtype),
         in_specs=[vmem()] * 2,
         out_specs=hbm(),
-        scratch_shapes=[pltpu.VMEM(left.shape, left.dtype), pltpu.SemaphoreType.DMA((5,))],
+        scratch_shapes=[pltpu.VMEM(left.shape, left.dtype), pltpu.SemaphoreType.DMA((2,))],
         compiler_params=pltpu.CompilerParams(vmem_limit_bytes=12 * MIB),
         name="add",
     )(in_vmem(left), in_vmem(right))

time: 96.6 us -> 96.7 us (level)
  no operation moved by 1% of the time
where the time goes in v12:
time: 96.7 us; the launch traced here: 95.1 us
  waiting for transfers between devices  32.3 us (33%)
  starting transfers between devices  32 us (33%)
  Pallas kernels  29.8 us (31%)
    all_to_all x2, waiting for transfers between devices, exchange(): return lax.all_to_all(pieces, 'seq', 0, 0, tiled=True).reshape(rows.shape)  20.9 us
    all_to_all x2, starting transfers between devices, exchange(): return lax.all_to_all(pieces, 'seq', 0, 0, tiled=True).reshape(rows.shape)  15 us
    pallas_call x1, Pallas kernels, run_backward(): pl.pallas_call(backward_kernel, out_shape=pltpu.HBM(tokens.shape, low), i...  14.4 us
    ppermute x3, starting transfers between devices, per_device(): met = lax.ppermute(total, 'dp', [(i, i ^ stride) for i in range(groups)])  11.6 us
    pallas_call x1, Pallas kernels, run_forward(): pl.pallas_call(forward_kernel, out_shape=tuple((pltpu.VMEM(size, low) for...  7.7 us
    all_to_all x1, waiting for transfers between devices, per_device(): lax.all_to_all(pair, 'seq', 0, 0, tiled=True, axis_index_groups=same_core)  6.69 us
    all_to_all x1, starting transfers between devices, per_device(): lax.all_to_all(pair, 'seq', 0, 0, tiled=True, axis_index_groups=same_core)  5.24 us
    ppermute x3, waiting for transfers between devices, per_device(): met = lax.ppermute(total, 'dp', [(i, i ^ stride) for i in range(groups)])  4.5 us
  transfers between devices with their start and end apart: 7, of which 5 were waited for; matrix products, arithmetic and copies ran while one was open for 0% of the time, Pallas kernels for 18%

profile of v12, /device:TPU:2, one launch (start us, length us, event | category | flops | bytes accessed | tf_op | source)
XLA Modules:
  0.0 95.1 jit_solution(4942244370088434355)
XLA Ops:
  0.6 2.1 %pack.1 = bf16[256,2304]{1,0:T(8,128)(2,1)} custom-call(bf16[256,1152]{1,0:T(8,128)(2,1)} %bitcast.23, bf16[256,1152]{1,0:T(8,128)(2,1)} %bitcast.24), custom_call_target="tpu_custom_call" | custom-call | tf_op jit(solution)/shard_map/pack/pallas_call | solution.py:443
  2.8 0.0 copy-start
  2.8 0.0 copy-start.1
  2.8 0.0 copy-start.2
  2.8 7.8 %all-to-all-start = ((bf16[32,8,2304]{2,1,0:T(8,128)(2,1)}), bf16[32,8,2304]{2,1,0:T(8,128)(2,1)S(1)}, u32[]{:S(2)}, u32[]{:S(2)}) async-start(bf16[32,8,2304]{2,1,0:T(8,128)(2,1)} %bitcast.22), calls=%async_computation | async-start | bytes 2359296 | tf_op jit(solution)/shard_map/all_to_all | solution.py:548
  10.6 0.1 pad_add_fusion.place_ref
  10.7 17.4 %all-to-all-done = bf16[32,8,2304]{2,1,0:T(8,128)(2,1)S(1)} async-done(((bf16[32,8,2304]{2,1,0:T(8,128)(2,1)}), bf16[32,8,2304]{2,1,0:T(8,128)(2,1)S(1)}, u32[]{:S(2)}, u32[]{:S(2)}) %all-to-all-start) | async-done | bytes 1179680 | tf_op jit(solution)/shard_map/all_to_all | solution.py:548
  28.1 0.0 copy-done
  28.1 0.0 copy-done.1
  28.1 0.0 copy-done.2
  28.1 7.7 %forward.1 = (bf16[256,3456]{1,0:T(8,128)(2,1)S(1)}, bf16[16,256,256]{2,1,0:T(8,128)(2,1)S(1)}, bf16[256,1152]{1,0:T(8,128)(2,1)S(1)}, bf16[256,1152]{1,0:T(8,12...) custom-call(s32[1,32]{1,0:T(1,128)S(1)} %copy-done.1, s32[1,4]{1,0:T(1,128)S(1)} %copy-done.2, ...), custom_call_target="tpu_custom_call" | custom-call | flops 2717908992 | bytes 12582912 | tf_op jit(solution)/shard_map/forward/pallas_call | solution.py:366
  35.8 0.2 collective-permute-start
  36.1 2.9 %keep.1 = (bf16[640,1152]{1,0:T(8,128)(2,1)S(1)}, bf16[256,3456]{1,0:T(8,128)(2,1)}, bf16[16,256,256]{2,1,0:T(8,128)(2,1)}, bf16[256,1152]{1,0:T(8,128)(2,1)}, bf16[256,1152]{1,0:T(8,128)(2,1)}) custom-call(s32[2]{0:T(128)S(1)} %pad_add_fusion.place_ref, bf16[2,640,256]{2,1,0:T(8,128)(2,1)S(1)} %get-tuple-element.17.share_ref, ...), custom_call_target="tpu_custom_call" | custom-call | flops 377487360 | bytes 6291456 | tf_op jit(solution)/shard_map/keep/pallas_call | solution.py:214
  38.9 0.3 collective-permute-done.right_ref
  39.2 1.3 %add.18 = bf16[640,1152]{1,0:T(8,128)(2,1)} custom-call(bf16[640,1152]{1,0:T(8,128)(2,1)S(1)} %get-tuple-element.26.left_ref, bf16[640,1152]{1,0:T(8,128)(2,1)S(1)} %collective-permute-done.right_ref), custom_call_target="tpu_custom_call" | custom-call | tf_op jit(solution)/shard_map/add/pallas_call | solution.py:477
  40.5 5.2 %all-to-all-start.2 = ((bf16[16,40,1152]{2,1,0:T(8,128)(2,1)}), bf16[16,40,1152]{2,1,0:T(8,128)(2,1)S(1)}, u32[]{:S(2)}, u32[]{:S(2)}) async-start(bf16[16,40,1152]{2,1,0:T(8,128)(2,1)} %bitcast.19), calls=%async_computation.2 | async-start | bytes 2949120 | tf_op jit(solution)/shard_map/all_to_all | solution.py:559
  45.7 14.4 %backward.1.after_ref = bf16[256,2304]{1,0:T(8,128)(2,1)} custom-call(s32[1,32]{1,0:T(1,128)S(1)} %copy-done.1, s32[1,4]{1,0:T(1,128)S(1)} %copy-done.2, s32[2]{0:T(128)S(1)} %pad_add_fusion.place_ref, bf16[256,2304]{1,0:T(8,128)(2,1)S(1)} %bitcast.15, f32[3,4,1152]{2,1,0:T(4,128)S(1)} %bitcast.18, bf16[256,1152]{1,0:T(8,128)(2,1)} %get-tuple-element.22.gdy_hbm, ...), custom_call_target="tpu_custom_call" | custom-call | flops 4076863488 | bytes 16777216 | tf_op jit(solution)/shard_map/backward/pallas_call | solution.py:389
  60.2 6.7 %all-to-all-done.2.terms_ref = bf16[16,40,1152]{2,1,0:T(8,128)(2,1)S(1)} async-done(((bf16[16,40,1152]{2,1,0:T(8,128)(2,1)}), bf16[16,40,1152]{2,1,0:T(8,128)(2,1)S(1)}, u32[]{:S(2)}, u32[]{:S(2)}) %all-to-all-start.2) | async-done | bytes 1474592 | tf_op jit(solution)/shard_map/all_to_all | solution.py:559
  66.9 0.2 sum.1
  67.1 2.0 %collective-permute-start.1 = (bf16[40,1152]{1,0:T(8,128)(2,1)S(1)}, bf16[40,1152]{1,0:T(8,128)(2,1)S(1)}, u32[]{:S(2)}, u32[]{:S(2)}) collective-permute-start(bf16[40,1152]{1,0:T(8,128)(2,1)S(1)} %convert_element_type.21), channel_id=1, source_target_pairs={{0,32},{32,0},{64,96},{96,64},{128,160},{160,128},{192,224},{224,1... | collective-permute-start | bytes 276488 | tf_op jit(solution)/shard_map/ppermute | solution.py:565
  69.1 7.2 %all-to-all-start.1 = ((bf16[32,8,2304]{2,1,0:T(8,128)(2,1)}), bf16[32,8,2304]{2,1,0:T(8,128)(2,1)S(1)}, u32[]{:S(2)}, u32[]{:S(2)}) async-start(bf16[32,8,2304]{2,1,0:T(8,128)(2,1)} %bitcast.21), calls=%async_computation.1 | async-start | bytes 2359296 | tf_op jit(solution)/shard_map/all_to_all | solution.py:548
  76.3 0.0 collective-permute-done.1
  76.3 3.4 %collective-permute-start.2 = (bf16[40,1152]{1,0:T(8,128)(2,1)S(1)}, bf16[40,1152]{1,0:T(8,128)(2,1)S(1)}, u32[]{:S(2)}, u32[]{:S(2)}) collective-permute-start(bf16[40,1152]{1,0:T(8,128)(2,1)S(1)} %add_convert_fusion.1), channel_id=1, source_target_pairs={{0,64},{32,96},{64,0},{96,32},{128,192},{160,224},{192,128},{224,1... | collective-permute-start | bytes 276488 | tf_op jit(solution)/shard_map/ppermute | solution.py:565
  79.7 4.5 %collective-permute-done.2 = bf16[40,1152]{1,0:T(8,128)(2,1)S(1)} collective-permute-done((bf16[40,1152]{1,0:T(8,128)(2,1)S(1)}, bf16[40,1152]{1,0:T(8,128)(2,1)S(1)}, u32[]{:S(2)}, u32[]{:S(2)}) %collective-permute-start.2) | collective-permute-done | bytes 92192 | tf_op jit(solution)/shard_map/ppermute | solution.py:565
  84.2 6.2 %collective-permute-start.3 = (bf16[40,1152]{1,0:T(8,128)(2,1)S(1)}, bf16[40,1152]{1,0:T(8,128)(2,1)S(1)}, u32[]{:S(2)}, u32[]{:S(2)}) collective-permute-start(bf16[40,1152]{1,0:T(8,128)(2,1)S(1)} %add_convert_fusion.left_ref), channel_id=1, source_target_pairs={{0,128},{32,160},{64,192},{96,224},{128,0},{160,32},{192,64},{224,... | collective-permute-start | bytes 276488 | tf_op jit(solution)/shard_map/ppermute | solution.py:565
  90.4 3.5 %all-to-all-done.1 = bf16[32,8,2304]{2,1,0:T(8,128)(2,1)S(1)} async-done(((bf16[32,8,2304]{2,1,0:T(8,128)(2,1)}), bf16[32,8,2304]{2,1,0:T(8,128)(2,1)S(1)}, u32[]{:S(2)}, u32[]{:S(2)}) %all-to-all-start.1) | async-done | bytes 1179680 | tf_op jit(solution)/shard_map/all_to_all | solution.py:548
  93.9 0.0 collective-permute-done.3.right_ref
  93.9 1.2 %finish.1 = (bf16[256,1152]{1,0:T(8,128)(2,1)}, bf16[256,1152]{1,0:T(8,128)(2,1)}, f32[36,1152]{1,0:T(8,128)}) custom-call(bf16[256,2304]{1,0:T(8,128)(2,1)S(1)} %bitcast.16, bf16[40,1152]{1,0:T(8,128)(2,1)S(1)} %add_convert_fusion.left_ref, bf16[40,1152]{1,0:T(8,128)(2,1)S(1)} %collective-permute-done.3.right_ref), custom_call_target="tpu_custom_call" | custom-call | bytes 4194304 | tf_op jit(solution)/shard_map/finish/pallas_call | solution.py:521
  (3 shorter events, 0.1 us)
Async XLA Ops:
  2.8 25.3 %copy-start = (f32[1,4,3,1152]{3,1,2,0:T(4,128)S(1)}, f32[1,4,3,1152]{3,1,2,0:T(4,128)}, u32[]{:S(2)}) copy-start(f32[1,4,3,1152]{3,1,2,0:T(4,128)} %param.11) | copy-start | bytes 165892
  2.8 25.3 %copy-start.1 = (s32[1,32]{1,0:T(1,128)S(1)}, s32[1,32]{1,0:T(1,128)}, u32[]{:S(2)}) copy-start(s32[1,32]{1,0:T(1,128)} %clip_ref.3) | copy-start | bytes 388
  2.8 25.3 %copy-start.2 = (s32[1,4]{1,0:T(1,128)S(1)}, s32[1,4]{1,0:T(1,128)}, u32[]{:S(2)}) copy-start(s32[1,4]{1,0:T(1,128)} %count_ref.3) | copy-start | bytes 52
  2.8 25.3 %all-to-all-start = ((bf16[32,8,2304]{2,1,0:T(8,128)(2,1)}), bf16[32,8,2304]{2,1,0:T(8,128)(2,1)S(1)}, u32[]{:S(2)}, u32[]{:S(2)}) async-start(bf16[32,8,2304]{2,1,0:T(8,128)(2,1)} %bitcast.22), calls=%async_computation | async-start | bytes 2359296 | tf_op jit(solution)/shard_map/all_to_all | solution.py:548
  35.8 3.4 %collective-permute-start = (bf16[640,1152]{1,0:T(8,128)(2,1)S(1)}, bf16[640,1152]{1,0:T(8,128)(2,1)S(1)}, u32[]{:S(2)}, u32[]{:S(2)}) collective-permute-start(bf16[640,1152]{1,0:T(8,128)(2,1)S(1)} %get-tuple-element.27), channel_id=1, source_target_pairs={{0,1},{1,0},{2,3},{3,2},{4,5},{5,4},{6,7},{7,6},{8,9},{9,8},{10,11... | collective-permute-start | bytes 4423688 | tf_op jit(solution)/shard_map/ppermute | solution.py:555
  40.5 26.4 %all-to-all-start.2 = ((bf16[16,40,1152]{2,1,0:T(8,128)(2,1)}), bf16[16,40,1152]{2,1,0:T(8,128)(2,1)S(1)}, u32[]{:S(2)}, u32[]{:S(2)}) async-start(bf16[16,40,1152]{2,1,0:T(8,128)(2,1)} %bitcast.19), calls=%async_computation.2 | async-start | bytes 2949120 | tf_op jit(solution)/shard_map/all_to_all | solution.py:559
  67.1 9.2 %collective-permute-start.1 = (bf16[40,1152]{1,0:T(8,128)(2,1)S(1)}, bf16[40,1152]{1,0:T(8,128)(2,1)S(1)}, u32[]{:S(2)}, u32[]{:S(2)}) collective-permute-start(bf16[40,1152]{1,0:T(8,128)(2,1)S(1)} %convert_element_type.21), channel_id=1, source_target_pairs={{0,32},{32,0},{64,96},{96,64},{128,160},{160,128},{192,224},{224,1... | collective-permute-start | bytes 276488 | tf_op jit(solution)/shard_map/ppermute | solution.py:565
  69.1 24.8 %all-to-all-start.1 = ((bf16[32,8,2304]{2,1,0:T(8,128)(2,1)}), bf16[32,8,2304]{2,1,0:T(8,128)(2,1)S(1)}, u32[]{:S(2)}, u32[]{:S(2)}) async-start(bf16[32,8,2304]{2,1,0:T(8,128)(2,1)} %bitcast.21), calls=%async_computation.1 | async-start | bytes 2359296 | tf_op jit(solution)/shard_map/all_to_all | solution.py:548
  76.3 7.9 %collective-permute-start.2 = (bf16[40,1152]{1,0:T(8,128)(2,1)S(1)}, bf16[40,1152]{1,0:T(8,128)(2,1)S(1)}, u32[]{:S(2)}, u32[]{:S(2)}) collective-permute-start(bf16[40,1152]{1,0:T(8,128)(2,1)S(1)} %add_convert_fusion.1), channel_id=1, source_target_pairs={{0,64},{32,96},{64,0},{96,32},{128,192},{160,224},{192,128},{224,1... | collective-permute-start | bytes 276488 | tf_op jit(solution)/shard_map/ppermute | solution.py:565
  84.2 9.7 %collective-permute-start.3 = (bf16[40,1152]{1,0:T(8,128)(2,1)S(1)}, bf16[40,1152]{1,0:T(8,128)(2,1)S(1)}, u32[]{:S(2)}, u32[]{:S(2)}) collective-permute-start(bf16[40,1152]{1,0:T(8,128)(2,1)S(1)} %add_convert_fusion.left_ref), channel_id=1, source_target_pairs={{0,128},{32,160},{64,192},{96,224},{128,0},{160,32},{192,64},{224,... | collective-permute-start | bytes 276488 | tf_op jit(solution)/shard_map/ppermute | solution.py:565
